TPU v7x, 128 devices: a whole 4x4x4 slice. The times are simulated.
128 devices in a mesh: row: 8 (over z, core), col: 16 (over y, x).
Axes of the slice: x: 4, y: 4, z: 4, core: 2. Of those that a mesh axis runs over, the one named last changes fastest.
Arguments:
- tile_values: bfloat16 [8, 384, 128, 128], P('row', 'col'), may hold values from -0.5 to 0.5
- tile_rows: int32 [8, 384], P('row', 'col'), may hold values from 0 to 47, as said below
Outputs:
- expanded: bfloat16 [8, 8, 384, 128, 128], P('row', None, 'col')
Inputs may be any that keep to these rules, and one draw needn't show every extreme that they name: For each row panel p and each aligned run of 24 block columns, the entries tile_rows[p, run] take exactly 8 distinct values, all inside one aligned run of 24 block rows of the panel.
All inputs are finite; a program needn't handle non-finite values.
Results may differ from a plain program's by a relative error of at most 0.001.
Values may be sent and summed in bfloat16 or wider, within the bound.
No kernel may reach another device: no remote copies, remote signals or barrier semaphores. Data moves between devices by JAX's collectives and lax.ppermute only.
A program may use at most 64 MiB of HBM per device.

v0:
```python
import jax
import jax.numpy as jnp
from jax import lax
from jax.sharding import PartitionSpec as P


def from_root(shard, axis, root):
    mine = lax.axis_index(axis) == root
    return lax.psum(jnp.where(mine, shard, jnp.zeros_like(shard)), axis)


def on_device(tile_values, tile_rows):
    panels = lax.axis_size("row")
    col_count = lax.axis_size("col")
    block_cols = tile_values.shape[1]
    tile_size = tile_values.shape[2]
    panel_rows = block_cols * col_count // panels
    right_vals, right_rows = (
        lax.all_gather(tile_values, "row", axis=0, tiled=True),
        lax.all_gather(tile_rows, "row", axis=0, tiled=True),
    )
    inner_index = (jnp.arange(panels, dtype=jnp.int32)[:, None] * panel_rows + right_rows).astype(
        jnp.int32
    )

    def take_section(source, selected):
        chosen_vals, chosen_rows = selected
        piece_vals, piece_rows = (
            from_root(tile_values, "col", source),
            from_root(tile_rows, "col", source),
        )
        offset_cols = inner_index - source * block_cols
        inside = (offset_cols >= 0) & (offset_cols < block_cols)
        slot_index = jnp.clip(offset_cols, 0, block_cols - 1)
        chosen_vals = jnp.where(inside[:, :, None, None], piece_vals[0][slot_index], chosen_vals)
        chosen_rows = jnp.where(inside, piece_rows[0][slot_index], chosen_rows)
        return (chosen_vals, chosen_rows)

    start_pair = (
        jnp.zeros((panels, block_cols, tile_size, tile_size), jnp.bfloat16),
        jnp.zeros((panels, block_cols), jnp.int32),
    )
    left_tiles, out_rows = lax.fori_loop(0, col_count, take_section, start_pair)
    products = jnp.einsum(
        "qcab,qcbd->qcad", left_tiles, right_vals, preferred_element_type=jnp.float32
    )
    matches = out_rows[:, None, :] == out_rows[None, :, :]
    merged = jnp.einsum(
        "qsc,scab->qcab", matches.astype(jnp.float32), products, precision=lax.Precision.HIGHEST
    )
    inflated = merged * merged
    lower = jnp.arange(panels)[None, :] < jnp.arange(panels)[:, None]
    repeated = jnp.any(matches & lower[:, :, None], axis=1)
    first_mask = 1.0 - repeated.astype(jnp.float32)
    partial_sums = jnp.einsum("qc,qcab->cb", first_mask, inflated, precision=lax.Precision.HIGHEST)
    scaling = float(panels * panels * tile_size)
    column_total = lax.psum(partial_sums, "row")
    factor = scaling / (column_total + 1e-06)
    expanded = (inflated * factor[None, :, None, :]).astype(jnp.bfloat16)
    return expanded[None]


def solution(mesh):
    placed = (P("row", "col", None, None), P("row", "col"))
    return jax.shard_map(
        on_device,
        mesh=mesh,
        in_specs=placed,
        out_specs=P("row", None, "col", None, None),
        check_vma=False,
    )
```

profile of v0, /device:TPU:1, one launch (start us, length us, event | category | flops | bytes accessed | tf_op | source)
XLA Modules:
  0.0 1819.8 jit_solution(2017605151199530931)
XLA Ops:
  7.4 13.2 all-gather
  20.7 1695.1 %while.16 = (s32[]{:T(128)}, bf16[8,24,128,128]{3,2,1,0:T(8,128)(2,1)}, s32[8,24]{1,0:T(8,128)S(1)}, s32[8,24]{1,0:T(8,128)S(1)}, bf16[1,24,128,128]{3,2,1,0:T(8...) while((s32[]{:T(128)}, ...), condition=%wide.region_3.4_spmd.clone, body=%wide.region_0.3_spmd.clone.sunk | while | flops 7081079 | bytes 37765320 | solution.py:43
  23.4 11.0 psum.35
  36.2 71.7 %all-reduce.2.cloned.1.call-done = bf16[24,128,128]{2,1,0:T(8,128)(2,1)} async-done(((bf16[24,128,128]{2,1,0:T(8,128)(2,1)}), bf16[24,128,128]{2,1,0:T(8,128)(2,1)}) %all-reduce.2.cloned.1.call-update) | async-done | bytes 786448 | tf_op jit(solution)/shard_map/while/body/eval_jaxpr/psum | solution.py:9
  136.2 76.4 %all-reduce.2.cloned.1.call-done = bf16[24,128,128]{2,1,0:T(8,128)(2,1)} async-done(((bf16[24,128,128]{2,1,0:T(8,128)(2,1)}), bf16[24,128,128]{2,1,0:T(8,128)(2,1)}) %all-reduce.2.cloned.1.call-update) | async-done | bytes 786448 | tf_op jit(solution)/shard_map/while/body/eval_jaxpr/psum | solution.py:9
  242.3 76.4 %all-reduce.2.cloned.1.call-done = bf16[24,128,128]{2,1,0:T(8,128)(2,1)} async-done(((bf16[24,128,128]{2,1,0:T(8,128)(2,1)}), bf16[24,128,128]{2,1,0:T(8,128)(2,1)}) %all-reduce.2.cloned.1.call-update) | async-done | bytes 786448 | tf_op jit(solution)/shard_map/while/body/eval_jaxpr/psum | solution.py:9
  348.5 76.1 %all-reduce.2.cloned.1.call-done = bf16[24,128,128]{2,1,0:T(8,128)(2,1)} async-done(((bf16[24,128,128]{2,1,0:T(8,128)(2,1)}), bf16[24,128,128]{2,1,0:T(8,128)(2,1)}) %all-reduce.2.cloned.1.call-update) | async-done | bytes 786448 | tf_op jit(solution)/shard_map/while/body/eval_jaxpr/psum | solution.py:9
  454.3 76.1 %all-reduce.2.cloned.1.call-done = bf16[24,128,128]{2,1,0:T(8,128)(2,1)} async-done(((bf16[24,128,128]{2,1,0:T(8,128)(2,1)}), bf16[24,128,128]{2,1,0:T(8,128)(2,1)}) %all-reduce.2.cloned.1.call-update) | async-done | bytes 786448 | tf_op jit(solution)/shard_map/while/body/eval_jaxpr/psum | solution.py:9
  560.3 76.1 %all-reduce.2.cloned.1.call-done = bf16[24,128,128]{2,1,0:T(8,128)(2,1)} async-done(((bf16[24,128,128]{2,1,0:T(8,128)(2,1)}), bf16[24,128,128]{2,1,0:T(8,128)(2,1)}) %all-reduce.2.cloned.1.call-update) | async-done | bytes 786448 | tf_op jit(solution)/shard_map/while/body/eval_jaxpr/psum | solution.py:9
  666.3 76.4 %all-reduce.2.cloned.1.call-done = bf16[24,128,128]{2,1,0:T(8,128)(2,1)} async-done(((bf16[24,128,128]{2,1,0:T(8,128)(2,1)}), bf16[24,128,128]{2,1,0:T(8,128)(2,1)}) %all-reduce.2.cloned.1.call-update) | async-done | bytes 786448 | tf_op jit(solution)/shard_map/while/body/eval_jaxpr/psum | solution.py:9
  772.6 76.4 %all-reduce.2.cloned.1.call-done = bf16[24,128,128]{2,1,0:T(8,128)(2,1)} async-done(((bf16[24,128,128]{2,1,0:T(8,128)(2,1)}), bf16[24,128,128]{2,1,0:T(8,128)(2,1)}) %all-reduce.2.cloned.1.call-update) | async-done | bytes 786448 | tf_op jit(solution)/shard_map/while/body/eval_jaxpr/psum | solution.py:9
  879.0 76.3 %all-reduce.2.cloned.1.call-done = bf16[24,128,128]{2,1,0:T(8,128)(2,1)} async-done(((bf16[24,128,128]{2,1,0:T(8,128)(2,1)}), bf16[24,128,128]{2,1,0:T(8,128)(2,1)}) %all-reduce.2.cloned.1.call-update) | async-done | bytes 786448 | tf_op jit(solution)/shard_map/while/body/eval_jaxpr/psum | solution.py:9
  985.3 76.1 %all-reduce.2.cloned.1.call-done = bf16[24,128,128]{2,1,0:T(8,128)(2,1)} async-done(((bf16[24,128,128]{2,1,0:T(8,128)(2,1)}), bf16[24,128,128]{2,1,0:T(8,128)(2,1)}) %all-reduce.2.cloned.1.call-update) | async-done | bytes 786448 | tf_op jit(solution)/shard_map/while/body/eval_jaxpr/psum | solution.py:9
  1091.4 76.4 %all-reduce.2.cloned.1.call-done = bf16[24,128,128]{2,1,0:T(8,128)(2,1)} async-done(((bf16[24,128,128]{2,1,0:T(8,128)(2,1)}), bf16[24,128,128]{2,1,0:T(8,128)(2,1)}) %all-reduce.2.cloned.1.call-update) | async-done | bytes 786448 | tf_op jit(solution)/shard_map/while/body/eval_jaxpr/psum | solution.py:9
  1197.9 76.1 %all-reduce.2.cloned.1.call-done = bf16[24,128,128]{2,1,0:T(8,128)(2,1)} async-done(((bf16[24,128,128]{2,1,0:T(8,128)(2,1)}), bf16[24,128,128]{2,1,0:T(8,128)(2,1)}) %all-reduce.2.cloned.1.call-update) | async-done | bytes 786448 | tf_op jit(solution)/shard_map/while/body/eval_jaxpr/psum | solution.py:9
  1304.8 75.6 %all-reduce.2.cloned.1.call-done = bf16[24,128,128]{2,1,0:T(8,128)(2,1)} async-done(((bf16[24,128,128]{2,1,0:T(8,128)(2,1)}), bf16[24,128,128]{2,1,0:T(8,128)(2,1)}) %all-reduce.2.cloned.1.call-update) | async-done | bytes 786448 | tf_op jit(solution)/shard_map/while/body/eval_jaxpr/psum | solution.py:9
  1410.4 76.1 %all-reduce.2.cloned.1.call-done = bf16[24,128,128]{2,1,0:T(8,128)(2,1)} async-done(((bf16[24,128,128]{2,1,0:T(8,128)(2,1)}), bf16[24,128,128]{2,1,0:T(8,128)(2,1)}) %all-reduce.2.cloned.1.call-update) | async-done | bytes 786448 | tf_op jit(solution)/shard_map/while/body/eval_jaxpr/psum | solution.py:9
  1504.7 12.1 psum.35
  1518.6 74.0 %all-reduce.2.cloned.1.call-done = bf16[24,128,128]{2,1,0:T(8,128)(2,1)} async-done(((bf16[24,128,128]{2,1,0:T(8,128)(2,1)}), bf16[24,128,128]{2,1,0:T(8,128)(2,1)}) %all-reduce.2.cloned.1.call-update) | async-done | bytes 786448 | tf_op jit(solution)/shard_map/while/body/eval_jaxpr/psum | solution.py:9
  1610.7 11.7 psum.35
  1624.2 74.5 %all-reduce.2.cloned.1.call-done = bf16[24,128,128]{2,1,0:T(8,128)(2,1)} async-done(((bf16[24,128,128]{2,1,0:T(8,128)(2,1)}), bf16[24,128,128]{2,1,0:T(8,128)(2,1)}) %all-reduce.2.cloned.1.call-update) | async-done | bytes 786448 | tf_op jit(solution)/shard_map/while/body/eval_jaxpr/psum | solution.py:9
  1717.0 43.1 %all-gather.3.cloned.1.call-done = bf16[8,24,128,128]{3,2,1,0:T(8,128)(2,1)} async-done(((bf16[1,24,128,128]{3,2,1,0:T(8,128)(2,1)}), bf16[8,24,128,128]{3,2,1,0:T(8,128)(2,1)}) %all-gather.3.cloned.1.call-update) | async-done | bytes 6291472 | tf_op jit(solution)/shard_map/all_gather | solution.py:19
  1766.4 14.3 bitcast_reduce_fusion
  1781.1 20.8 %psum.29 = f32[24,128]{1,0:T(8,128)S(1)} all-reduce(f32[24,128]{1,0:T(8,128)S(1)} %bitcast.45), channel_id=1, replica_groups=mesh['row'=8,'col'=16] {'row'}, use_global_device_ids=true, to_apply=%region_6.7 | all-reduce | flops 3072 | bytes 24576 | tf_op jit(solution)/shard_map/psum | solution.py:57
  (220 shorter events, 467.6 us)
Async XLA Ops:
  20.7 87.2 %all-reduce.2.cloned.1.call-start = ((), (), s32[]{:S(2)}) async-start(), calls=%async_computation.1 | async-start | bytes 1572864 | tf_op jit(solution)/shard_map/while/body/eval_jaxpr/psum | solution.py:9
  123.4 89.2 %all-reduce.2.cloned.1.call-start = ((), (), s32[]{:S(2)}) async-start(), calls=%async_computation.1 | async-start | bytes 1572864 | tf_op jit(solution)/shard_map/while/body/eval_jaxpr/psum | solution.py:9
  229.5 89.3 %all-reduce.2.cloned.1.call-start = ((), (), s32[]{:S(2)}) async-start(), calls=%async_computation.1 | async-start | bytes 1572864 | tf_op jit(solution)/shard_map/while/body/eval_jaxpr/psum | solution.py:9
  335.6 88.9 %all-reduce.2.cloned.1.call-start = ((), (), s32[]{:S(2)}) async-start(), calls=%async_computation.1 | async-start | bytes 1572864 | tf_op jit(solution)/shard_map/while/body/eval_jaxpr/psum | solution.py:9
  441.5 88.9 %all-reduce.2.cloned.1.call-start = ((), (), s32[]{:S(2)}) async-start(), calls=%async_computation.1 | async-start | bytes 1572864 | tf_op jit(solution)/shard_map/while/body/eval_jaxpr/psum | solution.py:9
  547.5 88.9 %all-reduce.2.cloned.1.call-start = ((), (), s32[]{:S(2)}) async-start(), calls=%async_computation.1 | async-start | bytes 1572864 | tf_op jit(solution)/shard_map/while/body/eval_jaxpr/psum | solution.py:9
  653.4 89.2 %all-reduce.2.cloned.1.call-start = ((), (), s32[]{:S(2)}) async-start(), calls=%async_computation.1 | async-start | bytes 1572864 | tf_op jit(solution)/shard_map/while/body/eval_jaxpr/psum | solution.py:9
  759.7 89.2 %all-reduce.2.cloned.1.call-start = ((), (), s32[]{:S(2)}) async-start(), calls=%async_computation.1 | async-start | bytes 1572864 | tf_op jit(solution)/shard_map/while/body/eval_jaxpr/psum | solution.py:9
  866.1 89.2 %all-reduce.2.cloned.1.call-start = ((), (), s32[]{:S(2)}) async-start(), calls=%async_computation.1 | async-start | bytes 1572864 | tf_op jit(solution)/shard_map/while/body/eval_jaxpr/psum | solution.py:9
  972.5 88.9 %all-reduce.2.cloned.1.call-start = ((), (), s32[]{:S(2)}) async-start(), calls=%async_computation.1 | async-start | bytes 1572864 | tf_op jit(solution)/shard_map/while/body/eval_jaxpr/psum | solution.py:9
  1078.6 89.2 %all-reduce.2.cloned.1.call-start = ((), (), s32[]{:S(2)}) async-start(), calls=%async_computation.1 | async-start | bytes 1572864 | tf_op jit(solution)/shard_map/while/body/eval_jaxpr/psum | solution.py:9
  1185.1 88.9 %all-reduce.2.cloned.1.call-start = ((), (), s32[]{:S(2)}) async-start(), calls=%async_computation.1 | async-start | bytes 1572864 | tf_op jit(solution)/shard_map/while/body/eval_jaxpr/psum | solution.py:9
  1291.2 89.2 %all-reduce.2.cloned.1.call-start = ((), (), s32[]{:S(2)}) async-start(), calls=%async_computation.1 | async-start | bytes 1572864 | tf_op jit(solution)/shard_map/while/body/eval_jaxpr/psum | solution.py:9
  1397.6 88.9 %all-reduce.2.cloned.1.call-start = ((), (), s32[]{:S(2)}) async-start(), calls=%async_computation.1 | async-start | bytes 1572864 | tf_op jit(solution)/shard_map/while/body/eval_jaxpr/psum | solution.py:9
  1503.7 88.9 %all-reduce.2.cloned.1.call-start = ((), (), s32[]{:S(2)}) async-start(), calls=%async_computation.1 | async-start | bytes 1572864 | tf_op jit(solution)/shard_map/while/body/eval_jaxpr/psum | solution.py:9
  1609.7 88.9 %all-reduce.2.cloned.1.call-start = ((), (), s32[]{:S(2)}) async-start(), calls=%async_computation.1 | async-start | bytes 1572864 | tf_op jit(solution)/shard_map/while/body/eval_jaxpr/psum | solution.py:9
  1715.8 44.3 %all-gather.3.cloned.1.call-start = ((), (), s32[]{:S(2)}) async-start(), calls=%async_computation | async-start | bytes 7077888 | tf_op jit(solution)/shard_map/all_gather | solution.py:19
Sparse Core Ops, SparseCore 0:
  24.7 83.1 all-reduce.1
  127.4 85.1 all-reduce.1
  233.5 85.1 all-reduce.1
  339.4 85.1 all-reduce.1
  445.3 85.1 all-reduce.1
  551.2 85.1 all-reduce.1
  657.5 85.1 all-reduce.1
  763.8 85.1 all-reduce.1
  870.2 85.1 all-reduce.1
  976.2 85.1 all-reduce.1
  1082.7 85.1 all-reduce.1
  1188.8 85.1 all-reduce.1
  1295.3 85.1 all-reduce.1
  1401.4 85.1 all-reduce.1
  1507.5 85.0 all-reduce.1
  1613.5 85.1 all-reduce.1
Sparse Core Ops, SparseCore 1:
  1717.9 42.1 all-gather.2
where the time goes:
time: 1820 us
  waiting for transfers between devices  1250 us (69%)
  blocking collectives  201 us (11%)
  local copies, waits for them, and re-layouts  176 us (10%)
  other arithmetic  152 us (8%)
  matrix products  21 us (1%)
    psum x16, waiting for transfers between devices, from_root(): return lax.psum(jnp.where(mine, shard, jnp.zeros_like(shard)), axis)  1210 us
    psum x16, blocking collectives, from_root(): return lax.psum(jnp.where(mine, shard, jnp.zeros_like(shard)), axis)  167 us
    gather x16, local copies, waits for them, and re-layouts, take_section(): piece_vals[0][slot_index]  144 us
    select_n x16, other arithmetic, take_section(): jnp.where(inside[:, :, None, None], piece_vals[0][slot_index], chosen_vals)  128 us
    all_gather x1, waiting for transfers between devices, on_device(): lax.all_gather(tile_values, 'row', axis=0, tiled=True)  43.1 us
  transfers between devices with their start and end apart: 17, of which 17 were waited for; matrix products, arithmetic and copies ran while one was open for 2% of the time, Pallas kernels for 0%

commit v1 on v0

v1 whole, which is shorter than its diff:
```python
import jax
import jax.numpy as jnp
import numpy as np
from jax import lax
from jax.experimental import pallas as pl
from jax.experimental.pallas import tpu as pltpu
from jax.sharding import Mesh, PartitionSpec as P

TILE = 128
BLK = 24
USED = 8
PANELS = 8
COLS = 16
BRD = 48
HALF = BLK // 2
DZ = (0, 3, 1, 2)
INNER = [(0, 1), (1, 0), (2, 3), (3, 2)]
OUTER = [(0, 3), (3, 0), (1, 2), (2, 1)]
UP = [(i, (i + 1) % 4) for i in range(4)]
DOWN = [(i, (i + 3) % 4) for i in range(4)]
SWAP = [(0, 1), (1, 0)]

SMEM = pl.BlockSpec(memory_space=pltpu.SMEM)
VMEM = pl.BlockSpec(memory_space=pltpu.VMEM)


def zero_table(ref, size):
    def step(n, carry):
        ref[n] = jnp.int32(-1)
        return carry

    lax.fori_loop(0, size, step, 0)


def copy_used(meta, seen, place, panel, column, first_half, put):
    zero_table(seen, BRD)

    def step(t, count):
        row = meta[column, panel * BLK + t]
        fresh = seen[row] < 0
        upper = (row >= BLK).astype(jnp.int32)
        local = row - upper * BLK

        @pl.when(fresh)
        def _():
            seen[row] = count
            put(count, upper, local)

        return count + fresh.astype(jnp.int32)

    lax.fori_loop(0, BLK, step, jnp.int32(0))


def select_own_kernel(pos, meta, own, inner, out, seen):
    x, y = pos[0], pos[1]
    panel = 2 * y + x // 2
    side = x % 2
    for dest in range(4):

        def put(slot, upper, local, dest=dest):
            @pl.when(upper == side)
            def _():
                out[dest, slot] = own[local]

            @pl.when(upper != side)
            def _():
                out[dest, slot] = inner[local]

        copy_used(meta, seen, None, panel, dest * 4 + x, None, put)


def select_other_kernel(pos, meta, outer, diag_a, diag_b, out, seen):
    x, y = pos[0], pos[1]
    panel = 2 * y + 1 - x // 2
    side = (3 - x) % 2
    for dest in range(4):

        def put(slot, upper, local, dest=dest):
            @pl.when(upper == side)
            def _():
                out[dest, slot] = outer[local]

            @pl.when((upper != side) & (local < HALF))
            def _():
                out[dest, slot] = diag_a[local]

            @pl.when((upper != side) & (local >= HALF))
            def _():
                out[dest, slot] = diag_b[local - HALF]

        copy_used(meta, seen, None, panel, dest * 4 + x, None, put)


def select(kernel, pos, meta, *blocks):
    return pl.pallas_call(
        kernel,
        out_shape=jax.ShapeDtypeStruct((4, USED, TILE, TILE), jnp.bfloat16),
        in_specs=[SMEM, SMEM] + [VMEM] * len(blocks),
        out_specs=VMEM,
        scratch_shapes=[pltpu.SMEM((BRD,), jnp.int32)],
        compiler_params=pltpu.CompilerParams(vmem_limit_bytes=16 << 20),
        cost_estimate=pl.CostEstimate(flops=0, bytes_accessed=4 << 20, transcendentals=0),
    )(pos, meta, *blocks)


def panel_of(pos, j):
    z = (pos[2] + DZ[j % 4]) % 4
    core = pos[3] if j < 4 else 1 - pos[3]
    return z, 2 * z + core


def plan_kernel(pos, meta, slot, rep, seen, stamp):
    column = pos[1] * 4 + pos[0]
    mine = 2 * pos[2] + pos[3]
    zero_table(seen, PANELS * BRD)
    zero_table(stamp, BRD)

    def step(t, counts):
        later = []
        for j in range(PANELS):
            _, panel = panel_of(pos, j)
            row = meta[column, panel * BLK + t]
            upper = (row >= BLK).astype(jnp.int32)
            old = seen[j * BRD + row]
            fresh = old < 0
            place = jnp.where(fresh, counts[j], old)
            seen[j * BRD + row] = place
            slot[j * BLK + t] = place
            later.append(counts[j] + fresh.astype(jnp.int32))
            out_row = meta[2 * panel + upper, mine * BLK + row - upper * BLK]
            mark = stamp[out_row]
            now = jnp.where(mark >= t * PANELS, mark, t * PANELS + j)
            stamp[out_row] = now
            rep[j * BLK + t] = now - t * PANELS
        return tuple(later)

    lax.fori_loop(0, BLK, step, (jnp.int32(0),) * PANELS)


def make_plan(pos, meta):
    shape = jax.ShapeDtypeStruct((PANELS * BLK,), jnp.int32)
    return pl.pallas_call(
        plan_kernel,
        out_shape=(shape, shape),
        in_specs=[SMEM, SMEM],
        out_specs=(SMEM, SMEM),
        scratch_shapes=[pltpu.SMEM((PANELS * BRD,), jnp.int32), pltpu.SMEM((BRD,), jnp.int32)],
        cost_estimate=pl.CostEstimate(flops=0, bytes_accessed=4 << 20, transcendentals=0),
    )(pos, meta)


def main_kernel(pos, slot, rep, left1, left2, *refs):
    mine, theirs, (merged, totals) = refs[:5], refs[5:10], refs[10:]

    def work(first_left, second_left):
        for half in range(2):

            def step(n, carry, half=half):
                t = half * HALF + n
                for j in range(PANELS):
                    lefts, rights = (first_left, mine) if j < 4 else (second_left, theirs)
                    d = j % 4
                    z, _ = panel_of(pos, j)
                    right = rights[d][t] if d < 3 else rights[3 + half][n]
                    product = jnp.dot(lefts[z, slot[j * BLK + t]], right, preferred_element_type=jnp.float32)
                    if j == 0:
                        merged[t, 0] = product
                    else:
                        r = rep[j * BLK + t]
                        merged[t, r] = jnp.where(r == j, 0.0, merged[t, r]) + product
                total = jnp.zeros((8, TILE), jnp.float32)
                for j in range(PANELS):
                    tile = merged[t, j]
                    part = jnp.sum((tile * tile).reshape(16, 8, TILE), axis=0)
                    total = total + jnp.where(rep[j * BLK + t] == j, part, 0.0)
                total = jnp.sum(total, axis=0, keepdims=True)
                for i in range(PANELS):
                    totals[i, pl.ds(t, 1), :] = total
                return carry

            lax.fori_loop(0, HALF, step, 0)

    own_is_mine = pos[0] // 2 == pos[3]

    @pl.when(own_is_mine)
    def _():
        work(left1, left2)

    @pl.when(jnp.logical_not(own_is_mine))
    def _():
        work(left2, left1)


def multiply(pos, slot, rep, left1, left2, mine, theirs):
    return pl.pallas_call(
        main_kernel,
        out_shape=(
            jax.ShapeDtypeStruct((BLK, PANELS, TILE, TILE), jnp.float32),
            jax.ShapeDtypeStruct((PANELS, BLK, TILE), jnp.float32),
        ),
        in_specs=[SMEM] * 3 + [VMEM] * 12,
        out_specs=(VMEM, VMEM),
        compiler_params=pltpu.CompilerParams(vmem_limit_bytes=40 << 20),
        cost_estimate=pl.CostEstimate(flops=2 * 192 * TILE**3, bytes_accessed=20 << 20, transcendentals=0),
    )(pos, slot, rep, left1, left2, *mine, *theirs)


def scale_kernel(pos, rep, merged, totals, out, factor):
    j = pl.program_id(0)

    @pl.when(j == 0)
    def _():
        factor[...] = float(PANELS * PANELS * TILE) / (jnp.sum(totals[...], axis=0) + 1e-6)

    def step(t, carry):
        tile = merged[t, rep[j * BLK + t]]
        out[0, t] = (tile * tile * factor[pl.ds(t, 1), :]).astype(jnp.bfloat16)
        return carry

    lax.fori_loop(0, BLK, step, 0)


def scale(pos, rep, merged, totals):
    def place(j, pos, rep):
        dz = jnp.where(j % 4 == 1, 3, jnp.where(j % 4 == 2, 1, jnp.where(j % 4 == 3, 2, 0)))
        core = jnp.where(j < 4, pos[3], 1 - pos[3])
        return 2 * ((pos[2] + dz) % 4) + core, 0, 0, 0

    return pl.pallas_call(
        scale_kernel,
        out_shape=jax.ShapeDtypeStruct((PANELS, BLK, TILE, TILE), jnp.bfloat16),
        grid_spec=pltpu.PrefetchScalarGridSpec(
            num_scalar_prefetch=2,
            grid=(PANELS,),
            in_specs=[VMEM, VMEM],
            out_specs=pl.BlockSpec((1, BLK, TILE, TILE), place),
            scratch_shapes=[pltpu.VMEM((BLK, TILE), jnp.float32)],
        ),
        compiler_params=pltpu.CompilerParams(vmem_limit_bytes=24 << 20),
        cost_estimate=pl.CostEstimate(flops=2 * 192 * TILE**2, bytes_accessed=20 << 20, transcendentals=0),
    )(pos, rep, merged, totals)


def on_device(tile_values, tile_rows):
    own = tile_values[0]
    pos = jnp.stack([lax.axis_index(a) for a in ("x", "y", "z", "core")]).astype(jnp.int32)

    inner = lax.ppermute(own, "x", INNER)
    outer = lax.ppermute(own, "x", OUTER)
    below = lax.ppermute(own, "z", UP)
    above = lax.ppermute(own, "z", DOWN)

    rows = lax.all_to_all(jnp.broadcast_to(tile_rows, (PANELS, BLK)), ("z", "core"), 0, 0)
    meta = lax.all_to_all(
        jnp.broadcast_to(rows.reshape(1, PANELS * BLK), (COLS, PANELS * BLK)), ("y", "x"), 0, 0
    )

    diag_a = lax.ppermute(outer[:HALF], "x", INNER)
    diag_b = lax.ppermute(inner[HALF:], "x", OUTER)
    far_a = lax.ppermute(below[:HALF], "z", UP)
    far_b = lax.ppermute(above[HALF:], "z", DOWN)

    send1 = select(select_own_kernel, pos, meta, own, inner)
    left1 = lax.all_to_all(send1, "y", 0, 0)
    send2 = select(select_other_kernel, pos, meta, outer, diag_a, diag_b)
    left2 = lax.all_to_all(send2, "y", 0, 0)

    mine = (own, below, above, far_a, far_b)
    theirs = tuple(lax.ppermute(block, "core", SWAP) for block in mine)
    slot, rep = make_plan(pos, meta)
    merged, totals = multiply(pos, slot, rep, left1, left2, mine, theirs)
    totals = lax.all_to_all(totals, ("z", "core"), 0, 0)
    return scale(pos, rep, merged, totals)[None]


def solution(mesh):
    fine = Mesh(np.asarray(mesh.devices).reshape(4, 2, 4, 4), ("z", "core", "y", "x"))
    rows, cols = ("z", "core"), ("y", "x")
    return jax.shard_map(
        on_device,
        mesh=fine,
        in_specs=(P(rows, cols, None, None), P(rows, cols)),
        out_specs=P(rows, None, cols, None, None),
        check_vma=False,
    )
```

time: 1820 us -> 127 us (0.07)
  waiting for transfers between devices: 1250 us -> 26.9 us
  blocking collectives: 201 us -> 8.46 us
  local copies, waits for them, and re-layouts: 176 us -> 15 us
  other arithmetic: 152 us -> 0.74 us
  Pallas kernels: 0 us -> 38.4 us
  starting transfers between devices: 0.04 us -> 36.4 us
  matrix products: 21 us -> 0 us
    psum x16 -> x0, waiting for transfers between devices: 1210 us -> none  [from_root(): return lax.psum(jnp.where(mine, shard, jnp.zeros_like(shard)), axis)]
    psum x17 -> x0, blocking collectives: 188 us -> none  [the longest x16 167 us: from_root(): return lax.psum(jnp.where(mine, shard, jnp.zeros_like(shard)), axis)]
    gather x48 -> x0, local copies, waits for them, and re-layouts: 170 us -> none  [the longest x16 144 us: take_section(): piece_vals[0][slot_index]]
    select_n x48 -> x0, other arithmetic: 128 us -> none  [the longest x16 128 us: take_section(): jnp.where(inside[:, :, None, None], piece_vals[0][slot_index], chosen_vals)]
    all_gather x1 -> x0, waiting for transfers between devices: 43.1 us -> none  [on_device(): lax.all_gather(tile_values, 'row', axis=0, tiled=True)]
    pallas_call x0 -> x5, Pallas kernels: none -> 38.4 us  [the longest x1 13.8 us: multiply(): pl.pallas_call(main_kernel, out_shape=(jax.ShapeDtypeStruct((BLK, PANELS,...]
    all_to_all x0 -> x4, waiting for transfers between devices: none -> 26.9 us  [the longest x1 13.8 us: on_device(): lax.all_to_all(jnp.broadcast_to(tile_rows, (PANELS, BLK)), ('z', 'core'),...]
    dot_general x3 -> x0, matrix products: 21 us -> none  [the longest x1 14.3 us: on_device(): jnp.einsum('qsc,scab->qcab', matches.astype(jnp.float32), products, preci...]
  transfers between devices with their start and end apart: 17 -> 17, of which waited for: 17 -> 3; matrix products, arithmetic and copies ran while one was open for 2% -> 6% of each run, Pallas kernels for 0% -> 15%
where the time goes in v1:
time: 127 us; the launch traced here: 126 us
  Pallas kernels  38.4 us (30%)
  starting transfers between devices  36.4 us (29%)
  waiting for transfers between devices  26.9 us (21%)
  local copies, waits for them, and re-layouts  15 us (12%)
  blocking collectives  8.46 us (7%)
    all_to_all x1, waiting for transfers between devices, on_device(): lax.all_to_all(jnp.broadcast_to(tile_rows, (PANELS, BLK)), ('z', 'core'),...  13.8 us
    pallas_call x1, Pallas kernels, multiply(): pl.pallas_call(main_kernel, out_shape=(jax.ShapeDtypeStruct((BLK, PANELS,...  13.8 us
    pallas_call x2, Pallas kernels, select(): pl.pallas_call(kernel, out_shape=jax.ShapeDtypeStruct((4, USED, TILE, TIL...  10.8 us
    all_to_all x1, blocking collectives, on_device(): totals = lax.all_to_all(totals, ('z', 'core'), 0, 0)  8.46 us
    unnamed x19, local copies, waits for them, and re-layouts  7.91 us
    pallas_call x1, Pallas kernels, make_plan(): pl.pallas_call(plan_kernel, out_shape=(shape, shape), in_specs=[SMEM, SME...  7.68 us
    ppermute x5, starting transfers between devices, on_device(): theirs = tuple((lax.ppermute(block, 'core', SWAP) for block in mine))  7.3 us
    all_to_all x1, waiting for transfers between devices, on_device(): left2 = lax.all_to_all(send2, 'y', 0, 0)  6.68 us
  transfers between devices with their start and end apart: 17, of which 3 were waited for; matrix products, arithmetic and copies ran while one was open for 6% of the time, Pallas kernels for 15%

profile of v1, /device:TPU:1, one launch (start us, length us, event | category | flops | bytes accessed | tf_op | source)
XLA Modules:
  0.0 125.9 jit_solution(7202064436296810932)
XLA Ops:
  0.0 2.0 %collective-permute-start = (bf16[24,128,128]{2,1,0:T(8,128)(2,1)}, bf16[24,128,128]{2,1,0:T(8,128)(2,1)S(1)}, u32[]{:S(2)}, u32[]{:S(2)}) collective-permute-start(bf16[24,128,128]{2,1,0:T(8,128)(2,1)} %bitcast.10), channel_id=1, source_target_pairs={{0,1},{1,0},{2,3},{3,2},{4,5},{5,4},{6,7},{7,6},{8,9},{9,8},{10,11... | collective-permute-start | bytes 2359304 | tf_op jit(solution)/shard_map/ppermute | solution.py:248
  2.0 1.8 %collective-permute-start.1 = (bf16[24,128,128]{2,1,0:T(8,128)(2,1)}, bf16[24,128,128]{2,1,0:T(8,128)(2,1)S(1)}, u32[]{:S(2)}, u32[]{:S(2)}) collective-permute-start(bf16[24,128,128]{2,1,0:T(8,128)(2,1)} %bitcast.11), channel_id=1, source_target_pairs={{0,3},{3,0},{1,2},{2,1},{4,7},{7,4},{5,6},{6,5},{8,11},{11,8},{9,1... | collective-permute-start | bytes 2359304 | tf_op jit(solution)/shard_map/ppermute | solution.py:249
  3.9 3.8 %collective-permute-start.5 = (bf16[24,128,128]{2,1,0:T(8,128)(2,1)}, bf16[24,128,128]{2,1,0:T(8,128)(2,1)}, u32[]{:S(2)}, u32[]{:S(2)}) collective-permute-start(bf16[24,128,128]{2,1,0:T(8,128)(2,1)} %bitcast.12), channel_id=1, source_target_pairs={{0,96},{32,0},{64,32},{96,64},{1,97},{33,1},{65,33},{97,65},{2,98}... | collective-permute-start | bytes 2359304 | tf_op jit(solution)/shard_map/ppermute | solution.py:251
  8.9 6.0 %all-to-all-start = ((s32[8,1,24]{2,1,0:T(1,128)}), s32[8,1,24]{2,1,0:T(1,128)S(1)}, u32[]{:S(2)}, u32[]{:S(2)}) async-start(s32[8,1,24]{2,1,0:T(1,128)} %broadcast_in_dim.15), calls=%async_computation | async-start | bytes 8192 | tf_op jit(solution)/shard_map/all_to_all | solution.py:253
  14.9 13.8 %all-to-all-done = s32[8,1,24]{2,1,0:T(1,128)S(1)} async-done(((s32[8,1,24]{2,1,0:T(1,128)}), s32[8,1,24]{2,1,0:T(1,128)S(1)}, u32[]{:S(2)}, u32[]{:S(2)}) %all-to-all-start) | async-done | bytes 800 | tf_op jit(solution)/shard_map/all_to_all | solution.py:253
  30.6 4.9 %all-to-all-start.1 = ((s32[16,1,192]{2,1,0:T(1,128)}), s32[16,1,192]{2,1,0:T(1,128)S(1)}, u32[]{:S(2)}, u32[]{:S(2)}) async-start(s32[16,1,192]{2,1,0:T(1,128)} %broadcast_in_dim.17), calls=%async_computation.1 | async-start | bytes 32768 | tf_op jit(solution)/shard_map/all_to_all | solution.py:254
  35.6 6.4 %all-to-all-done.1 = s32[16,1,192]{2,1,0:T(1,128)S(1)} async-done(((s32[16,1,192]{2,1,0:T(1,128)}), s32[16,1,192]{2,1,0:T(1,128)S(1)}, u32[]{:S(2)}, u32[]{:S(2)}) %all-to-all-start.1) | async-done | bytes 12320 | tf_op jit(solution)/shard_map/all_to_all | solution.py:254
  41.9 1.4 %copy-done.1 = bf16[1,24,128,128]{3,2,1,0:T(8,128)(2,1)S(1)} copy-done((bf16[1,24,128,128]{3,2,1,0:T(8,128)(2,1)S(1)}, bf16[1,24,128,128]{3,2,1,0:T(8,128)(2,1)}, u32[]{:S(2)}) %copy-start.1) | copy-done | bytes 786456
  43.3 5.3 %shard_map.32 = bf16[4,8,128,128]{3,2,1,0:T(8,128)(2,1)} custom-call(s32[4]{0:T(128)S(1)} %pad_add_fusion.pos, s32[16,192]{1,0:T(8,128)S(1)} %bitcast.17, bf16[24,128,128]{2,1,0:T(8,128)(2,1)S(1)} %bitcast.15, bf16[24,128,128]{2,1,0:T(8,128)(2,1)S(1)} %collective-permute-done.inner), custom_call_target="tpu_custom_call" | custom-call | bytes 4194304 | tf_op jit(solution)/shard_map/pallas_call | solution.py:95
  48.6 3.5 %all-to-all-start.2 = ((bf16[4,8,128,128]{3,2,1,0:T(8,128)(2,1)}), bf16[4,8,128,128]{3,2,1,0:T(8,128)(2,1)S(1)}, u32[]{:S(2)}, u32[]{:S(2)}) async-start(bf16[4,8,128,128]{3,2,1,0:T(8,128)(2,1)} %shard_map.32), calls=%async_computation.2 | async-start | bytes 2097152 | tf_op jit(solution)/shard_map/all_to_all | solution.py:264
  54.6 2.4 %collective-permute-start.8 = (bf16[24,128,128]{2,1,0:T(8,128)(2,1)}, bf16[24,128,128]{2,1,0:T(8,128)(2,1)}, u32[]{:S(2)}, u32[]{:S(2)}) collective-permute-start(bf16[24,128,128]{2,1,0:T(8,128)(2,1)} %bitcast.14), channel_id=1, source_target_pairs={{0,16},{16,0},{1,17},{17,1},{2,18},{18,2},{3,19},{19,3},{4,20},{20... | collective-permute-start | bytes 2359304 | tf_op jit(solution)/shard_map/ppermute | solution.py:269
  57.0 1.8 %slice.19 = bf16[12,128,128]{2,1,0:T(8,128)(2,1)} slice(bf16[24,128,128]{2,1,0:T(8,128)(2,1)} %collective-permute-done.5.refs_2_), slice={[12:24], [0:128], [0:128]} | slice | bytes 786432 | tf_op jit(solution)/shard_map/slice | solution.py:261
  58.8 1.8 %slice.18 = bf16[12,128,128]{2,1,0:T(8,128)(2,1)} slice(bf16[24,128,128]{2,1,0:T(8,128)(2,1)} %collective-permute-done.4.refs_1_), slice={[0:12], [0:128], [0:128]} | slice | bytes 786432 | tf_op jit(solution)/shard_map/slice | solution.py:260
  60.6 1.5 %collective-permute-start.6 = (bf16[12,128,128]{2,1,0:T(8,128)(2,1)}, bf16[12,128,128]{2,1,0:T(8,128)(2,1)}, u32[]{:S(2)}, u32[]{:S(2)}) collective-permute-start(bf16[12,128,128]{2,1,0:T(8,128)(2,1)} %slice.18), channel_id=1, source_target_pairs={{0,32},{32,64},{64,96},{96,0},{1,33},{33,65},{65,97},{97,1},{2,34}... | collective-permute-start | bytes 1179656 | tf_op jit(solution)/shard_map/ppermute | solution.py:260
  62.0 1.8 %collective-permute-start.10 = (bf16[24,128,128]{2,1,0:T(8,128)(2,1)}, bf16[24,128,128]{2,1,0:T(8,128)(2,1)}, u32[]{:S(2)}, u32[]{:S(2)}) collective-permute-start(bf16[24,128,128]{2,1,0:T(8,128)(2,1)} %collective-permute-done.5.refs_2_), channel_id=1, source_target_pairs={{0,16},{16,0},{1,17},{17,1},{2,18},{18,2},{3,19},{19,3},{4,20},{20... | collective-permute-start | bytes 2359304 | tf_op jit(solution)/shard_map/ppermute | solution.py:269
  63.8 2.6 %collective-permute-start.9 = (bf16[24,128,128]{2,1,0:T(8,128)(2,1)}, bf16[24,128,128]{2,1,0:T(8,128)(2,1)}, u32[]{:S(2)}, u32[]{:S(2)}) collective-permute-start(bf16[24,128,128]{2,1,0:T(8,128)(2,1)} %collective-permute-done.4.refs_1_), channel_id=1, source_target_pairs={{0,16},{16,0},{1,17},{17,1},{2,18},{18,2},{3,19},{19,3},{4,20},{20... | collective-permute-start | bytes 2359304 | tf_op jit(solution)/shard_map/ppermute | solution.py:269
  66.4 5.5 %shard_map.33 = bf16[4,8,128,128]{3,2,1,0:T(8,128)(2,1)} custom-call(s32[4]{0:T(128)S(1)} %pad_add_fusion.pos, s32[16,192]{1,0:T(8,128)S(1)} %bitcast.18, bf16[24,128,128]{2,1,0:T(8,128)(2,1)S(1)} %collective-permute-done.1.outer, bf16[12,128,128]{2,1,0:T(8,128)(2,1)S(1)} %collective-permute-done.2.diag_a, ...), custom_call_target="tpu_custom_call" | custom-call | bytes 4194304 | tf_op jit(solution)/shard_map/pallas_call | solution.py:95
  72.0 4.2 %all-to-all-start.3 = ((bf16[4,8,128,128]{3,2,1,0:T(8,128)(2,1)}), bf16[4,8,128,128]{3,2,1,0:T(8,128)(2,1)S(1)}, u32[]{:S(2)}, u32[]{:S(2)}) async-start(bf16[4,8,128,128]{3,2,1,0:T(8,128)(2,1)} %shard_map.33), calls=%async_computation.3 | async-start | bytes 2097152 | tf_op jit(solution)/shard_map/all_to_all | solution.py:266
  76.7 7.7 %shard_map.31 = (s32[192]{0:T(256)}, s32[192]{0:T(256)}) custom-call(s32[4]{0:T(128)} %copy-done.5, s32[16,192]{1,0:T(8,128)} %bitcast.19), custom_call_target="tpu_custom_call" | custom-call | bytes 4194304 | tf_op jit(solution)/shard_map/pallas_call | solution.py:142
  84.4 6.7 %all-to-all-done.3.left2 = bf16[4,8,128,128]{3,2,1,0:T(8,128)(2,1)S(1)} async-done(((bf16[4,8,128,128]{3,2,1,0:T(8,128)(2,1)}), bf16[4,8,128,128]{3,2,1,0:T(8,128)(2,1)S(1)}, u32[]{:S(2)}, u32[]{:S(2)}) %all-to-all-start.3) | async-done | bytes 1048608 | tf_op jit(solution)/shard_map/all_to_all | solution.py:266
  93.0 13.8 %shard_map.34 = (f32[24,8,128,128]{3,2,1,0:T(8,128)}, f32[8,24,128]{2,1,0:T(8,128)S(1)}) custom-call(s32[4]{0:T(128)S(1)} %copy-done.6, s32[192]{0:T(256)S(1)} %copy-done.8, s32[192]{0:T(256)S(1)} %copy-done.7, bf16[4,8,128,128]{3,2,1,0:T(8,128)(2,1)S(1)} %all-to-all-done.2.left1, bf16[4,8,128,128]{3,2,1,0:T(8,128)(2,1)S(1)} %all-to-all-done.3.left2, ...), custom_call_target="tpu_custom_call" | custom-call | flops 805306368 | bytes 20971520 | tf_op jit(solution)/shard_map/pallas_call | solution.py:195
  106.8 8.5 %all_to_all.29.totals = f32[8,24,128]{2,1,0:T(8,128)S(1)} all-to-all(f32[8,24,128]{2,1,0:T(8,128)S(1)} %get-tuple-element.12), channel_id=1, replica_groups=mesh['z'=4,'core'=2,'y'=4,'x'=4] {'z','core'}, dimensions={0} | all-to-all | bytes 196608 | tf_op jit(solution)/shard_map/all_to_all | solution.py:272
  115.3 4.6 %copy-done = f32[24,8,128,128]{3,2,1,0:T(8,128)S(1)} copy-done((f32[24,8,128,128]{3,2,1,0:T(8,128)S(1)}, f32[24,8,128,128]{3,2,1,0:T(8,128)}, u32[]{:S(2)}) %copy-start) | copy-done | bytes 12582936
  119.9 6.1 %shard_map.35 = bf16[8,24,128,128]{3,2,1,0:T(8,128)(2,1)} custom-call(s32[4]{0:T(128)S(1)} %copy-done.6, s32[192]{0:T(256)S(1)} %copy-done.7, f32[24,8,128,128]{3,2,1,0:T(8,128)S(1)} %copy-done, f32[8,24,128]{2,1,0:T(8,128)S(1)} %all_to_all.29.totals), custom_call_target="tpu_custom_call" | custom-call | flops 6291456 | bytes 20971520 | tf_op jit(solution)/shard_map/pallas_call | solution.py:229
  (45 shorter events, 8.1 us)
Async XLA Ops:
  0.0 41.9 %collective-permute-start = (bf16[24,128,128]{2,1,0:T(8,128)(2,1)}, bf16[24,128,128]{2,1,0:T(8,128)(2,1)S(1)}, u32[]{:S(2)}, u32[]{:S(2)}) collective-permute-start(bf16[24,128,128]{2,1,0:T(8,128)(2,1)} %bitcast.10), channel_id=1, source_target_pairs={{0,1},{1,0},{2,3},{3,2},{4,5},{5,4},{6,7},{7,6},{8,9},{9,8},{10,11... | collective-permute-start | bytes 2359304 | tf_op jit(solution)/shard_map/ppermute | solution.py:248
  2.0 50.1 %collective-permute-start.1 = (bf16[24,128,128]{2,1,0:T(8,128)(2,1)}, bf16[24,128,128]{2,1,0:T(8,128)(2,1)S(1)}, u32[]{:S(2)}, u32[]{:S(2)}) collective-permute-start(bf16[24,128,128]{2,1,0:T(8,128)(2,1)} %bitcast.11), channel_id=1, source_target_pairs={{0,3},{3,0},{1,2},{2,1},{4,7},{7,4},{5,6},{6,5},{8,11},{11,8},{9,1... | collective-permute-start | bytes 2359304 | tf_op jit(solution)/shard_map/ppermute | solution.py:249
  3.9 53.2 %collective-permute-start.5 = (bf16[24,128,128]{2,1,0:T(8,128)(2,1)}, bf16[24,128,128]{2,1,0:T(8,128)(2,1)}, u32[]{:S(2)}, u32[]{:S(2)}) collective-permute-start(bf16[24,128,128]{2,1,0:T(8,128)(2,1)} %bitcast.12), channel_id=1, source_target_pairs={{0,96},{32,0},{64,32},{96,64},{1,97},{33,1},{65,33},{97,65},{2,98}... | collective-permute-start | bytes 2359304 | tf_op jit(solution)/shard_map/ppermute | solution.py:251
  7.6 51.2 %collective-permute-start.4 = (bf16[24,128,128]{2,1,0:T(8,128)(2,1)}, bf16[24,128,128]{2,1,0:T(8,128)(2,1)}, u32[]{:S(2)}, u32[]{:S(2)}) collective-permute-start(bf16[24,128,128]{2,1,0:T(8,128)(2,1)} %bitcast.13), channel_id=1, source_target_pairs={{0,32},{32,64},{64,96},{96,0},{1,33},{33,65},{65,97},{97,1},{2,34}... | collective-permute-start | bytes 2359304 | tf_op jit(solution)/shard_map/ppermute | solution.py:250
  8.9 19.8 %all-to-all-start = ((s32[8,1,24]{2,1,0:T(1,128)}), s32[8,1,24]{2,1,0:T(1,128)S(1)}, u32[]{:S(2)}, u32[]{:S(2)}) async-start(s32[8,1,24]{2,1,0:T(1,128)} %broadcast_in_dim.15), calls=%async_computation | async-start | bytes 8192 | tf_op jit(solution)/shard_map/all_to_all | solution.py:253
  30.6 11.3 %all-to-all-start.1 = ((s32[16,1,192]{2,1,0:T(1,128)}), s32[16,1,192]{2,1,0:T(1,128)S(1)}, u32[]{:S(2)}, u32[]{:S(2)}) async-start(s32[16,1,192]{2,1,0:T(1,128)} %broadcast_in_dim.17), calls=%async_computation.1 | async-start | bytes 32768 | tf_op jit(solution)/shard_map/all_to_all | solution.py:254
  35.6 41.1 %copy-start.5 = (s32[4]{0:T(128)}, s32[4]{0:T(128)S(1)}, u32[]{:S(2)}) copy-start(s32[4]{0:T(128)S(1)} %pad_add_fusion.pos) | copy-start | bytes 52
  41.9 34.8 %copy-start.4 = (s32[16,1,192]{2,0,1:T(8,128)}, s32[16,1,192]{2,0,1:T(8,128)S(1)}, u32[]{:S(2)}) copy-start(s32[16,1,192]{2,0,1:T(8,128)S(1)} %copy.5) | copy-start | bytes 36868
  41.9 6.7 %copy-start.3 = (bf16[24,128,128]{2,1,0:T(8,128)(2,1)}, bf16[24,128,128]{2,1,0:T(8,128)(2,1)S(1)}, u32[]{:S(2)}) copy-start(bf16[24,128,128]{2,1,0:T(8,128)(2,1)S(1)} %collective-permute-done.inner) | copy-start | bytes 2359300
  41.9 1.4 %copy-start.1 = (bf16[1,24,128,128]{3,2,1,0:T(8,128)(2,1)S(1)}, bf16[1,24,128,128]{3,2,1,0:T(8,128)(2,1)}, u32[]{:S(2)}) copy-start(bf16[1,24,128,128]{3,2,1,0:T(8,128)(2,1)} %param.2) | copy-start | bytes 2359300
  43.3 47.8 %copy-start.2 = (bf16[1,24,128,128]{3,2,1,0:T(8,128)(2,1)S(1)}, bf16[1,24,128,128]{3,2,1,0:T(8,128)(2,1)}, u32[]{:S(2)}) copy-start(bf16[1,24,128,128]{3,2,1,0:T(8,128)(2,1)} %param.2) | copy-start | bytes 2359300
  48.6 23.3 %all-to-all-start.2 = ((bf16[4,8,128,128]{3,2,1,0:T(8,128)(2,1)}), bf16[4,8,128,128]{3,2,1,0:T(8,128)(2,1)S(1)}, u32[]{:S(2)}, u32[]{:S(2)}) async-start(bf16[4,8,128,128]{3,2,1,0:T(8,128)(2,1)} %shard_map.32), calls=%async_computation.2 | async-start | bytes 2097152 | tf_op jit(solution)/shard_map/all_to_all | solution.py:264
  52.2 9.8 %collective-permute-start.2 = (bf16[12,128,128]{2,1,0:T(8,128)(2,1)S(1)}, bf16[12,128,128]{2,1,0:T(8,128)(2,1)S(1)}, u32[]{:S(2)}, u32[]{:S(2)}) collective-permute-start(bf16[12,128,128]{2,1,0:T(8,128)(2,1)S(1)} %slice.16), channel_id=1, source_target_pairs={{0,1},{1,0},{2,3},{3,2},{4,5},{5,4},{6,7},{7,6},{8,9},{9,8},{10,11... | collective-permute-start | bytes 1179656 | tf_op jit(solution)/shard_map/ppermute | solution.py:258
  53.6 10.2 %collective-permute-start.3 = (bf16[12,128,128]{2,1,0:T(8,128)(2,1)S(1)}, bf16[12,128,128]{2,1,0:T(8,128)(2,1)S(1)}, u32[]{:S(2)}, u32[]{:S(2)}) collective-permute-start(bf16[12,128,128]{2,1,0:T(8,128)(2,1)S(1)} %slice.17), channel_id=1, source_target_pairs={{0,3},{3,0},{1,2},{2,1},{4,7},{7,4},{5,6},{6,5},{8,11},{11,8},{9,1... | collective-permute-start | bytes 1179656 | tf_op jit(solution)/shard_map/ppermute | solution.py:259
  54.6 29.7 %collective-permute-start.8 = (bf16[24,128,128]{2,1,0:T(8,128)(2,1)}, bf16[24,128,128]{2,1,0:T(8,128)(2,1)}, u32[]{:S(2)}, u32[]{:S(2)}) collective-permute-start(bf16[24,128,128]{2,1,0:T(8,128)(2,1)} %bitcast.14), channel_id=1, source_target_pairs={{0,16},{16,0},{1,17},{17,1},{2,18},{18,2},{3,19},{19,3},{4,20},{20... | collective-permute-start | bytes 2359304 | tf_op jit(solution)/shard_map/ppermute | solution.py:269
  58.8 17.3 %collective-permute-start.7 = (bf16[12,128,128]{2,1,0:T(8,128)(2,1)}, bf16[12,128,128]{2,1,0:T(8,128)(2,1)S(1)}, u32[]{:S(2)}, u32[]{:S(2)}) collective-permute-start(bf16[12,128,128]{2,1,0:T(8,128)(2,1)} %slice.19), channel_id=1, source_target_pairs={{0,96},{32,0},{64,32},{96,64},{1,97},{33,1},{65,33},{97,65},{2,98}... | collective-permute-start | bytes 1179656 | tf_op jit(solution)/shard_map/ppermute | solution.py:261
  60.6 15.9 %collective-permute-start.6 = (bf16[12,128,128]{2,1,0:T(8,128)(2,1)}, bf16[12,128,128]{2,1,0:T(8,128)(2,1)}, u32[]{:S(2)}, u32[]{:S(2)}) collective-permute-start(bf16[12,128,128]{2,1,0:T(8,128)(2,1)} %slice.18), channel_id=1, source_target_pairs={{0,32},{32,64},{64,96},{96,0},{1,33},{33,65},{65,97},{97,1},{2,34}... | collective-permute-start | bytes 1179656 | tf_op jit(solution)/shard_map/ppermute | solution.py:260
  62.0 22.3 %collective-permute-start.10 = (bf16[24,128,128]{2,1,0:T(8,128)(2,1)}, bf16[24,128,128]{2,1,0:T(8,128)(2,1)}, u32[]{:S(2)}, u32[]{:S(2)}) collective-permute-start(bf16[24,128,128]{2,1,0:T(8,128)(2,1)} %collective-permute-done.5.refs_2_), channel_id=1, source_target_pairs={{0,16},{16,0},{1,17},{17,1},{2,18},{18,2},{3,19},{19,3},{4,20},{20... | collective-permute-start | bytes 2359304 | tf_op jit(solution)/shard_map/ppermute | solution.py:269
  63.8 20.6 %collective-permute-start.9 = (bf16[24,128,128]{2,1,0:T(8,128)(2,1)}, bf16[24,128,128]{2,1,0:T(8,128)(2,1)}, u32[]{:S(2)}, u32[]{:S(2)}) collective-permute-start(bf16[24,128,128]{2,1,0:T(8,128)(2,1)} %collective-permute-done.4.refs_1_), channel_id=1, source_target_pairs={{0,16},{16,0},{1,17},{17,1},{2,18},{18,2},{3,19},{19,3},{4,20},{20... | collective-permute-start | bytes 2359304 | tf_op jit(solution)/shard_map/ppermute | solution.py:269
  72.0 19.1 %all-to-all-start.3 = ((bf16[4,8,128,128]{3,2,1,0:T(8,128)(2,1)}), bf16[4,8,128,128]{3,2,1,0:T(8,128)(2,1)S(1)}, u32[]{:S(2)}, u32[]{:S(2)}) async-start(bf16[4,8,128,128]{3,2,1,0:T(8,128)(2,1)} %shard_map.33), calls=%async_computation.3 | async-start | bytes 2097152 | tf_op jit(solution)/shard_map/all_to_all | solution.py:266
  76.1 8.2 %collective-permute-start.12 = (bf16[12,128,128]{2,1,0:T(8,128)(2,1)S(1)}, bf16[12,128,128]{2,1,0:T(8,128)(2,1)}, u32[]{:S(2)}, u32[]{:S(2)}) collective-permute-start(bf16[12,128,128]{2,1,0:T(8,128)(2,1)S(1)} %collective-permute-done.7.refs_4_), channel_id=1, source_target_pairs={{0,16},{16,0},{1,17},{17,1},{2,18},{18,2},{3,19},{19,3},{4,20},{20... | collective-permute-start | bytes 1179656 | tf_op jit(solution)/shard_map/ppermute | solution.py:269
  76.4 8.0 %collective-permute-start.11 = (bf16[12,128,128]{2,1,0:T(8,128)(2,1)}, bf16[12,128,128]{2,1,0:T(8,128)(2,1)}, u32[]{:S(2)}, u32[]{:S(2)}) collective-permute-start(bf16[12,128,128]{2,1,0:T(8,128)(2,1)} %collective-permute-done.6.refs_3_), channel_id=1, source_target_pairs={{0,16},{16,0},{1,17},{17,1},{2,18},{18,2},{3,19},{19,3},{4,20},{20... | collective-permute-start | bytes 1179656 | tf_op jit(solution)/shard_map/ppermute | solution.py:269
  92.3 0.7 copy-start.8
  115.3 4.6 %copy-start = (f32[24,8,128,128]{3,2,1,0:T(8,128)S(1)}, f32[24,8,128,128]{3,2,1,0:T(8,128)}, u32[]{:S(2)}) copy-start(f32[24,8,128,128]{3,2,1,0:T(8,128)} %get-tuple-element.11.merged) | copy-start | bytes 37748740
  (2 other events, 1.2 us)

commit v2 on v0

v2 whole, which is shorter than its diff:
```python
import jax
import jax.numpy as jnp
import numpy as np
from jax import lax
from jax.experimental import pallas as pl
from jax.experimental.pallas import tpu as pltpu
from jax.sharding import Mesh, PartitionSpec as P

TILE = 128
BLK = 24
USED = 8
PANELS = 8
COLS = 16
GROUP = 4
AT = 10
MERGE = PANELS * BLK
END = 2 * MERGE
OWN_ROWS = 32
LIMIT = 12 << 20
PLAN_COST = 32 << 20
TOKEN_COST = 16 << 20
LISTS_COST = 0
SPREAD_COST = 0
DZ = (0, 3, 1, 2)
INNER = [(0, 1), (1, 0), (2, 3), (3, 2)]
OUTER = [(0, 3), (3, 0), (1, 2), (2, 1)]
UP = [(i, (i + 1) % 4) for i in range(4)]
DOWN = [(i, (i + 3) % 4) for i in range(4)]
ACROSS = [(i, (i + 2) % 4) for i in range(4)]
SWAP = [(0, 1), (1, 0)]

SMEM = pl.BlockSpec(memory_space=pltpu.SMEM)
VMEM = pl.BlockSpec(memory_space=pltpu.VMEM)
ANY = pl.BlockSpec(memory_space=pl.ANY)


def split_row(row):
    upper = (row >= BLK).astype(jnp.int32)
    return upper, row - upper * BLK


def used_rows(load):
    mask = jnp.int32(0)
    for t in range(BLK):
        upper, local = split_row(load(t))
        mask = mask | lax.shift_left(jnp.int32(1), local)
    return upper, mask


def spread_kernel(rows, out):
    for i in range(PANELS):
        out[i] = rows[...]


def spread(rows):
    return pl.pallas_call(
        spread_kernel,
        out_shape=jax.ShapeDtypeStruct((PANELS, 1, TILE), jnp.int32),
        in_specs=[VMEM],
        out_specs=VMEM,
        compiler_params=pltpu.CompilerParams(vmem_limit_bytes=1 << 20),
        cost_estimate=pl.CostEstimate(flops=0, bytes_accessed=SPREAD_COST, transcendentals=0),
    )(rows)


def token_kernel(*refs):
    refs[-1][0] = jnp.int32(0)


def token(cost, *arrays):
    return pl.pallas_call(
        token_kernel,
        out_shape=pltpu.SMEM((8,), jnp.int32),
        in_specs=[ANY] * len(arrays),
        out_specs=SMEM,
        compiler_params=pltpu.CompilerParams(vmem_limit_bytes=1 << 20),
        cost_estimate=pl.CostEstimate(flops=cost * 1000, bytes_accessed=cost, transcendentals=0),
    )(*arrays)


def bit(mask, v):
    return lax.shift_right_logical(mask, jnp.int32(v)) & 1


def lists_kernel(pos, req, lists):
    for pair in range(2):
        for dest in range(4):
            base = (pair * 4 + dest) * 16
            upper, mask = used_rows(lambda t: req[dest * 4 + pos[0], pair, t])
            count = jnp.int32(0)
            for v in range(BLK):
                lists[base + count] = jnp.int32(v)
                count = count + bit(mask, v)
            lists[base + 15] = upper
    for n in range(4):
        lists[AT + n] = pos[n]


def make_lists(pos, req):
    return pl.pallas_call(
        lists_kernel,
        out_shape=pltpu.SMEM((128,), jnp.int32),
        in_specs=[SMEM, SMEM],
        out_specs=SMEM,
        compiler_params=pltpu.CompilerParams(vmem_limit_bytes=1 << 20),
        cost_estimate=pl.CostEstimate(flops=0, bytes_accessed=LISTS_COST, transcendentals=0),
    )(pos, req)


def select_own_kernel(lists, _, own, inner, out):
    pair = lists[AT] // 2
    side = lists[AT] % 2
    for dest in range(4):
        base = (pair * 4 + dest) * 16
        upper = lists[base + 15]

        def copy(source):
            for n in range(USED):
                out[dest, n] = source[lists[base + n]]

        pl.when(upper == side)(lambda: copy(own))
        pl.when(upper != side)(lambda: copy(inner))


def select_other_kernel(lists, _, outer, diag, *outs):
    pair = 1 - lists[AT] // 2
    side = (3 - lists[AT]) % 2
    for away in range(4):
        base = (pair * 4 + (lists[AT + 1] + away) % 4) * 16
        upper = lists[base + 15]

        def copy(source, out=outs[away], base=base):
            for n in range(USED):
                out[n] = source[lists[base + n]]

        pl.when(upper == side)(lambda: copy(outer))
        pl.when(upper != side)(lambda: copy(diag))


def select(kernel, out_shape, lists, after, *blocks):
    return pl.pallas_call(
        kernel,
        out_shape=out_shape,
        in_specs=[SMEM, ANY] + [VMEM] * len(blocks),
        out_specs=jax.tree.map(lambda _: VMEM, out_shape),
        compiler_params=pltpu.CompilerParams(vmem_limit_bytes=8 << 20),
        cost_estimate=pl.CostEstimate(flops=0, bytes_accessed=2 << 20, transcendentals=0),
    )(lists, after, *blocks)


def panel_of(pos, at, j):
    z = (pos[at + 2] + DZ[j % 4]) % 4
    pair = pos[at] // 2
    return z, 2 * z + (pair if j < 4 else 1 - pair)


def plan_kernel(pos, rows, req, _, plan, rank):
    uppers = []
    sources = []
    for j in range(PANELS):
        z, panel = panel_of(pos, 0, j)
        upper, mask = used_rows(lambda t: rows[panel, 0, t])
        uppers.append(upper)
        sources.append(z * 4 + 2 * (panel % 2) + upper)
        count = jnp.int32(0)
        for v in range(BLK):
            rank[j * BLK + v] = count
            count = count + bit(mask, v)

    def step(t, carry):
        out_rows = []
        for j in range(PANELS):
            _, panel = panel_of(pos, 0, j)
            local = rows[panel, 0, t] - uppers[j] * BLK
            plan[j * BLK + t] = rank[j * BLK + local]
            out_row = req[sources[j], 0, OWN_ROWS + local]
            place = jnp.int32(j)
            for earlier in reversed(range(j)):
                place = jnp.where(out_rows[earlier] == out_row, earlier, place)
            out_rows.append(out_row)
            plan[MERGE + j * BLK + t] = place
        return carry

    lax.fori_loop(0, BLK, step, 0)
    for n in range(4):
        plan[END + n] = pos[n]


def make_plan(pos, rows, req, after):
    return pl.pallas_call(
        plan_kernel,
        out_shape=pltpu.SMEM((512,), jnp.int32),
        in_specs=[SMEM] * 3 + [ANY],
        out_specs=SMEM,
        scratch_shapes=[pltpu.SMEM((PANELS * BLK,), jnp.int32)],
        compiler_params=pltpu.CompilerParams(vmem_limit_bytes=1 << 20),
        cost_estimate=pl.CostEstimate(flops=0, bytes_accessed=PLAN_COST, transcendentals=0),
    )(pos, rows, req, after)


def products(plan, left, rights, first, n, put):
    for u in range(GROUP):
        t = n * GROUP + u
        for d in range(4):
            j = first + d
            z, _ = panel_of(plan, END, j)
            put(t, j, jnp.dot(left[z, plan[j * BLK + t]], rights[d][t], preferred_element_type=jnp.float32))


def run_both(plan, first, mine, theirs, work):
    same = plan[END] // 2 == plan[END + 3]
    here, there = (mine, theirs) if first == 0 else (theirs, mine)
    pl.when(same)(lambda: work(here))
    pl.when(jnp.logical_not(same))(lambda: work(there))


def own_kernel(plan, left, *refs):
    mine, theirs, (early,) = refs[:4], refs[4:8], refs[8:]

    def work(rights):
        def step(n, carry):
            def put(t, j, product):
                if j == 0:
                    early[t, 0] = product
                else:
                    r = plan[MERGE + j * BLK + t]
                    early[t, r] = jnp.where(r == j, 0.0, early[t, r]) + product

            products(plan, left, rights, 0, n, put)
            return carry

        lax.fori_loop(0, BLK // GROUP, step, 0)

    run_both(plan, 0, mine, theirs, work)


def other_kernel(plan, left0, left1, left2, left3, *refs):
    mine, theirs, (early, merged, totals, left, sums) = refs[:4], refs[4:8], refs[8:]
    for away, piece in enumerate((left0, left1, left2, left3)):
        left[(plan[END + 1] - away) % 4] = piece[...]

    def add_up(n):
        for u in range(GROUP):
            t = n * GROUP + u
            total = jnp.zeros((8, TILE), jnp.float32)
            for j in range(PANELS):
                tile = merged[t, j]
                part = jnp.sum((tile * tile).reshape(16, 8, TILE), axis=0)
                total = total + jnp.where(plan[MERGE + j * BLK + t] == j, part, 0.0)
            sums[pl.ds(t, 1), :] = jnp.sum(total, axis=0, keepdims=True)

    def work(rights):
        def step(n, carry):
            def put(t, j, product):
                r = plan[MERGE + j * BLK + t]
                merged[t, r] = jnp.where(r == j, 0.0, merged[t, r]) + product

            for u in range(GROUP):
                for j in range(4):
                    merged[n * GROUP + u, j] = early[n * GROUP + u, j]
            products(plan, left, rights, 4, n, put)
            add_up(jnp.maximum(n - 1, 0))
            return carry

        lax.fori_loop(0, BLK // GROUP, step, 0)

    run_both(plan, 4, mine, theirs, work)
    add_up(BLK // GROUP - 1)
    for i in range(PANELS):
        totals[i] = sums[...]


EARLY = (BLK, 4, TILE, TILE)
MERGED = (BLK, PANELS, TILE, TILE)


def in_vmem(*arrays):
    return tuple(pltpu.with_memory_space_constraint(a, pltpu.VMEM) for a in arrays)


def multiply_own(plan, left, mine, theirs):
    return pl.pallas_call(
        own_kernel,
        out_shape=pltpu.VMEM(EARLY, jnp.float32),
        in_specs=[SMEM] + [VMEM] * 9,
        out_specs=VMEM,
        compiler_params=pltpu.CompilerParams(vmem_limit_bytes=LIMIT),
        cost_estimate=pl.CostEstimate(flops=2 * 96 * TILE**3, bytes_accessed=16 << 20, transcendentals=0),
    )(plan, *in_vmem(left, *mine, *theirs))


def multiply_other(plan, left, mine, theirs, early):
    return pl.pallas_call(
        other_kernel,
        out_shape=(pltpu.VMEM(MERGED, jnp.float32), pltpu.HBM((PANELS, BLK, TILE), jnp.float32)),
        in_specs=[SMEM] + [VMEM] * 13,
        out_specs=(VMEM, VMEM),
        scratch_shapes=[pltpu.VMEM((4, USED, TILE, TILE), jnp.bfloat16), pltpu.VMEM((BLK, TILE), jnp.float32)],
        compiler_params=pltpu.CompilerParams(vmem_limit_bytes=LIMIT),
        cost_estimate=pl.CostEstimate(flops=2 * 96 * TILE**3, bytes_accessed=16 << 20, transcendentals=0),
    )(plan, *in_vmem(*left, *mine, *theirs, early))


def scale_kernel(plan, merged, totals, out, factor):
    j = pl.program_id(0)

    @pl.when(j == 0)
    def _():
        factor[...] = float(PANELS * PANELS * TILE) / (jnp.sum(totals[...], axis=0) + 1e-6)

    def step(n, carry):
        for u in range(GROUP):
            t = n * GROUP + u
            tile = merged[t, plan[MERGE + j * BLK + t]]
            out[0, t] = (tile * tile * factor[pl.ds(t, 1), :]).astype(jnp.bfloat16)
        return carry

    lax.fori_loop(0, BLK // GROUP, step, 0)


def scale(plan, merged, totals):
    def place(j, plan):
        d = j % 4
        z = (plan[END + 2] + jnp.where(d == 1, 3, jnp.where(d == 2, 1, jnp.where(d == 3, 2, 0)))) % 4
        pair = plan[END] // 2
        return 2 * z + jnp.where(j < 4, pair, 1 - pair), 0, 0, 0

    return pl.pallas_call(
        scale_kernel,
        out_shape=jax.ShapeDtypeStruct((PANELS, BLK, TILE, TILE), jnp.bfloat16),
        grid_spec=pltpu.PrefetchScalarGridSpec(
            num_scalar_prefetch=1,
            grid=(PANELS,),
            in_specs=[VMEM, VMEM],
            out_specs=pl.BlockSpec((1, BLK, TILE, TILE), place),
            scratch_shapes=[pltpu.VMEM((BLK, TILE), jnp.float32)],
        ),
        compiler_params=pltpu.CompilerParams(vmem_limit_bytes=LIMIT),
        cost_estimate=pl.CostEstimate(flops=2 * 192 * TILE**2, bytes_accessed=20 << 20, transcendentals=0),
    )(plan, *in_vmem(merged), totals)


def on_device(tile_values, tile_rows):
    own = tile_values[0]
    pos = jnp.stack([lax.axis_index(a) for a in ("x", "y", "z", "core")]).astype(jnp.int32)
    wide_rows = jnp.pad(tile_rows, ((0, 0), (0, TILE - BLK)))

    inner = lax.ppermute(own, "x", INNER)
    outer = lax.ppermute(own, "x", OUTER)
    rows = lax.all_to_all(spread(wide_rows), ("z", "core"), 0, 0)
    own_rows = jnp.pad(tile_rows, ((0, 0), (OWN_ROWS, TILE - OWN_ROWS - BLK)))
    asks = jnp.broadcast_to(rows.reshape(4, 1, 2, TILE) + own_rows, (4, 4, 2, TILE)).reshape(COLS, 2, TILE)
    req = lax.all_to_all(asks, ("y", "x"), 0, 0)
    own_z, rows_z = lax.optimization_barrier((own, rows))
    below = lax.ppermute(own_z, "z", UP)
    above = lax.ppermute(own_z, "z", DOWN)

    lists = make_lists(pos, req)
    arrived = token(TOKEN_COST, inner, outer)
    send1 = select(select_own_kernel, pltpu.HBM((4, USED, TILE, TILE), jnp.bfloat16), lists, arrived, own, inner)
    left1 = lax.all_to_all(send1, "y", 0, 0)
    diag = lax.ppermute(outer, "x", INNER)

    far = lax.ppermute(below, "z", UP)
    plan = make_plan(pos, rows_z, req, send1)
    sent = pltpu.HBM((USED, TILE, TILE), jnp.bfloat16)
    ready = token(0, left1, plan)
    send2 = select(select_other_kernel, (sent,) * 4, lists, ready, outer, diag)
    kept, far_later = lax.optimization_barrier((send2[0], far))
    left2 = (
        kept,
        lax.ppermute(send2[1], "y", UP),
        lax.ppermute(send2[2], "y", ACROSS),
        lax.ppermute(send2[3], "y", DOWN),
    )

    mine = (own, below, above, far)
    theirs = tuple(lax.ppermute(block, "core", SWAP) for block in (own, below, above, far_later))
    early = multiply_own(plan, left1, mine, theirs)
    merged, totals = multiply_other(plan, left2, mine, theirs, early)
    totals = lax.all_to_all(totals, ("z", "core"), 0, 0)
    return scale(plan, merged, totals)[None]


def solution(mesh):
    fine = Mesh(np.asarray(mesh.devices).reshape(4, 2, 4, 4), ("z", "core", "y", "x"))
    rows, cols = ("z", "core"), ("y", "x")
    return jax.shard_map(
        on_device,
        mesh=fine,
        in_specs=(P(rows, cols, None, None), P(rows, cols)),
        out_specs=P(rows, None, cols, None, None),
        check_vma=False,
    )
```

time: 1820 us -> 99.3 us (0.05)
  waiting for transfers between devices: 1250 us -> 28.3 us
  blocking collectives: 201 us -> 9.01 us
  local copies, waits for them, and re-layouts: 176 us -> 5.15 us
  other arithmetic: 152 us -> 0.08 us
  starting transfers between devices: 0.04 us -> 31.2 us
  Pallas kernels: 0 us -> 24.9 us
  matrix products: 21 us -> 0 us
    psum x16 -> x0, waiting for transfers between devices: 1210 us -> none  [from_root(): return lax.psum(jnp.where(mine, shard, jnp.zeros_like(shard)), axis)]
    psum x17 -> x0, blocking collectives: 188 us -> none  [the longest x16 167 us: from_root(): return lax.psum(jnp.where(mine, shard, jnp.zeros_like(shard)), axis)]
    gather x48 -> x0, local copies, waits for them, and re-layouts: 170 us -> none  [the longest x16 144 us: take_section(): piece_vals[0][slot_index]]
    select_n x48 -> x0, other arithmetic: 128 us -> none  [the longest x16 128 us: take_section(): jnp.where(inside[:, :, None, None], piece_vals[0][slot_index], chosen_vals)]
    all_gather x1 -> x0, waiting for transfers between devices: 43.1 us -> none  [on_device(): lax.all_gather(tile_values, 'row', axis=0, tiled=True)]
    pallas_call x0 -> x10, Pallas kernels: none -> 24.9 us  [the longest x1 6.04 us: multiply_other(): pl.pallas_call(other_kernel, out_shape=(pltpu.VMEM(MERGED, jnp.float32),...]
    dot_general x3 -> x0, matrix products: 21 us -> none  [the longest x1 14.3 us: on_device(): jnp.einsum('qsc,scab->qcab', matches.astype(jnp.float32), products, preci...]
    ppermute x0 -> x13, waiting for transfers between devices: none -> 18.8 us  [the longest x1 6.42 us: on_device(): lax.ppermute(send2[2], 'y', ACROSS)]
  transfers between devices with their start and end apart: 17 -> 16, of which waited for: 17 -> 8; matrix products, arithmetic and copies ran while one was open for 2% -> 2% of each run, Pallas kernels for 0% -> 14%
where the time goes in v2:
time: 99.3 us; the launch traced here: 98.7 us
  starting transfers between devices  31.2 us (31%)
  waiting for transfers between devices  28.3 us (28%)
  Pallas kernels  24.9 us (25%)
  blocking collectives  9.01 us (9%)
  local copies, waits for them, and re-layouts  5.15 us (5%)
    all_to_all x1, blocking collectives, on_device(): totals = lax.all_to_all(totals, ('z', 'core'), 0, 0)  9.01 us
    all_to_all x1, starting transfers between devices, on_device(): rows = lax.all_to_all(spread(wide_rows), ('z', 'core'), 0, 0)  6.48 us
    ppermute x1, waiting for transfers between devices, on_device(): lax.ppermute(send2[2], 'y', ACROSS)  6.42 us
    pallas_call x1, Pallas kernels, multiply_other(): pl.pallas_call(other_kernel, out_shape=(pltpu.VMEM(MERGED, jnp.float32),...  6.04 us
    ppermute x4, starting transfers between devices, on_device(): lax.ppermute(block, 'core', SWAP)  5.87 us
    all_to_all x1, starting transfers between devices, on_device(): req = lax.all_to_all(asks, ('y', 'x'), 0, 0)  5.53 us
    all_to_all x1, waiting for transfers between devices, on_device(): req = lax.all_to_all(asks, ('y', 'x'), 0, 0)  4.88 us
    ppermute x1, waiting for transfers between devices, on_device(): below = lax.ppermute(own_z, 'z', UP)  4.61 us
  transfers between devices with their start and end apart: 16, of which 8 were waited for; matrix products, arithmetic and copies ran while one was open for 2% of the time, Pallas kernels for 14%

profile of v2, /device:TPU:1, one launch (start us, length us, event | category | flops | bytes accessed | tf_op | source)
XLA Modules:
  0.0 98.7 jit_solution(4237519093608001449)
XLA Ops:
  0.0 3.3 %collective-permute-start.1 = (bf16[24,128,128]{2,1,0:T(8,128)(2,1)}, bf16[24,128,128]{2,1,0:T(8,128)(2,1)S(1)}, u32[]{:S(2)}, u32[]{:S(2)}) collective-permute-start(bf16[24,128,128]{2,1,0:T(8,128)(2,1)} %bitcast.10), channel_id=1, source_target_pairs={{0,3},{3,0},{1,2},{2,1},{4,7},{7,4},{5,6},{6,5},{8,11},{11,8},{9,1... | collective-permute-start | bytes 2359304 | tf_op jit(solution)/shard_map/ppermute | solution.py:349
  4.7 6.5 %all-to-all-start = ((s32[8,1,128]{2,1,0:T(1,128)}), s32[8,1,128]{2,1,0:T(1,128)S(1)}, u32[]{:S(2)}, u32[]{:S(2)}) async-start(s32[8,1,128]{2,1,0:T(1,128)} %shard_map.28), calls=%async_computation | async-start | bytes 8192 | tf_op jit(solution)/shard_map/all_to_all | solution.py:350
  11.2 4.5 %all-to-all-done.rows = s32[8,1,128]{2,1,0:T(1,128)S(1)} async-done(((s32[8,1,128]{2,1,0:T(1,128)}), s32[8,1,128]{2,1,0:T(1,128)S(1)}, u32[]{:S(2)}, u32[]{:S(2)}) %all-to-all-start) | async-done | bytes 4128 | tf_op jit(solution)/shard_map/all_to_all | solution.py:350
  16.3 5.5 %all-to-all-start.1 = ((s32[16,2,128]{2,1,0:T(2,128)}), s32[16,2,128]{2,1,0:T(2,128)S(1)}, u32[]{:S(2)}, u32[]{:S(2)}) async-start(s32[16,2,128]{2,1,0:T(2,128)} %bitcast.7), calls=%async_computation.1 | async-start | bytes 32768 | tf_op jit(solution)/shard_map/all_to_all | solution.py:353
  23.4 4.9 %all-to-all-done.1.req = s32[16,2,128]{2,1,0:T(2,128)S(1)} async-done(((s32[16,2,128]{2,1,0:T(2,128)}), s32[16,2,128]{2,1,0:T(2,128)S(1)}, u32[]{:S(2)}, u32[]{:S(2)}) %all-to-all-start.1) | async-done | bytes 16416 | tf_op jit(solution)/shard_map/all_to_all | solution.py:353
  28.3 1.6 %shard_map.29.lists = s32[128]{0:T(128)S(4)} custom-call(s32[4]{0:T(128)S(1)} %pad_add_fusion.pos, s32[16,2,128]{2,1,0:T(2,128)S(1)} %all-to-all-done.1.req), custom_call_target="tpu_custom_call" | custom-call | tf_op jit(solution)/shard_map/pallas_call | solution.py:100
  31.3 2.2 %shard_map.31._ = bf16[4,8,128,128]{3,2,1,0:T(8,128)(2,1)} custom-call(s32[128]{0:T(128)S(4)} %shard_map.29.lists, s32[8]{0:T(128)S(4)} %shard_map.30._, bf16[24,128,128]{2,1,0:T(8,128)(2,1)S(1)} %bitcast.14, bf16[24,128,128]{2,1,0:T(8,128)(2,1)} %collective-permute-done.refs_0_.inner), custom_call_target="tpu_custom_call" | custom-call | bytes 2097152 | tf_op jit(solution)/shard_map/pallas_call | solution.py:141
  33.5 3.5 %all-to-all-start.2 = ((bf16[4,8,128,128]{3,2,1,0:T(8,128)(2,1)}), bf16[4,8,128,128]{3,2,1,0:T(8,128)(2,1)S(1)}, u32[]{:S(2)}, u32[]{:S(2)}) async-start(bf16[4,8,128,128]{3,2,1,0:T(8,128)(2,1)} %shard_map.31._), calls=%async_computation.2 | async-start | bytes 2097152 | tf_op jit(solution)/shard_map/all_to_all | solution.py:361
  37.4 4.6 %collective-permute-done.3.refs_1_ = bf16[24,128,128]{2,1,0:T(8,128)(2,1)S(1)} collective-permute-done((bf16[24,128,128]{2,1,0:T(8,128)(2,1)}, bf16[24,128,128]{2,1,0:T(8,128)(2,1)S(1)}, u32[]{:S(2)}, u32[]{:S(2)}) %collective-permute-start.3) | collective-permute-done | bytes 786464 | tf_op jit(solution)/shard_map/ppermute | solution.py:355
  42.0 2.2 %collective-permute-start.9 = (bf16[24,128,128]{2,1,0:T(8,128)(2,1)S(1)}, bf16[24,128,128]{2,1,0:T(8,128)(2,1)}, u32[]{:S(2)}, u32[]{:S(2)}) collective-permute-start(bf16[24,128,128]{2,1,0:T(8,128)(2,1)S(1)} %bitcast.15), channel_id=1, source_target_pairs={{0,16},{16,0},{1,17},{17,1},{2,18},{18,2},{3,19},{19,3},{4,20},{20... | collective-permute-start | bytes 2359304 | tf_op jit(solution)/shard_map/ppermute | solution.py:378
  44.3 1.2 %copy-done = bf16[4,8,128,128]{3,2,1,0:T(8,128)(2,1)S(1)} copy-done((bf16[4,8,128,128]{3,2,1,0:T(8,128)(2,1)S(1)}, bf16[4,8,128,128]{3,2,1,0:T(8,128)(2,1)}, u32[]{:S(2)}) %copy-start) | copy-done | bytes 1048600
  45.5 3.9 %shard_map.32.refs_1_.plan = s32[512]{0:T(512)S(4)} custom-call(s32[4]{0:T(128)S(1)} %pad_add_fusion.pos, s32[8,1,128]{2,1,0:T(1,128)S(1)} %all-to-all-done.rows, s32[16,2,128]{2,1,0:T(2,128)S(1)} %all-to-all-done.1.req, bf16[4,8,128,128]{3,2,1,0:T(8,128)(2,1)S(1)} %copy-done), custom_call_target="tpu_custom_call" | custom-call | bytes 33554432 | tf_op jit(solution)/shard_map/pallas_call | solution.py:190
  50.0 4.3 %collective-permute-done.2.diag = bf16[24,128,128]{2,1,0:T(8,128)(2,1)} collective-permute-done((bf16[24,128,128]{2,1,0:T(8,128)(2,1)}, bf16[24,128,128]{2,1,0:T(8,128)(2,1)}, u32[]{:S(2)}, u32[]{:S(2)}) %collective-permute-start.2) | collective-permute-done | bytes 786464 | tf_op jit(solution)/shard_map/ppermute | solution.py:362
  54.4 1.1 %copy-done.3 = bf16[24,128,128]{2,1,0:T(8,128)(2,1)S(1)} copy-done((bf16[24,128,128]{2,1,0:T(8,128)(2,1)S(1)}, bf16[24,128,128]{2,1,0:T(8,128)(2,1)}, u32[]{:S(2)}) %copy-start.3) | copy-done | bytes 786456
  55.5 2.2 %shard_map.34 = (bf16[8,128,128]{2,1,0:T(8,128)(2,1)}, bf16[8,128,128]{2,1,0:T(8,128)(2,1)}, bf16[8,128,128]{2,1,0:T(8,128)(2,1)}, bf16[8,128,128]{2,1,0:T(8,128)(2,1)}) custom-call(s32[128]{0:T(128)S(4)} %shard_map.29.lists, s32[8]{0:T(128)S(4)} %shard_map.33._, bf16[24,128,128]{2,1,0:T(8,128)(2,1)S(1)} %copy-done.3, ...), custom_call_target="tpu_custom_call" | custom-call | bytes 2097152 | tf_op jit(solution)/shard_map/pallas_call | solution.py:141
  57.7 2.5 %collective-permute-done.4.refs_3_ = bf16[24,128,128]{2,1,0:T(8,128)(2,1)} collective-permute-done((bf16[24,128,128]{2,1,0:T(8,128)(2,1)S(1)}, bf16[24,128,128]{2,1,0:T(8,128)(2,1)}, u32[]{:S(2)}, u32[]{:S(2)}) %collective-permute-start.4) | collective-permute-done | bytes 786464 | tf_op jit(solution)/shard_map/ppermute | solution.py:364
  60.2 3.1 %collective-permute-start.12 = (bf16[24,128,128]{2,1,0:T(8,128)(2,1)}, bf16[24,128,128]{2,1,0:T(8,128)(2,1)S(1)}, u32[]{:S(2)}, u32[]{:S(2)}) collective-permute-start(bf16[24,128,128]{2,1,0:T(8,128)(2,1)} %collective-permute-done.4.refs_3_), channel_id=1, source_target_pairs={{0,16},{16,0},{1,17},{17,1},{2,18},{18,2},{3,19},{19,3},{4,20},{20... | collective-permute-start | bytes 2359304 | tf_op jit(solution)/shard_map/ppermute | solution.py:378
  64.4 2.4 %collective-permute-start.6 = (bf16[8,128,128]{2,1,0:T(8,128)(2,1)}, bf16[8,128,128]{2,1,0:T(8,128)(2,1)S(1)}, u32[]{:S(2)}, u32[]{:S(2)}) collective-permute-start(bf16[8,128,128]{2,1,0:T(8,128)(2,1)} %get-tuple-element.20), channel_id=1, source_target_pairs={{0,8},{4,12},{8,0},{12,4},{1,9},{5,13},{9,1},{13,5},{2,10},{6,14},... | collective-permute-start | bytes 786440 | tf_op jit(solution)/shard_map/ppermute | solution.py:373
  66.8 1.2 %collective-permute-start.7 = (bf16[8,128,128]{2,1,0:T(8,128)(2,1)}, bf16[8,128,128]{2,1,0:T(8,128)(2,1)S(1)}, u32[]{:S(2)}, u32[]{:S(2)}) collective-permute-start(bf16[8,128,128]{2,1,0:T(8,128)(2,1)} %get-tuple-element.21), channel_id=1, source_target_pairs={{0,12},{4,0},{8,4},{12,8},{1,13},{5,1},{9,5},{13,9},{2,14},{6,2},{... | collective-permute-start | bytes 786440 | tf_op jit(solution)/shard_map/ppermute | solution.py:374
  68.0 3.7 %shard_map.35.refs_8_ = f32[24,4,128,128]{3,2,1,0:T(8,128)S(1)} custom-call(s32[512]{0:T(512)S(4)} %shard_map.32.refs_1_.plan, bf16[4,8,128,128]{3,2,1,0:T(8,128)(2,1)S(1)} %all-to-all-done.2.refs_0_.left, bf16[24,128,128]{2,1,0:T(8,128)(2,1)S(1)} %bitcast.16, bf16[24,128,128]{2,1,0:T(8,128)(2,1)S(1)} %collective-permute-done.3.refs_1_, ...), custom_call_target="tpu_custom_call" | custom-call | flops 402653184 | bytes 16777216 | tf_op jit(solution)/shard_map/pallas_call | solution.py:282
  72.7 6.4 %collective-permute-done.6.left2 = bf16[8,128,128]{2,1,0:T(8,128)(2,1)S(1)} collective-permute-done((bf16[8,128,128]{2,1,0:T(8,128)(2,1)}, bf16[8,128,128]{2,1,0:T(8,128)(2,1)S(1)}, u32[]{:S(2)}, u32[]{:S(2)}) %collective-permute-start.6) | collective-permute-done | bytes 262176 | tf_op jit(solution)/shard_map/ppermute | solution.py:373
  79.1 6.0 %shard_map.36 = (f32[24,8,128,128]{3,2,1,0:T(8,128)S(1)}, f32[8,24,128]{2,1,0:T(8,128)}) custom-call(s32[512]{0:T(512)S(4)} %shard_map.32.refs_1_.plan, bf16[8,128,128]{2,1,0:T(8,128)(2,1)S(1)} %copy-done.4, bf16[8,128,128]{2,1,0:T(8,128)(2,1)S(1)} %collective-permute-done.5.left1, bf16[8,128,128]{2,1,0:T(8,128)(2,1)S(1)} %collective-permute-done.6.left2, ...), custom_call_target="tpu_custom_call" | custom-call | flops 402653184 | bytes 16777216 | tf_op jit(solution)/shard_map/pallas_call | solution.py:293
  85.1 9.0 %all_to_all.20.totals = f32[8,24,128]{2,1,0:T(8,128)S(1)} all-to-all(f32[8,24,128]{2,1,0:T(8,128)} %get-tuple-element.24), channel_id=1, replica_groups=mesh['z'=4,'core'=2,'y'=4,'x'=4] {'z','core'}, dimensions={0} | all-to-all | bytes 196608 | tf_op jit(solution)/shard_map/all_to_all | solution.py:381
  94.1 4.6 %shard_map.37 = bf16[8,24,128,128]{3,2,1,0:T(8,128)(2,1)} custom-call(s32[512]{0:T(512)S(4)} %shard_map.32.refs_1_.plan, f32[24,8,128,128]{3,2,1,0:T(8,128)S(1)} %get-tuple-element.23.merged, f32[8,24,128]{2,1,0:T(8,128)S(1)} %all_to_all.20.totals), custom_call_target="tpu_custom_call" | custom-call | flops 6291456 | bytes 20971520 | tf_op jit(solution)/shard_map/pallas_call | solution.py:328
  (33 shorter events, 8.1 us)
Async XLA Ops:
  0.0 29.9 %collective-permute-start.1 = (bf16[24,128,128]{2,1,0:T(8,128)(2,1)}, bf16[24,128,128]{2,1,0:T(8,128)(2,1)S(1)}, u32[]{:S(2)}, u32[]{:S(2)}) collective-permute-start(bf16[24,128,128]{2,1,0:T(8,128)(2,1)} %bitcast.10), channel_id=1, source_target_pairs={{0,3},{3,0},{1,2},{2,1},{4,7},{7,4},{5,6},{6,5},{8,11},{11,8},{9,1... | collective-permute-start | bytes 2359304 | tf_op jit(solution)/shard_map/ppermute | solution.py:349
  3.3 26.6 %collective-permute-start = (bf16[24,128,128]{2,1,0:T(8,128)(2,1)}, bf16[24,128,128]{2,1,0:T(8,128)(2,1)}, u32[]{:S(2)}, u32[]{:S(2)}) collective-permute-start(bf16[24,128,128]{2,1,0:T(8,128)(2,1)} %bitcast.11), channel_id=1, source_target_pairs={{0,1},{1,0},{2,3},{3,2},{4,5},{5,4},{6,7},{7,6},{8,9},{9,8},{10,11... | collective-permute-start | bytes 2359304 | tf_op jit(solution)/shard_map/ppermute | solution.py:348
  4.7 11.0 %all-to-all-start = ((s32[8,1,128]{2,1,0:T(1,128)}), s32[8,1,128]{2,1,0:T(1,128)S(1)}, u32[]{:S(2)}, u32[]{:S(2)}) async-start(s32[8,1,128]{2,1,0:T(1,128)} %shard_map.28), calls=%async_computation | async-start | bytes 8192 | tf_op jit(solution)/shard_map/all_to_all | solution.py:350
  16.3 12.0 %all-to-all-start.1 = ((s32[16,2,128]{2,1,0:T(2,128)}), s32[16,2,128]{2,1,0:T(2,128)S(1)}, u32[]{:S(2)}, u32[]{:S(2)}) async-start(s32[16,2,128]{2,1,0:T(2,128)} %bitcast.7), calls=%async_computation.1 | async-start | bytes 32768 | tf_op jit(solution)/shard_map/all_to_all | solution.py:353
  21.9 22.3 %collective-permute-start.8 = (bf16[24,128,128]{2,1,0:T(8,128)(2,1)}, bf16[24,128,128]{2,1,0:T(8,128)(2,1)S(1)}, u32[]{:S(2)}, u32[]{:S(2)}) collective-permute-start(bf16[24,128,128]{2,1,0:T(8,128)(2,1)} %bitcast.12), channel_id=1, source_target_pairs={{0,96},{32,0},{64,32},{96,64},{1,97},{33,1},{65,33},{97,65},{2,98}... | collective-permute-start | bytes 2359304 | tf_op jit(solution)/shard_map/ppermute | solution.py:356
  22.8 19.2 %collective-permute-start.3 = (bf16[24,128,128]{2,1,0:T(8,128)(2,1)}, bf16[24,128,128]{2,1,0:T(8,128)(2,1)S(1)}, u32[]{:S(2)}, u32[]{:S(2)}) collective-permute-start(bf16[24,128,128]{2,1,0:T(8,128)(2,1)} %bitcast.13), channel_id=1, source_target_pairs={{0,32},{32,64},{64,96},{96,0},{1,33},{33,65},{65,97},{97,1},{2,34}... | collective-permute-start | bytes 2359304 | tf_op jit(solution)/shard_map/ppermute | solution.py:355
  29.9 1.4 %copy-start.1 = (bf16[1,24,128,128]{3,2,1,0:T(8,128)(2,1)S(1)}, bf16[1,24,128,128]{3,2,1,0:T(8,128)(2,1)}, u32[]{:S(2)}) copy-start(bf16[1,24,128,128]{3,2,1,0:T(8,128)(2,1)} %param.2) | copy-start | bytes 2359300
  29.9 0.9 copy-start.2
  33.5 16.5 %all-to-all-start.2 = ((bf16[4,8,128,128]{3,2,1,0:T(8,128)(2,1)}), bf16[4,8,128,128]{3,2,1,0:T(8,128)(2,1)S(1)}, u32[]{:S(2)}, u32[]{:S(2)}) async-start(bf16[4,8,128,128]{3,2,1,0:T(8,128)(2,1)} %shard_map.31._), calls=%async_computation.2 | async-start | bytes 2097152 | tf_op jit(solution)/shard_map/all_to_all | solution.py:361
  37.1 17.3 %collective-permute-start.2 = (bf16[24,128,128]{2,1,0:T(8,128)(2,1)}, bf16[24,128,128]{2,1,0:T(8,128)(2,1)}, u32[]{:S(2)}, u32[]{:S(2)}) collective-permute-start(bf16[24,128,128]{2,1,0:T(8,128)(2,1)} %copy-done.2), channel_id=1, source_target_pairs={{0,1},{1,0},{2,3},{3,2},{4,5},{5,4},{6,7},{7,6},{8,9},{9,8},{10,11... | collective-permute-start | bytes 2359304 | tf_op jit(solution)/shard_map/ppermute | solution.py:362
  42.0 18.2 %collective-permute-start.4 = (bf16[24,128,128]{2,1,0:T(8,128)(2,1)S(1)}, bf16[24,128,128]{2,1,0:T(8,128)(2,1)}, u32[]{:S(2)}, u32[]{:S(2)}) collective-permute-start(bf16[24,128,128]{2,1,0:T(8,128)(2,1)S(1)} %collective-permute-done.3.refs_1_), channel_id=1, source_target_pairs={{0,32},{32,64},{64,96},{96,0},{1,33},{33,65},{65,97},{97,1},{2,34}... | collective-permute-start | bytes 2359304 | tf_op jit(solution)/shard_map/ppermute | solution.py:364
  42.0 22.4 %collective-permute-start.9 = (bf16[24,128,128]{2,1,0:T(8,128)(2,1)S(1)}, bf16[24,128,128]{2,1,0:T(8,128)(2,1)}, u32[]{:S(2)}, u32[]{:S(2)}) collective-permute-start(bf16[24,128,128]{2,1,0:T(8,128)(2,1)S(1)} %bitcast.15), channel_id=1, source_target_pairs={{0,16},{16,0},{1,17},{17,1},{2,18},{18,2},{3,19},{19,3},{4,20},{20... | collective-permute-start | bytes 2359304 | tf_op jit(solution)/shard_map/ppermute | solution.py:378
  44.2 22.6 %collective-permute-start.11 = (bf16[24,128,128]{2,1,0:T(8,128)(2,1)S(1)}, bf16[24,128,128]{2,1,0:T(8,128)(2,1)}, u32[]{:S(2)}, u32[]{:S(2)}) collective-permute-start(bf16[24,128,128]{2,1,0:T(8,128)(2,1)S(1)} %collective-permute-done.8.refs_2_), channel_id=1, source_target_pairs={{0,16},{16,0},{1,17},{17,1},{2,18},{18,2},{3,19},{19,3},{4,20},{20... | collective-permute-start | bytes 2359304 | tf_op jit(solution)/shard_map/ppermute | solution.py:378
  44.3 1.2 %copy-start = (bf16[4,8,128,128]{3,2,1,0:T(8,128)(2,1)S(1)}, bf16[4,8,128,128]{3,2,1,0:T(8,128)(2,1)}, u32[]{:S(2)}) copy-start(bf16[4,8,128,128]{3,2,1,0:T(8,128)(2,1)} %shard_map.31._) | copy-start | bytes 3145732
  49.4 18.5 %collective-permute-start.10 = (bf16[24,128,128]{2,1,0:T(8,128)(2,1)S(1)}, bf16[24,128,128]{2,1,0:T(8,128)(2,1)}, u32[]{:S(2)}, u32[]{:S(2)}) collective-permute-start(bf16[24,128,128]{2,1,0:T(8,128)(2,1)S(1)} %collective-permute-done.3.refs_1_), channel_id=1, source_target_pairs={{0,16},{16,0},{1,17},{17,1},{2,18},{18,2},{3,19},{19,3},{4,20},{20... | collective-permute-start | bytes 2359304 | tf_op jit(solution)/shard_map/ppermute | solution.py:378
  54.4 1.1 %copy-start.3 = (bf16[24,128,128]{2,1,0:T(8,128)(2,1)S(1)}, bf16[24,128,128]{2,1,0:T(8,128)(2,1)}, u32[]{:S(2)}) copy-start(bf16[24,128,128]{2,1,0:T(8,128)(2,1)} %copy-done.2) | copy-start | bytes 2359300
  60.2 7.8 %collective-permute-start.12 = (bf16[24,128,128]{2,1,0:T(8,128)(2,1)}, bf16[24,128,128]{2,1,0:T(8,128)(2,1)S(1)}, u32[]{:S(2)}, u32[]{:S(2)}) collective-permute-start(bf16[24,128,128]{2,1,0:T(8,128)(2,1)} %collective-permute-done.4.refs_3_), channel_id=1, source_target_pairs={{0,16},{16,0},{1,17},{17,1},{2,18},{18,2},{3,19},{19,3},{4,20},{20... | collective-permute-start | bytes 2359304 | tf_op jit(solution)/shard_map/ppermute | solution.py:378
  63.3 9.4 %collective-permute-start.5 = (bf16[8,128,128]{2,1,0:T(8,128)(2,1)}, bf16[8,128,128]{2,1,0:T(8,128)(2,1)S(1)}, u32[]{:S(2)}, u32[]{:S(2)}) collective-permute-start(bf16[8,128,128]{2,1,0:T(8,128)(2,1)} %get-tuple-element.19), channel_id=1, source_target_pairs={{0,4},{4,8},{8,12},{12,0},{1,5},{5,9},{9,13},{13,1},{2,6},{6,10},{... | collective-permute-start | bytes 786440 | tf_op jit(solution)/shard_map/ppermute | solution.py:372
  64.4 14.7 %collective-permute-start.6 = (bf16[8,128,128]{2,1,0:T(8,128)(2,1)}, bf16[8,128,128]{2,1,0:T(8,128)(2,1)S(1)}, u32[]{:S(2)}, u32[]{:S(2)}) collective-permute-start(bf16[8,128,128]{2,1,0:T(8,128)(2,1)} %get-tuple-element.20), channel_id=1, source_target_pairs={{0,8},{4,12},{8,0},{12,4},{1,9},{5,13},{9,1},{13,5},{2,10},{6,14},... | collective-permute-start | bytes 786440 | tf_op jit(solution)/shard_map/ppermute | solution.py:373
  66.8 12.3 %copy-start.4 = (bf16[8,128,128]{2,1,0:T(8,128)(2,1)S(1)}, bf16[8,128,128]{2,1,0:T(8,128)(2,1)}, u32[]{:S(2)}) copy-start(bf16[8,128,128]{2,1,0:T(8,128)(2,1)} %get-tuple-element.18.left0) | copy-start | bytes 786436
  66.8 12.3 %collective-permute-start.7 = (bf16[8,128,128]{2,1,0:T(8,128)(2,1)}, bf16[8,128,128]{2,1,0:T(8,128)(2,1)S(1)}, u32[]{:S(2)}, u32[]{:S(2)}) collective-permute-start(bf16[8,128,128]{2,1,0:T(8,128)(2,1)} %get-tuple-element.21), channel_id=1, source_target_pairs={{0,12},{4,0},{8,4},{12,8},{1,13},{5,1},{9,5},{13,9},{2,14},{6,2},{... | collective-permute-start | bytes 786440 | tf_op jit(solution)/shard_map/ppermute | solution.py:374

commit v3 on v2

--- a/solution.py
+++ b/solution.py
@@ -18,7 +18,10 @@
 OWN_ROWS = 32
 LIMIT = 12 << 20
 PLAN_COST = 32 << 20
-TOKEN_COST = 16 << 20
+TOKEN_COST = 16
+Y1_COST = 0
+Y2_COST = 20
+DIAG_COST = 20
 LISTS_COST = 0
 SPREAD_COST = 0
 DZ = (0, 3, 1, 2)
@@ -27,6 +30,7 @@
 UP = [(i, (i + 1) % 4) for i in range(4)]
 DOWN = [(i, (i + 3) % 4) for i in range(4)]
 ACROSS = [(i, (i + 2) % 4) for i in range(4)]
+FAR = [(2 * z, 2 * ((z + 1) % 4)) for z in range(4)] + [(2 * z + 1, 2 * ((z + 3) % 4) + 1) for z in range(4)]
 SWAP = [(0, 1), (1, 0)]
 
 SMEM = pl.BlockSpec(memory_space=pltpu.SMEM)
@@ -48,8 +52,9 @@
 
 
 def spread_kernel(rows, out):
+    out[...] = jnp.zeros_like(out)
     for i in range(PANELS):
-        out[i] = rows[...]
+        out[i, :, :BLK] = rows[...]
 
 
 def spread(rows):
@@ -74,7 +79,7 @@
         in_specs=[ANY] * len(arrays),
         out_specs=SMEM,
         compiler_params=pltpu.CompilerParams(vmem_limit_bytes=1 << 20),
-        cost_estimate=pl.CostEstimate(flops=cost * 1000, bytes_accessed=cost, transcendentals=0),
+        cost_estimate=pl.CostEstimate(flops=cost * 10**9, bytes_accessed=0, transcendentals=0),
     )(*arrays)
 
 
@@ -96,18 +101,8 @@
         lists[AT + n] = pos[n]
 
 
-def make_lists(pos, req):
-    return pl.pallas_call(
-        lists_kernel,
-        out_shape=pltpu.SMEM((128,), jnp.int32),
-        in_specs=[SMEM, SMEM],
-        out_specs=SMEM,
-        compiler_params=pltpu.CompilerParams(vmem_limit_bytes=1 << 20),
-        cost_estimate=pl.CostEstimate(flops=0, bytes_accessed=LISTS_COST, transcendentals=0),
-    )(pos, req)
-
-
-def select_own_kernel(lists, _, own, inner, out):
+def select_own_kernel(pos, req, own, inner, _, out, lists):
+    lists_kernel(pos, req, lists)
     pair = lists[AT] // 2
     side = lists[AT] % 2
     for dest in range(4):
@@ -122,7 +117,7 @@
         pl.when(upper != side)(lambda: copy(inner))
 
 
-def select_other_kernel(lists, _, outer, diag, *outs):
+def select_other_kernel(lists, outer, diag, _, __, ___, *outs):
     pair = 1 - lists[AT] // 2
     side = (3 - lists[AT]) % 2
     for away in range(4):
@@ -137,15 +132,26 @@
         pl.when(upper != side)(lambda: copy(diag))
 
 
-def select(kernel, out_shape, lists, after, *blocks):
+def select_own(pos, req, own, inner, after):
+    return pl.pallas_call(
+        select_own_kernel,
+        out_shape=(pltpu.HBM((4, USED, TILE, TILE), jnp.bfloat16), pltpu.SMEM((128,), jnp.int32)),
+        in_specs=[SMEM, SMEM, VMEM, VMEM, ANY],
+        out_specs=(VMEM, SMEM),
+        compiler_params=pltpu.CompilerParams(vmem_limit_bytes=8 << 20),
+        cost_estimate=pl.CostEstimate(flops=0, bytes_accessed=2 << 20, transcendentals=0),
+    )(pos, req, own, inner, after)
+
+
+def select(kernel, out_shape, lists, blocks, after):
     return pl.pallas_call(
         kernel,
         out_shape=out_shape,
-        in_specs=[SMEM, ANY] + [VMEM] * len(blocks),
+        in_specs=[SMEM] + [VMEM] * len(blocks) + [ANY] * len(after),
         out_specs=jax.tree.map(lambda _: VMEM, out_shape),
         compiler_params=pltpu.CompilerParams(vmem_limit_bytes=8 << 20),
         cost_estimate=pl.CostEstimate(flops=0, bytes_accessed=2 << 20, transcendentals=0),
-    )(lists, after, *blocks)
+    )(lists, *blocks, *after)
 
 
 def panel_of(pos, at, j):
@@ -198,26 +204,25 @@
     )(pos, rows, req, after)
 
 
-def products(plan, left, rights, first, n, put):
+def products(plan, left, rights, places, n, put):
     for u in range(GROUP):
         t = n * GROUP + u
-        for d in range(4):
-            j = first + d
+        for j in places:
             z, _ = panel_of(plan, END, j)
-            put(t, j, jnp.dot(left[z, plan[j * BLK + t]], rights[d][t], preferred_element_type=jnp.float32))
-
-
-def run_both(plan, first, mine, theirs, work):
+            product = jnp.dot(left[z, plan[j * BLK + t]], rights[j % 4][t], preferred_element_type=jnp.float32)
+            put(t, j, product)
+
+
+def run_both(plan, mine, theirs, work):
     same = plan[END] // 2 == plan[END + 3]
-    here, there = (mine, theirs) if first == 0 else (theirs, mine)
-    pl.when(same)(lambda: work(here))
-    pl.when(jnp.logical_not(same))(lambda: work(there))
+    pl.when(same)(lambda: work(mine, theirs))
+    pl.when(jnp.logical_not(same))(lambda: work(theirs, mine))
 
 
 def own_kernel(plan, left, *refs):
-    mine, theirs, (early,) = refs[:4], refs[4:8], refs[8:]
-
-    def work(rights):
+    mine, theirs, early = refs[:3], refs[3:6], refs[7]
+
+    def work(rights, _):
         def step(n, carry):
             def put(t, j, product):
                 if j == 0:
@@ -226,16 +231,16 @@
                     r = plan[MERGE + j * BLK + t]
                     early[t, r] = jnp.where(r == j, 0.0, early[t, r]) + product
 
-            products(plan, left, rights, 0, n, put)
+            products(plan, left, rights, range(3), n, put)
             return carry
 
         lax.fori_loop(0, BLK // GROUP, step, 0)
 
-    run_both(plan, 0, mine, theirs, work)
-
-
-def other_kernel(plan, left0, left1, left2, left3, *refs):
-    mine, theirs, (early, merged, totals, left, sums) = refs[:4], refs[4:8], refs[8:]
+    run_both(plan, mine, theirs, work)
+
+
+def other_kernel(plan, own_left, left0, left1, left2, left3, *refs):
+    mine, theirs, (early, _, merged, totals, left, sums) = refs[:4], refs[4:8], refs[8:]
     for away, piece in enumerate((left0, left1, left2, left3)):
         left[(plan[END + 1] - away) % 4] = piece[...]
 
@@ -249,28 +254,29 @@
                 total = total + jnp.where(plan[MERGE + j * BLK + t] == j, part, 0.0)
             sums[pl.ds(t, 1), :] = jnp.sum(total, axis=0, keepdims=True)
 
-    def work(rights):
+    def work(own_rights, rights):
         def step(n, carry):
             def put(t, j, product):
                 r = plan[MERGE + j * BLK + t]
                 merged[t, r] = jnp.where(r == j, 0.0, merged[t, r]) + product
 
             for u in range(GROUP):
-                for j in range(4):
+                for j in range(3):
                     merged[n * GROUP + u, j] = early[n * GROUP + u, j]
-            products(plan, left, rights, 4, n, put)
+            products(plan, own_left, own_rights, (3,), n, put)
+            products(plan, left, rights, range(4, PANELS), n, put)
             add_up(jnp.maximum(n - 1, 0))
             return carry
 
         lax.fori_loop(0, BLK // GROUP, step, 0)
 
-    run_both(plan, 4, mine, theirs, work)
+    run_both(plan, mine, theirs, work)
     add_up(BLK // GROUP - 1)
     for i in range(PANELS):
         totals[i] = sums[...]
 
 
-EARLY = (BLK, 4, TILE, TILE)
+EARLY = (BLK, 3, TILE, TILE)
 MERGED = (BLK, PANELS, TILE, TILE)
 
 
@@ -278,61 +284,62 @@
     return tuple(pltpu.with_memory_space_constraint(a, pltpu.VMEM) for a in arrays)
 
 
-def multiply_own(plan, left, mine, theirs):
+def multiply_own(plan, left, mine, theirs, after):
     return pl.pallas_call(
         own_kernel,
         out_shape=pltpu.VMEM(EARLY, jnp.float32),
-        in_specs=[SMEM] + [VMEM] * 9,
+        in_specs=[SMEM] + [VMEM] * 7 + [ANY],
         out_specs=VMEM,
         compiler_params=pltpu.CompilerParams(vmem_limit_bytes=LIMIT),
         cost_estimate=pl.CostEstimate(flops=2 * 96 * TILE**3, bytes_accessed=16 << 20, transcendentals=0),
-    )(plan, *in_vmem(left, *mine, *theirs))
-
-
-def multiply_other(plan, left, mine, theirs, early):
+    )(plan, *in_vmem(left, *mine, *theirs), after)
+
+
+def multiply_other(plan, own_left, left, mine, theirs, early):
     return pl.pallas_call(
         other_kernel,
         out_shape=(pltpu.VMEM(MERGED, jnp.float32), pltpu.HBM((PANELS, BLK, TILE), jnp.float32)),
-        in_specs=[SMEM] + [VMEM] * 13,
+        in_specs=[SMEM] + [VMEM] * 14 + [ANY],
         out_specs=(VMEM, VMEM),
         scratch_shapes=[pltpu.VMEM((4, USED, TILE, TILE), jnp.bfloat16), pltpu.VMEM((BLK, TILE), jnp.float32)],
         compiler_params=pltpu.CompilerParams(vmem_limit_bytes=LIMIT),
         cost_estimate=pl.CostEstimate(flops=2 * 96 * TILE**3, bytes_accessed=16 << 20, transcendentals=0),
-    )(plan, *in_vmem(*left, *mine, *theirs, early))
+    )(plan, *in_vmem(own_left, *left, *mine, *theirs, early), token(Y2_COST, *left[1:]))
 
 
 def scale_kernel(plan, merged, totals, out, factor):
-    j = pl.program_id(0)
-
-    @pl.when(j == 0)
+    d = pl.program_id(0)
+    pair = plan[END] // 2
+
+    @pl.when(d == 0)
     def _():
         factor[...] = float(PANELS * PANELS * TILE) / (jnp.sum(totals[...], axis=0) + 1e-6)
 
     def step(n, carry):
         for u in range(GROUP):
             t = n * GROUP + u
-            tile = merged[t, plan[MERGE + j * BLK + t]]
-            out[0, t] = (tile * tile * factor[pl.ds(t, 1), :]).astype(jnp.bfloat16)
+            scaling = factor[pl.ds(t, 1), :]
+            for half in range(2):
+                tile = merged[t, plan[MERGE + (half * 4 + d) * BLK + t]]
+                out[pair if half == 0 else 1 - pair, t] = (tile * tile * scaling).astype(jnp.bfloat16)
         return carry
 
     lax.fori_loop(0, BLK // GROUP, step, 0)
 
 
 def scale(plan, merged, totals):
-    def place(j, plan):
-        d = j % 4
-        z = (plan[END + 2] + jnp.where(d == 1, 3, jnp.where(d == 2, 1, jnp.where(d == 3, 2, 0)))) % 4
-        pair = plan[END] // 2
-        return 2 * z + jnp.where(j < 4, pair, 1 - pair), 0, 0, 0
+    def place(d, plan):
+        away = jnp.where(d == 1, 3, jnp.where(d == 2, 1, jnp.where(d == 3, 2, 0)))
+        return (plan[END + 2] + away) % 4, 0, 0, 0
 
     return pl.pallas_call(
         scale_kernel,
         out_shape=jax.ShapeDtypeStruct((PANELS, BLK, TILE, TILE), jnp.bfloat16),
         grid_spec=pltpu.PrefetchScalarGridSpec(
             num_scalar_prefetch=1,
-            grid=(PANELS,),
+            grid=(4,),
             in_specs=[VMEM, VMEM],
-            out_specs=pl.BlockSpec((1, BLK, TILE, TILE), place),
+            out_specs=pl.BlockSpec((2, BLK, TILE, TILE), place),
             scratch_shapes=[pltpu.VMEM((BLK, TILE), jnp.float32)],
         ),
         compiler_params=pltpu.CompilerParams(vmem_limit_bytes=LIMIT),
@@ -343,11 +350,9 @@
 def on_device(tile_values, tile_rows):
     own = tile_values[0]
     pos = jnp.stack([lax.axis_index(a) for a in ("x", "y", "z", "core")]).astype(jnp.int32)
-    wide_rows = jnp.pad(tile_rows, ((0, 0), (0, TILE - BLK)))
-
     inner = lax.ppermute(own, "x", INNER)
     outer = lax.ppermute(own, "x", OUTER)
-    rows = lax.all_to_all(spread(wide_rows), ("z", "core"), 0, 0)
+    rows = lax.all_to_all(spread(tile_rows), ("z", "core"), 0, 0)
     own_rows = jnp.pad(tile_rows, ((0, 0), (OWN_ROWS, TILE - OWN_ROWS - BLK)))
     asks = jnp.broadcast_to(rows.reshape(4, 1, 2, TILE) + own_rows, (4, 4, 2, TILE)).reshape(COLS, 2, TILE)
     req = lax.all_to_all(asks, ("y", "x"), 0, 0)
@@ -355,29 +360,29 @@
     below = lax.ppermute(own_z, "z", UP)
     above = lax.ppermute(own_z, "z", DOWN)
 
-    lists = make_lists(pos, req)
     arrived = token(TOKEN_COST, inner, outer)
-    send1 = select(select_own_kernel, pltpu.HBM((4, USED, TILE, TILE), jnp.bfloat16), lists, arrived, own, inner)
+    send1, lists = select_own(pos, req, own, inner, arrived)
     left1 = lax.all_to_all(send1, "y", 0, 0)
     diag = lax.ppermute(outer, "x", INNER)
 
-    far = lax.ppermute(below, "z", UP)
+    far = lax.ppermute(jnp.where(lax.axis_index("core") == 0, below, above), ("z", "core"), FAR)
     plan = make_plan(pos, rows_z, req, send1)
     sent = pltpu.HBM((USED, TILE, TILE), jnp.bfloat16)
-    ready = token(0, left1, plan)
-    send2 = select(select_other_kernel, (sent,) * 4, lists, ready, outer, diag)
-    kept, far_later = lax.optimization_barrier((send2[0], far))
+    after = (token(Y1_COST, left1), token(DIAG_COST, diag), plan)
+    send2 = select(select_other_kernel, (sent,) * 4, lists, (outer, diag), after)
     left2 = (
-        kept,
+        send2[0],
         lax.ppermute(send2[1], "y", UP),
         lax.ppermute(send2[2], "y", ACROSS),
         lax.ppermute(send2[3], "y", DOWN),
     )
 
-    mine = (own, below, above, far)
-    theirs = tuple(lax.ppermute(block, "core", SWAP) for block in (own, below, above, far_later))
-    early = multiply_own(plan, left1, mine, theirs)
-    merged, totals = multiply_other(plan, left2, mine, theirs, early)
+    mine = (own, below, above)
+    theirs = tuple(lax.ppermute(block, "core", SWAP) for block in mine)
+    early = multiply_own(plan, left1, mine, theirs, send2[0])
+    early, far = lax.optimization_barrier((early, far))
+    mine, theirs = (*mine, far), (*theirs, lax.ppermute(far, "core", SWAP))
+    merged, totals = multiply_other(plan, left1, left2, mine, theirs, early)
     totals = lax.all_to_all(totals, ("z", "core"), 0, 0)
     return scale(plan, merged, totals)[None]
 

time: 99.3 us -> 86 us (0.87)
  waiting for transfers between devices: 28.3 us -> 14.2 us
  blocking collectives: 9.01 us -> 11.5 us
  Pallas kernels: 24.9 us -> 22.7 us
  local copies, waits for them, and re-layouts: 5.15 us -> 3.55 us
  starting transfers between devices: 31.2 us -> 32.3 us
  other arithmetic: 0.08 us -> 1.08 us
    ppermute x1, waiting for transfers between devices: 6.42 us -> 0.01 us  [on_device(): lax.ppermute(send2[2], 'y', ACROSS)]
    ppermute x1, waiting for transfers between devices: 4.61 us -> 0.01 us  [on_device(): below = lax.ppermute(own_z, 'z', UP)]
    ppermute x1, waiting for transfers between devices: 4.34 us -> 0.01 us  [on_device(): diag = lax.ppermute(outer, 'x', INNER)]
    ppermute x5, starting transfers between devices: 5.87 us -> 8.98 us  [the longest x1 4.55 us: on_device(): mine, theirs = ((*mine, far), (*theirs, lax.ppermute(far, 'core', SWAP)))]
    all_to_all x1, waiting for transfers between devices: 0.09 us -> 2.66 us  [on_device(): left1 = lax.all_to_all(send1, 'y', 0, 0)]
    all_to_all x1, blocking collectives: 9.01 us -> 11.5 us  [on_device(): totals = lax.all_to_all(totals, ('z', 'core'), 0, 0)]
    ppermute x5, waiting for transfers between devices: 2.48 us -> 0.87 us  [the longest x1 0.86 us: on_device(): mine, theirs = ((*mine, far), (*theirs, lax.ppermute(far, 'core', SWAP)))]
    ppermute x1, waiting for transfers between devices: 0.01 us -> 1.26 us  [on_device(): lax.ppermute(send2[3], 'y', DOWN)]
  transfers between devices with their start and end apart: 16 -> 16, of which waited for: 8 -> 5; matrix products, arithmetic and copies ran while one was open for 2% -> 2% of each run, Pallas kernels for 14% -> 15%
where the time goes in v3:
time: 86 us; the launch traced here: 85.5 us
  starting transfers between devices  32.3 us (38%)
  Pallas kernels  22.7 us (26%)
  waiting for transfers between devices  14.2 us (17%)
  blocking collectives  11.5 us (13%)
  local copies, waits for them, and re-layouts  3.55 us (4%)
  other arithmetic  1.08 us (1%)
    all_to_all x1, blocking collectives, on_device(): totals = lax.all_to_all(totals, ('z', 'core'), 0, 0)  11.5 us
    pallas_call x1, Pallas kernels, multiply_other(): pl.pallas_call(other_kernel, out_shape=(pltpu.VMEM(MERGED, jnp.float32),...  6.24 us
    all_to_all x1, starting transfers between devices, on_device(): req = lax.all_to_all(asks, ('y', 'x'), 0, 0)  5.44 us
    all_to_all x1, starting transfers between devices, on_device(): rows = lax.all_to_all(spread(tile_rows), ('z', 'core'), 0, 0)  5.42 us
    all_to_all x1, waiting for transfers between devices, on_device(): req = lax.all_to_all(asks, ('y', 'x'), 0, 0)  4.97 us
    ppermute x1, starting transfers between devices, on_device(): mine, theirs = ((*mine, far), (*theirs, lax.ppermute(far, 'core', SWAP)))  4.55 us
    all_to_all x1, waiting for transfers between devices, on_device(): rows = lax.all_to_all(spread(tile_rows), ('z', 'core'), 0, 0)  4.44 us
    pallas_call x1, Pallas kernels, make_plan(): pl.pallas_call(plan_kernel, out_shape=pltpu.SMEM((512,), jnp.int32), in_s...  3.89 us
  transfers between devices with their start and end apart: 16, of which 5 were waited for; matrix products, arithmetic and copies ran while one was open for 2% of the time, Pallas kernels for 15%

profile of v3, /device:TPU:1, one launch (start us, length us, event | category | flops | bytes accessed | tf_op | source)
XLA Modules:
  0.0 85.5 jit_solution(1159450158635702898)
XLA Ops:
  0.0 3.3 %collective-permute-start.1 = (bf16[24,128,128]{2,1,0:T(8,128)(2,1)}, bf16[24,128,128]{2,1,0:T(8,128)(2,1)}, u32[]{:S(2)}, u32[]{:S(2)}) collective-permute-start(bf16[24,128,128]{2,1,0:T(8,128)(2,1)} %bitcast.10), channel_id=1, source_target_pairs={{0,3},{3,0},{1,2},{2,1},{4,7},{7,4},{5,6},{6,5},{8,11},{11,8},{9,1... | collective-permute-start | bytes 2359304 | tf_op jit(solution)/shard_map/ppermute | solution.py:354
  3.3 1.2 %collective-permute-start.8 = (bf16[24,128,128]{2,1,0:T(8,128)(2,1)}, bf16[24,128,128]{2,1,0:T(8,128)(2,1)}, u32[]{:S(2)}, u32[]{:S(2)}) collective-permute-start(bf16[24,128,128]{2,1,0:T(8,128)(2,1)} %bitcast.12), channel_id=1, source_target_pairs={{0,16},{16,0},{1,17},{17,1},{2,18},{18,2},{3,19},{19,3},{4,20},{20... | collective-permute-start | bytes 2359304 | tf_op jit(solution)/shard_map/ppermute | solution.py:381
  5.7 5.4 %all-to-all-start = ((s32[8,1,128]{2,1,0:T(1,128)}), s32[8,1,128]{2,1,0:T(1,128)S(1)}, u32[]{:S(2)}, u32[]{:S(2)}) async-start(s32[8,1,128]{2,1,0:T(1,128)} %shard_map.28), calls=%async_computation | async-start | bytes 8192 | tf_op jit(solution)/shard_map/all_to_all | solution.py:355
  11.3 4.4 %all-to-all-done.rows = s32[8,1,128]{2,1,0:T(1,128)S(1)} async-done(((s32[8,1,128]{2,1,0:T(1,128)}), s32[8,1,128]{2,1,0:T(1,128)S(1)}, u32[]{:S(2)}, u32[]{:S(2)}) %all-to-all-start) | async-done | bytes 4128 | tf_op jit(solution)/shard_map/all_to_all | solution.py:355
  17.8 5.4 %all-to-all-start.1 = ((s32[16,2,128]{2,1,0:T(2,128)}), s32[16,2,128]{2,1,0:T(2,128)S(1)}, u32[]{:S(2)}, u32[]{:S(2)}) async-start(s32[16,2,128]{2,1,0:T(2,128)} %bitcast.7), calls=%async_computation.1 | async-start | bytes 32768 | tf_op jit(solution)/shard_map/all_to_all | solution.py:358
  23.3 1.4 %collective-permute-start.2 = (bf16[24,128,128]{2,1,0:T(8,128)(2,1)}, bf16[24,128,128]{2,1,0:T(8,128)(2,1)}, u32[]{:S(2)}, u32[]{:S(2)}) collective-permute-start(bf16[24,128,128]{2,1,0:T(8,128)(2,1)} %collective-permute-done.1.refs_1_.outer), channel_id=1, source_target_pairs={{0,1},{1,0},{2,3},{3,2},{4,5},{5,4},{6,7},{7,6},{8,9},{9,8},{10,11... | collective-permute-start | bytes 2359304 | tf_op jit(solution)/shard_map/ppermute | solution.py:366
  24.8 5.0 %all-to-all-done.1.req = s32[16,2,128]{2,1,0:T(2,128)S(1)} async-done(((s32[16,2,128]{2,1,0:T(2,128)}), s32[16,2,128]{2,1,0:T(2,128)S(1)}, u32[]{:S(2)}, u32[]{:S(2)}) %all-to-all-start.1) | async-done | bytes 16416 | tf_op jit(solution)/shard_map/all_to_all | solution.py:358
  29.7 2.7 %shard_map.30 = (bf16[4,8,128,128]{3,2,1,0:T(8,128)(2,1)}, s32[128]{0:T(128)S(4)}) custom-call(s32[4]{0:T(128)S(1)} %pad_add_fusion.pos, s32[16,2,128]{2,1,0:T(2,128)S(1)} %all-to-all-done.1.req, bf16[24,128,128]{2,1,0:T(8,128)(2,1)S(1)} %bitcast.15, bf16[24,128,128]{2,1,0:T(8,128)(2,1)S(1)} %collective-permute-done.refs_0_.inner, s32[8]{0:T(128)S(4)} %shard_map.29._), custom_call_target="tpu_custom_call" | custom-call | bytes 2097152 | tf_op jit(solution)/shard_map/pallas_call | solution.py:136
  32.5 3.5 %all-to-all-start.2 = ((bf16[4,8,128,128]{3,2,1,0:T(8,128)(2,1)}), bf16[4,8,128,128]{3,2,1,0:T(8,128)(2,1)S(1)}, u32[]{:S(2)}, u32[]{:S(2)}) async-start(bf16[4,8,128,128]{3,2,1,0:T(8,128)(2,1)} %get-tuple-element.18._), calls=%async_computation.2 | async-start | bytes 2097152 | tf_op jit(solution)/shard_map/all_to_all | solution.py:365
  36.0 1.2 %copy-done.1 = bf16[4,8,128,128]{3,2,1,0:T(8,128)(2,1)S(1)} copy-done((bf16[4,8,128,128]{3,2,1,0:T(8,128)(2,1)S(1)}, bf16[4,8,128,128]{3,2,1,0:T(8,128)(2,1)}, u32[]{:S(2)}) %copy-start.1) | copy-done | bytes 1048600
  37.2 3.9 %shard_map.31.___.plan = s32[512]{0:T(512)S(4)} custom-call(s32[4]{0:T(128)S(1)} %pad_add_fusion.pos, s32[8,1,128]{2,1,0:T(1,128)S(1)} %all-to-all-done.rows, s32[16,2,128]{2,1,0:T(2,128)S(1)} %all-to-all-done.1.req, bf16[4,8,128,128]{3,2,1,0:T(8,128)(2,1)S(1)} %copy-done.1), custom_call_target="tpu_custom_call" | custom-call | bytes 33554432 | tf_op jit(solution)/shard_map/pallas_call | solution.py:196
  41.2 1.0 %broadcast_select_fusion = bf16[24,128,128]{2,1,0:T(8,128)(2,1)} fusion(bf16[24,128,128]{2,1,0:T(8,128)(2,1)S(1)} %collective-permute-done.6.refs_1_, bf16[24,128,128]{2,1,0:T(8,128)(2,1)S(1)} %collective-permute-done.7.refs_2_, pred[]{:T(512)S(6)} %eq.3), kind=kLoop, calls=%fused_computation | loop fusion | flops 393216 | bytes 2359297 | tf_op jit(solution)/shard_map/jit(_where)/select_n | solution.py:368
  42.2 2.1 %collective-permute-start.11 = (bf16[24,128,128]{2,1,0:T(8,128)(2,1)}, bf16[24,128,128]{2,1,0:T(8,128)(2,1)}, u32[]{:S(2)}, u32[]{:S(2)}) collective-permute-start(bf16[24,128,128]{2,1,0:T(8,128)(2,1)} %broadcast_select_fusion), channel_id=1, source_target_pairs={{0,32},{32,64},{64,96},{96,0},{16,112},{48,16},{80,48},{112,80},{1... | collective-permute-start | bytes 2359304 | tf_op jit(solution)/shard_map/ppermute | solution.py:368
  44.3 1.2 %collective-permute-start.10 = (bf16[24,128,128]{2,1,0:T(8,128)(2,1)S(1)}, bf16[24,128,128]{2,1,0:T(8,128)(2,1)}, u32[]{:S(2)}, u32[]{:S(2)}) collective-permute-start(bf16[24,128,128]{2,1,0:T(8,128)(2,1)S(1)} %collective-permute-done.7.refs_2_), channel_id=1, source_target_pairs={{0,16},{16,0},{1,17},{17,1},{2,18},{18,2},{3,19},{19,3},{4,20},{20... | collective-permute-start | bytes 2359304 | tf_op jit(solution)/shard_map/ppermute | solution.py:381
  45.4 2.7 %all-to-all-done.2.refs_0_.left.own_left = bf16[4,8,128,128]{3,2,1,0:T(8,128)(2,1)S(1)} async-done(((bf16[4,8,128,128]{3,2,1,0:T(8,128)(2,1)}), bf16[4,8,128,128]{3,2,1,0:T(8,128)(2,1)S(1)}, u32[]{:S(2)}, u32[]{:S(2)}) %all-to-all-start.2) | async-done | bytes 1048608 | tf_op jit(solution)/shard_map/all_to_all | solution.py:365
  48.1 2.5 %shard_map.34 = (bf16[8,128,128]{2,1,0:T(8,128)(2,1)}, bf16[8,128,128]{2,1,0:T(8,128)(2,1)}, bf16[8,128,128]{2,1,0:T(8,128)(2,1)}, bf16[8,128,128]{2,1,0:T(8,128)(2,1)}) custom-call(s32[128]{0:T(128)S(4)} %get-tuple-element.19.lists, bf16[24,128,128]{2,1,0:T(8,128)(2,1)} %collective-permute-done.1.refs_1_.outer, ...), custom_call_target="tpu_custom_call" | custom-call | bytes 2097152 | tf_op jit(solution)/shard_map/pallas_call | solution.py:147
  50.9 1.8 %collective-permute-start.4 = (bf16[8,128,128]{2,1,0:T(8,128)(2,1)}, bf16[8,128,128]{2,1,0:T(8,128)(2,1)S(1)}, u32[]{:S(2)}, u32[]{:S(2)}) collective-permute-start(bf16[8,128,128]{2,1,0:T(8,128)(2,1)} %get-tuple-element.22), channel_id=1, source_target_pairs={{0,8},{4,12},{8,0},{12,4},{1,9},{5,13},{9,1},{13,5},{2,10},{6,14},... | collective-permute-start | bytes 786440 | tf_op jit(solution)/shard_map/ppermute | solution.py:376
  53.3 0.9 %copy-done.2 = bf16[8,128,128]{2,1,0:T(8,128)(2,1)S(1)} copy-done((bf16[8,128,128]{2,1,0:T(8,128)(2,1)S(1)}, bf16[8,128,128]{2,1,0:T(8,128)(2,1)}, u32[]{:S(2)}) %copy-start.2) | copy-done | bytes 262168
  54.3 3.2 %shard_map.35.refs_8_ = f32[24,3,128,128]{3,2,1,0:T(8,128)S(1)} custom-call(s32[512]{0:T(512)S(4)} %shard_map.31.___.plan, bf16[4,8,128,128]{3,2,1,0:T(8,128)(2,1)S(1)} %all-to-all-done.2.refs_0_.left.own_left, bf16[24,128,128]{2,1,0:T(8,128)(2,1)S(1)} %bitcast.16, bf16[24,128,128]{2,1,0:T(8,128)(2,1)S(1)} %collective-permute-done.6.refs_1_, ...), custom_call_target="tpu_custom_call" | custom-call | flops 402653184 | bytes 16777216 | tf_op jit(solution)/shard_map/pallas_call | solution.py:288
  57.5 4.5 %collective-permute-start.12 = (bf16[24,128,128]{2,1,0:T(8,128)(2,1)}, bf16[24,128,128]{2,1,0:T(8,128)(2,1)S(1)}, u32[]{:S(2)}, u32[]{:S(2)}) collective-permute-start(bf16[24,128,128]{2,1,0:T(8,128)(2,1)} %collective-permute-done.11.refs_3_), channel_id=1, source_target_pairs={{0,16},{16,0},{1,17},{17,1},{2,18},{18,2},{3,19},{19,3},{4,20},{20... | collective-permute-start | bytes 2359304 | tf_op jit(solution)/shard_map/ppermute | solution.py:384
  62.1 1.3 %collective-permute-done.5.refs_2_.left3 = bf16[8,128,128]{2,1,0:T(8,128)(2,1)S(1)} collective-permute-done((bf16[8,128,128]{2,1,0:T(8,128)(2,1)}, bf16[8,128,128]{2,1,0:T(8,128)(2,1)S(1)}, u32[]{:S(2)}, u32[]{:S(2)}) %collective-permute-start.5) | collective-permute-done | bytes 262176 | tf_op jit(solution)/shard_map/ppermute | solution.py:377
  64.2 6.2 %shard_map.37 = (f32[24,8,128,128]{3,2,1,0:T(8,128)S(1)}, f32[8,24,128]{2,1,0:T(8,128)}) custom-call(s32[512]{0:T(512)S(4)} %shard_map.31.___.plan, bf16[4,8,128,128]{3,2,1,0:T(8,128)(2,1)S(1)} %all-to-all-done.2.refs_0_.left.own_left, bf16[8,128,128]{2,1,0:T(8,128)(2,1)S(1)} %copy-done.3, bf16[8,128,128]{2,1,0:T(8,128)(2,1)S(1)} %collective-permute-done.3.refs_0_.left1, ...), custom_call_target="tpu_custom_call" | custom-call | flops 402653184 | bytes 16777216 | tf_op jit(solution)/shard_map/pallas_call | solution.py:299
  70.5 11.5 %all_to_all.20.totals = f32[8,24,128]{2,1,0:T(8,128)S(1)} all-to-all(f32[8,24,128]{2,1,0:T(8,128)} %get-tuple-element.28), channel_id=1, replica_groups=mesh['z'=4,'core'=2,'y'=4,'x'=4] {'z','core'}, dimensions={0} | all-to-all | bytes 196608 | tf_op jit(solution)/shard_map/all_to_all | solution.py:386
  81.9 3.6 %shard_map.38 = bf16[8,24,128,128]{3,2,1,0:T(8,128)(2,1)} custom-call(s32[512]{0:T(512)S(4)} %shard_map.31.___.plan, f32[24,8,128,128]{3,2,1,0:T(8,128)S(1)} %get-tuple-element.27.merged, f32[8,24,128]{2,1,0:T(8,128)S(1)} %all_to_all.20.totals), custom_call_target="tpu_custom_call" | custom-call | flops 6291456 | bytes 20971520 | tf_op jit(solution)/shard_map/pallas_call | solution.py:335
  (35 shorter events, 5.4 us)
Async XLA Ops:
  0.0 23.3 %collective-permute-start.1 = (bf16[24,128,128]{2,1,0:T(8,128)(2,1)}, bf16[24,128,128]{2,1,0:T(8,128)(2,1)}, u32[]{:S(2)}, u32[]{:S(2)}) collective-permute-start(bf16[24,128,128]{2,1,0:T(8,128)(2,1)} %bitcast.10), channel_id=1, source_target_pairs={{0,3},{3,0},{1,2},{2,1},{4,7},{7,4},{5,6},{6,5},{8,11},{11,8},{9,1... | collective-permute-start | bytes 2359304 | tf_op jit(solution)/shard_map/ppermute | solution.py:354
  3.3 21.4 %collective-permute-start = (bf16[24,128,128]{2,1,0:T(8,128)(2,1)}, bf16[24,128,128]{2,1,0:T(8,128)(2,1)S(1)}, u32[]{:S(2)}, u32[]{:S(2)}) collective-permute-start(bf16[24,128,128]{2,1,0:T(8,128)(2,1)} %bitcast.11), channel_id=1, source_target_pairs={{0,1},{1,0},{2,3},{3,2},{4,5},{5,4},{6,7},{7,6},{8,9},{9,8},{10,11... | collective-permute-start | bytes 2359304 | tf_op jit(solution)/shard_map/ppermute | solution.py:353
  3.3 47.5 %collective-permute-start.8 = (bf16[24,128,128]{2,1,0:T(8,128)(2,1)}, bf16[24,128,128]{2,1,0:T(8,128)(2,1)}, u32[]{:S(2)}, u32[]{:S(2)}) collective-permute-start(bf16[24,128,128]{2,1,0:T(8,128)(2,1)} %bitcast.12), channel_id=1, source_target_pairs={{0,16},{16,0},{1,17},{17,1},{2,18},{18,2},{3,19},{19,3},{4,20},{20... | collective-permute-start | bytes 2359304 | tf_op jit(solution)/shard_map/ppermute | solution.py:381
  4.5 0.7 copy-start.4
  5.7 10.0 %all-to-all-start = ((s32[8,1,128]{2,1,0:T(1,128)}), s32[8,1,128]{2,1,0:T(1,128)S(1)}, u32[]{:S(2)}, u32[]{:S(2)}) async-start(s32[8,1,128]{2,1,0:T(1,128)} %shard_map.28), calls=%async_computation | async-start | bytes 8192 | tf_op jit(solution)/shard_map/all_to_all | solution.py:355
  15.8 25.4 %collective-permute-start.7 = (bf16[24,128,128]{2,1,0:T(8,128)(2,1)}, bf16[24,128,128]{2,1,0:T(8,128)(2,1)S(1)}, u32[]{:S(2)}, u32[]{:S(2)}) collective-permute-start(bf16[24,128,128]{2,1,0:T(8,128)(2,1)} %bitcast.13), channel_id=1, source_target_pairs={{0,96},{32,0},{64,32},{96,64},{1,97},{33,1},{65,33},{97,65},{2,98}... | collective-permute-start | bytes 2359304 | tf_op jit(solution)/shard_map/ppermute | solution.py:361
  16.6 24.6 %collective-permute-start.6 = (bf16[24,128,128]{2,1,0:T(8,128)(2,1)}, bf16[24,128,128]{2,1,0:T(8,128)(2,1)S(1)}, u32[]{:S(2)}, u32[]{:S(2)}) collective-permute-start(bf16[24,128,128]{2,1,0:T(8,128)(2,1)} %bitcast.14), channel_id=1, source_target_pairs={{0,32},{32,64},{64,96},{96,0},{1,33},{33,65},{65,97},{97,1},{2,34}... | collective-permute-start | bytes 2359304 | tf_op jit(solution)/shard_map/ppermute | solution.py:360
  17.8 11.9 %all-to-all-start.1 = ((s32[16,2,128]{2,1,0:T(2,128)}), s32[16,2,128]{2,1,0:T(2,128)S(1)}, u32[]{:S(2)}, u32[]{:S(2)}) async-start(s32[16,2,128]{2,1,0:T(2,128)} %bitcast.7), calls=%async_computation.1 | async-start | bytes 32768 | tf_op jit(solution)/shard_map/all_to_all | solution.py:358
  23.3 6.4 %copy-start = (bf16[1,24,128,128]{3,2,1,0:T(8,128)(2,1)S(1)}, bf16[1,24,128,128]{3,2,1,0:T(8,128)(2,1)}, u32[]{:S(2)}) copy-start(bf16[1,24,128,128]{3,2,1,0:T(8,128)(2,1)} %param.2) | copy-start | bytes 2359300
  23.3 22.1 %collective-permute-start.2 = (bf16[24,128,128]{2,1,0:T(8,128)(2,1)}, bf16[24,128,128]{2,1,0:T(8,128)(2,1)}, u32[]{:S(2)}, u32[]{:S(2)}) collective-permute-start(bf16[24,128,128]{2,1,0:T(8,128)(2,1)} %collective-permute-done.1.refs_1_.outer), channel_id=1, source_target_pairs={{0,1},{1,0},{2,3},{3,2},{4,5},{5,4},{6,7},{7,6},{8,9},{9,8},{10,11... | collective-permute-start | bytes 2359304 | tf_op jit(solution)/shard_map/ppermute | solution.py:366
  32.5 15.6 %all-to-all-start.2 = ((bf16[4,8,128,128]{3,2,1,0:T(8,128)(2,1)}), bf16[4,8,128,128]{3,2,1,0:T(8,128)(2,1)S(1)}, u32[]{:S(2)}, u32[]{:S(2)}) async-start(bf16[4,8,128,128]{3,2,1,0:T(8,128)(2,1)} %get-tuple-element.18._), calls=%async_computation.2 | async-start | bytes 2097152 | tf_op jit(solution)/shard_map/all_to_all | solution.py:365
  36.0 1.3 %copy-start.1 = (bf16[4,8,128,128]{3,2,1,0:T(8,128)(2,1)S(1)}, bf16[4,8,128,128]{3,2,1,0:T(8,128)(2,1)}, u32[]{:S(2)}) copy-start(bf16[4,8,128,128]{3,2,1,0:T(8,128)(2,1)} %get-tuple-element.18._) | copy-start | bytes 3145732
  42.2 15.4 %collective-permute-start.11 = (bf16[24,128,128]{2,1,0:T(8,128)(2,1)}, bf16[24,128,128]{2,1,0:T(8,128)(2,1)}, u32[]{:S(2)}, u32[]{:S(2)}) collective-permute-start(bf16[24,128,128]{2,1,0:T(8,128)(2,1)} %broadcast_select_fusion), channel_id=1, source_target_pairs={{0,32},{32,64},{64,96},{96,0},{16,112},{48,16},{80,48},{112,80},{1... | collective-permute-start | bytes 2359304 | tf_op jit(solution)/shard_map/ppermute | solution.py:368
  44.3 8.4 %collective-permute-start.10 = (bf16[24,128,128]{2,1,0:T(8,128)(2,1)S(1)}, bf16[24,128,128]{2,1,0:T(8,128)(2,1)}, u32[]{:S(2)}, u32[]{:S(2)}) collective-permute-start(bf16[24,128,128]{2,1,0:T(8,128)(2,1)S(1)} %collective-permute-done.7.refs_2_), channel_id=1, source_target_pairs={{0,16},{16,0},{1,17},{17,1},{2,18},{18,2},{3,19},{19,3},{4,20},{20... | collective-permute-start | bytes 2359304 | tf_op jit(solution)/shard_map/ppermute | solution.py:381
  45.4 7.9 %collective-permute-start.9 = (bf16[24,128,128]{2,1,0:T(8,128)(2,1)S(1)}, bf16[24,128,128]{2,1,0:T(8,128)(2,1)}, u32[]{:S(2)}, u32[]{:S(2)}) collective-permute-start(bf16[24,128,128]{2,1,0:T(8,128)(2,1)S(1)} %collective-permute-done.6.refs_1_), channel_id=1, source_target_pairs={{0,16},{16,0},{1,17},{17,1},{2,18},{18,2},{3,19},{19,3},{4,20},{20... | collective-permute-start | bytes 2359304 | tf_op jit(solution)/shard_map/ppermute | solution.py:381
  50.6 11.5 %collective-permute-start.3 = (bf16[8,128,128]{2,1,0:T(8,128)(2,1)}, bf16[8,128,128]{2,1,0:T(8,128)(2,1)S(1)}, u32[]{:S(2)}, u32[]{:S(2)}) collective-permute-start(bf16[8,128,128]{2,1,0:T(8,128)(2,1)} %get-tuple-element.21), channel_id=1, source_target_pairs={{0,4},{4,8},{8,12},{12,0},{1,5},{5,9},{9,13},{13,1},{2,6},{6,10},{... | collective-permute-start | bytes 786440 | tf_op jit(solution)/shard_map/ppermute | solution.py:375
  50.9 11.2 %collective-permute-start.4 = (bf16[8,128,128]{2,1,0:T(8,128)(2,1)}, bf16[8,128,128]{2,1,0:T(8,128)(2,1)S(1)}, u32[]{:S(2)}, u32[]{:S(2)}) collective-permute-start(bf16[8,128,128]{2,1,0:T(8,128)(2,1)} %get-tuple-element.22), channel_id=1, source_target_pairs={{0,8},{4,12},{8,0},{12,4},{1,9},{5,13},{9,1},{13,5},{2,10},{6,14},... | collective-permute-start | bytes 786440 | tf_op jit(solution)/shard_map/ppermute | solution.py:376
  52.6 10.7 %collective-permute-start.5 = (bf16[8,128,128]{2,1,0:T(8,128)(2,1)}, bf16[8,128,128]{2,1,0:T(8,128)(2,1)S(1)}, u32[]{:S(2)}, u32[]{:S(2)}) collective-permute-start(bf16[8,128,128]{2,1,0:T(8,128)(2,1)} %get-tuple-element.23), channel_id=1, source_target_pairs={{0,12},{4,0},{8,4},{12,8},{1,13},{5,1},{9,5},{13,9},{2,14},{6,2},{... | collective-permute-start | bytes 786440 | tf_op jit(solution)/shard_map/ppermute | solution.py:377
  53.3 1.0 %copy-start.2 = (bf16[8,128,128]{2,1,0:T(8,128)(2,1)S(1)}, bf16[8,128,128]{2,1,0:T(8,128)(2,1)}, u32[]{:S(2)}) copy-start(bf16[8,128,128]{2,1,0:T(8,128)(2,1)} %get-tuple-element.20.refs_6_.left0) | copy-start | bytes 786436
  57.5 6.7 %copy-start.3 = (bf16[8,128,128]{2,1,0:T(8,128)(2,1)S(1)}, bf16[8,128,128]{2,1,0:T(8,128)(2,1)}, u32[]{:S(2)}) copy-start(bf16[8,128,128]{2,1,0:T(8,128)(2,1)} %get-tuple-element.20.refs_6_.left0) | copy-start | bytes 786436
  57.5 6.7 %collective-permute-start.12 = (bf16[24,128,128]{2,1,0:T(8,128)(2,1)}, bf16[24,128,128]{2,1,0:T(8,128)(2,1)S(1)}, u32[]{:S(2)}, u32[]{:S(2)}) collective-permute-start(bf16[24,128,128]{2,1,0:T(8,128)(2,1)} %collective-permute-done.11.refs_3_), channel_id=1, source_target_pairs={{0,16},{16,0},{1,17},{17,1},{2,18},{18,2},{3,19},{19,3},{4,20},{20... | collective-permute-start | bytes 2359304 | tf_op jit(solution)/shard_map/ppermute | solution.py:384

commit v4 on v3

--- a/solution.py
+++ b/solution.py
@@ -20,10 +20,10 @@
 PLAN_COST = 32 << 20
 TOKEN_COST = 16
 Y1_COST = 0
+Y1_LATE_COST = 60
 Y2_COST = 20
 DIAG_COST = 20
 LISTS_COST = 0
-SPREAD_COST = 0
 DZ = (0, 3, 1, 2)
 INNER = [(0, 1), (1, 0), (2, 3), (3, 2)]
 OUTER = [(0, 3), (3, 0), (1, 2), (2, 1)]
@@ -49,23 +49,6 @@
         upper, local = split_row(load(t))
         mask = mask | lax.shift_left(jnp.int32(1), local)
     return upper, mask
-
-
-def spread_kernel(rows, out):
-    out[...] = jnp.zeros_like(out)
-    for i in range(PANELS):
-        out[i, :, :BLK] = rows[...]
-
-
-def spread(rows):
-    return pl.pallas_call(
-        spread_kernel,
-        out_shape=jax.ShapeDtypeStruct((PANELS, 1, TILE), jnp.int32),
-        in_specs=[VMEM],
-        out_specs=VMEM,
-        compiler_params=pltpu.CompilerParams(vmem_limit_bytes=1 << 20),
-        cost_estimate=pl.CostEstimate(flops=0, bytes_accessed=SPREAD_COST, transcendentals=0),
-    )(rows)
 
 
 def token_kernel(*refs):
@@ -101,17 +84,18 @@
         lists[AT + n] = pos[n]
 
 
-def select_own_kernel(pos, req, own, inner, _, out, lists):
+def select_own_kernel(pos, req, own, inner, _, *refs):
+    outs, lists = refs[:4], refs[4]
     lists_kernel(pos, req, lists)
     pair = lists[AT] // 2
     side = lists[AT] % 2
-    for dest in range(4):
-        base = (pair * 4 + dest) * 16
+    for away in range(4):
+        base = (pair * 4 + (lists[AT + 1] + away) % 4) * 16
         upper = lists[base + 15]
 
-        def copy(source):
+        def copy(source, out=outs[away], base=base):
             for n in range(USED):
-                out[dest, n] = source[lists[base + n]]
+                out[n] = source[lists[base + n]]
 
         pl.when(upper == side)(lambda: copy(own))
         pl.when(upper != side)(lambda: copy(inner))
@@ -135,9 +119,9 @@
 def select_own(pos, req, own, inner, after):
     return pl.pallas_call(
         select_own_kernel,
-        out_shape=(pltpu.HBM((4, USED, TILE, TILE), jnp.bfloat16), pltpu.SMEM((128,), jnp.int32)),
+        out_shape=(pltpu.HBM((USED, TILE, TILE), jnp.bfloat16),) * 4 + (pltpu.SMEM((128,), jnp.int32),),
         in_specs=[SMEM, SMEM, VMEM, VMEM, ANY],
-        out_specs=(VMEM, SMEM),
+        out_specs=(VMEM,) * 4 + (SMEM,),
         compiler_params=pltpu.CompilerParams(vmem_limit_bytes=8 << 20),
         cost_estimate=pl.CostEstimate(flops=0, bytes_accessed=2 << 20, transcendentals=0),
     )(pos, req, own, inner, after)
@@ -219,8 +203,14 @@
     pl.when(jnp.logical_not(same))(lambda: work(theirs, mine))
 
 
-def own_kernel(plan, left, *refs):
-    mine, theirs, early = refs[:3], refs[3:6], refs[7]
+def gather(plan, pieces, left):
+    for away, piece in enumerate(pieces):
+        left[(plan[END + 1] - away) % 4] = piece[...]
+
+
+def own_kernel(plan, *refs):
+    pieces, mine, theirs, (_, _, early, left) = refs[:4], refs[4:7], refs[7:10], refs[10:]
+    gather(plan, pieces, left)
 
     def work(rights, _):
         def step(n, carry):
@@ -239,10 +229,11 @@
     run_both(plan, mine, theirs, work)
 
 
-def other_kernel(plan, own_left, left0, left1, left2, left3, *refs):
-    mine, theirs, (early, _, merged, totals, left, sums) = refs[:4], refs[4:8], refs[8:]
-    for away, piece in enumerate((left0, left1, left2, left3)):
-        left[(plan[END + 1] - away) % 4] = piece[...]
+def other_kernel(plan, *refs):
+    own_pieces, pieces, mine, theirs = refs[:4], refs[4:8], refs[8:12], refs[12:16]
+    early, _, merged, totals, own_left, left, sums = refs[16:]
+    gather(plan, own_pieces, own_left)
+    gather(plan, pieces, left)
 
     def add_up(n):
         for u in range(GROUP):
@@ -278,6 +269,7 @@
 
 EARLY = (BLK, 3, TILE, TILE)
 MERGED = (BLK, PANELS, TILE, TILE)
+LEFT = pltpu.VMEM((4, USED, TILE, TILE), jnp.bfloat16)
 
 
 def in_vmem(*arrays):
@@ -288,23 +280,24 @@
     return pl.pallas_call(
         own_kernel,
         out_shape=pltpu.VMEM(EARLY, jnp.float32),
-        in_specs=[SMEM] + [VMEM] * 7 + [ANY],
+        in_specs=[SMEM] + [VMEM] * 10 + [ANY] * 2,
         out_specs=VMEM,
+        scratch_shapes=[LEFT],
         compiler_params=pltpu.CompilerParams(vmem_limit_bytes=LIMIT),
         cost_estimate=pl.CostEstimate(flops=2 * 96 * TILE**3, bytes_accessed=16 << 20, transcendentals=0),
-    )(plan, *in_vmem(left, *mine, *theirs), after)
+    )(plan, *in_vmem(*left, *mine, *theirs), *after)
 
 
 def multiply_other(plan, own_left, left, mine, theirs, early):
     return pl.pallas_call(
         other_kernel,
         out_shape=(pltpu.VMEM(MERGED, jnp.float32), pltpu.HBM((PANELS, BLK, TILE), jnp.float32)),
-        in_specs=[SMEM] + [VMEM] * 14 + [ANY],
+        in_specs=[SMEM] + [VMEM] * 17 + [ANY],
         out_specs=(VMEM, VMEM),
-        scratch_shapes=[pltpu.VMEM((4, USED, TILE, TILE), jnp.bfloat16), pltpu.VMEM((BLK, TILE), jnp.float32)],
+        scratch_shapes=[LEFT, LEFT, pltpu.VMEM((BLK, TILE), jnp.float32)],
         compiler_params=pltpu.CompilerParams(vmem_limit_bytes=LIMIT),
         cost_estimate=pl.CostEstimate(flops=2 * 96 * TILE**3, bytes_accessed=16 << 20, transcendentals=0),
-    )(plan, *in_vmem(own_left, *left, *mine, *theirs, early), token(Y2_COST, *left[1:]))
+    )(plan, *in_vmem(*own_left, *left, *mine, *theirs, early), token(Y2_COST, *left[1:]))
 
 
 def scale_kernel(plan, merged, totals, out, factor):
@@ -347,12 +340,17 @@
     )(plan, *in_vmem(merged), totals)
 
 
+def exchange(send):
+    return (send[0],) + tuple(lax.ppermute(part, "y", way) for part, way in zip(send[1:], (UP, ACROSS, DOWN)))
+
+
 def on_device(tile_values, tile_rows):
     own = tile_values[0]
     pos = jnp.stack([lax.axis_index(a) for a in ("x", "y", "z", "core")]).astype(jnp.int32)
     inner = lax.ppermute(own, "x", INNER)
     outer = lax.ppermute(own, "x", OUTER)
-    rows = lax.all_to_all(spread(tile_rows), ("z", "core"), 0, 0)
+    wide_rows = jnp.pad(tile_rows, ((0, 0), (0, TILE - BLK)))
+    rows = lax.all_to_all(jnp.broadcast_to(wide_rows, (PANELS, 1, TILE)), ("z", "core"), 0, 0)
     own_rows = jnp.pad(tile_rows, ((0, 0), (OWN_ROWS, TILE - OWN_ROWS - BLK)))
     asks = jnp.broadcast_to(rows.reshape(4, 1, 2, TILE) + own_rows, (4, 4, 2, TILE)).reshape(COLS, 2, TILE)
     req = lax.all_to_all(asks, ("y", "x"), 0, 0)
@@ -361,26 +359,23 @@
     above = lax.ppermute(own_z, "z", DOWN)
 
     arrived = token(TOKEN_COST, inner, outer)
-    send1, lists = select_own(pos, req, own, inner, arrived)
-    left1 = lax.all_to_all(send1, "y", 0, 0)
+    *send1, lists = select_own(pos, req, own, inner, arrived)
+    left1 = exchange(send1)
     diag = lax.ppermute(outer, "x", INNER)
 
     far = lax.ppermute(jnp.where(lax.axis_index("core") == 0, below, above), ("z", "core"), FAR)
-    plan = make_plan(pos, rows_z, req, send1)
+    plan = make_plan(pos, rows_z, req, diag)
     sent = pltpu.HBM((USED, TILE, TILE), jnp.bfloat16)
-    after = (token(Y1_COST, left1), token(DIAG_COST, diag), plan)
+    after = (token(Y1_COST, left1[1]), token(DIAG_COST, diag), lists)
     send2 = select(select_other_kernel, (sent,) * 4, lists, (outer, diag), after)
-    left2 = (
-        send2[0],
-        lax.ppermute(send2[1], "y", UP),
-        lax.ppermute(send2[2], "y", ACROSS),
-        lax.ppermute(send2[3], "y", DOWN),
-    )
-
+    left2 = exchange(send2)
     mine = (own, below, above)
-    theirs = tuple(lax.ppermute(block, "core", SWAP) for block in mine)
-    early = multiply_own(plan, left1, mine, theirs, send2[0])
-    early, far = lax.optimization_barrier((early, far))
+    kept, *later = lax.optimization_barrier((send2[0], *mine))
+    theirs = tuple(lax.ppermute(block, "core", SWAP) for block in later)
+    left2 = (kept, *left2[1:])
+    early = multiply_own(plan, left1, mine, theirs, (kept, token(Y1_LATE_COST, *left1[2:])))
+    kept2, far = lax.optimization_barrier((kept, far))
+    left2 = (kept2, *left2[1:])
     mine, theirs = (*mine, far), (*theirs, lax.ppermute(far, "core", SWAP))
     merged, totals = multiply_other(plan, left1, left2, mine, theirs, early)
     totals = lax.all_to_all(totals, ("z", "core"), 0, 0)

time: 86 us -> 83 us (0.965)
  starting transfers between devices: 32.3 us -> 38.7 us
  Pallas kernels: 22.7 us -> 19 us
  blocking collectives: 11.5 us -> 9.06 us
  local copies, waits for them, and re-layouts: 3.55 us -> 2.03 us
  other arithmetic: 1.08 us -> 0.16 us
    ppermute x6 -> x9, starting transfers between devices: 5.11 us -> 18.6 us  [the longest x3 9.62 us: on_device(): theirs = tuple((lax.ppermute(block, 'core', SWAP) for block in later))]
    ppermute x1, starting transfers between devices: 4.55 us -> 0.01 us  [on_device(): mine, theirs = ((*mine, far), (*theirs, lax.ppermute(far, 'core', SWAP)))]
    unnamed x10 -> x6, local copies, waits for them, and re-layouts: 2.86 us -> 0.02 us
    ppermute x6 -> x9, waiting for transfers between devices: 1.27 us -> 3.92 us  [the longest x6 2.05 us: exchange(): lax.ppermute(part, 'y', way)]
    all_to_all x2 -> x1, waiting for transfers between devices: 7.11 us -> 4.52 us  [on_device(): lax.all_to_all(jnp.broadcast_to(wide_rows, (PANELS, 1, TILE)), ('z', 'cor...]
    all_to_all x2 -> x1, starting transfers between devices: 8.94 us -> 6.48 us  [on_device(): lax.all_to_all(jnp.broadcast_to(wide_rows, (PANELS, 1, TILE)), ('z', 'cor...]
    all_to_all x1, blocking collectives: 11.5 us -> 9.06 us  [on_device(): totals = lax.all_to_all(totals, ('z', 'core'), 0, 0)]
    pallas_call x1, Pallas kernels: 6.24 us -> 4.48 us  [multiply_other(): pl.pallas_call(other_kernel, out_shape=(pltpu.VMEM(MERGED, jnp.float32),...]
  transfers between devices with their start and end apart: 16 -> 18, of which waited for: 5 -> 4; matrix products, arithmetic and copies ran while one was open for 2% -> 3% of each run, Pallas kernels for 15% -> 13%
where the time goes in v4:
time: 83 us; the launch traced here: 82.6 us
  starting transfers between devices  38.7 us (47%)
  Pallas kernels  19 us (23%)
  waiting for transfers between devices  13.4 us (16%)
  blocking collectives  9.06 us (11%)
  local copies, waits for them, and re-layouts  2.03 us (2%)
    ppermute x3, starting transfers between devices, on_device(): theirs = tuple((lax.ppermute(block, 'core', SWAP) for block in later))  9.62 us
    all_to_all x1, blocking collectives, on_device(): totals = lax.all_to_all(totals, ('z', 'core'), 0, 0)  9.06 us
    ppermute x6, starting transfers between devices, exchange(): lax.ppermute(part, 'y', way)  9.03 us
    all_to_all x1, starting transfers between devices, on_device(): lax.all_to_all(jnp.broadcast_to(wide_rows, (PANELS, 1, TILE)), ('z', 'cor...  6.48 us
    all_to_all x1, starting transfers between devices, on_device(): req = lax.all_to_all(asks, ('y', 'x'), 0, 0)  5.44 us
    all_to_all x1, waiting for transfers between devices, on_device(): req = lax.all_to_all(asks, ('y', 'x'), 0, 0)  4.97 us
    all_to_all x1, waiting for transfers between devices, on_device(): lax.all_to_all(jnp.broadcast_to(wide_rows, (PANELS, 1, TILE)), ('z', 'cor...  4.52 us
    pallas_call x1, Pallas kernels, multiply_other(): pl.pallas_call(other_kernel, out_shape=(pltpu.VMEM(MERGED, jnp.float32),...  4.48 us
  transfers between devices with their start and end apart: 18, of which 4 were waited for; matrix products, arithmetic and copies ran while one was open for 3% of the time, Pallas kernels for 13%

profile of v4, /device:TPU:1, one launch (start us, length us, event | category | flops | bytes accessed | tf_op | source)
XLA Modules:
  0.0 82.6 jit_solution(6234323155100306820)
XLA Ops:
  0.0 3.3 %collective-permute-start = (bf16[24,128,128]{2,1,0:T(8,128)(2,1)}, bf16[24,128,128]{2,1,0:T(8,128)(2,1)}, u32[]{:S(2)}, u32[]{:S(2)}) collective-permute-start(bf16[24,128,128]{2,1,0:T(8,128)(2,1)} %bitcast.12), channel_id=1, source_target_pairs={{0,3},{3,0},{1,2},{2,1},{4,7},{7,4},{5,6},{6,5},{8,11},{11,8},{9,1... | collective-permute-start | bytes 2359304 | tf_op jit(solution)/shard_map/ppermute | solution.py:351
  3.3 0.8 pad_bitcast_fusion
  4.7 6.5 %all-to-all-start = ((s32[8,1,128]{2,1,0:T(1,128)}), s32[8,1,128]{2,1,0:T(1,128)S(1)}, u32[]{:S(2)}, u32[]{:S(2)}) async-start(s32[8,1,128]{2,1,0:T(1,128)} %broadcast_in_dim.12), calls=%async_computation | async-start | bytes 8192 | tf_op jit(solution)/shard_map/all_to_all | solution.py:353
  11.3 4.5 %all-to-all-done.rows = s32[8,1,128]{2,1,0:T(1,128)S(1)} async-done(((s32[8,1,128]{2,1,0:T(1,128)}), s32[8,1,128]{2,1,0:T(1,128)S(1)}, u32[]{:S(2)}, u32[]{:S(2)}) %all-to-all-start) | async-done | bytes 4128 | tf_op jit(solution)/shard_map/all_to_all | solution.py:353
  17.9 5.4 %all-to-all-start.1 = ((s32[16,2,128]{2,1,0:T(2,128)}), s32[16,2,128]{2,1,0:T(2,128)S(1)}, u32[]{:S(2)}, u32[]{:S(2)}) async-start(s32[16,2,128]{2,1,0:T(2,128)} %bitcast.8), calls=%async_computation.1 | async-start | bytes 32768 | tf_op jit(solution)/shard_map/all_to_all | solution.py:356
  23.3 1.4 %collective-permute-start.1 = (bf16[24,128,128]{2,1,0:T(8,128)(2,1)}, bf16[24,128,128]{2,1,0:T(8,128)(2,1)S(1)}, u32[]{:S(2)}, u32[]{:S(2)}) collective-permute-start(bf16[24,128,128]{2,1,0:T(8,128)(2,1)} %collective-permute-done.refs_1_.outer), channel_id=1, source_target_pairs={{0,1},{1,0},{2,3},{3,2},{4,5},{5,4},{6,7},{7,6},{8,9},{9,8},{10,11... | collective-permute-start | bytes 2359304 | tf_op jit(solution)/shard_map/ppermute | solution.py:364
  24.8 5.0 %all-to-all-done.1.req = s32[16,2,128]{2,1,0:T(2,128)S(1)} async-done(((s32[16,2,128]{2,1,0:T(2,128)}), s32[16,2,128]{2,1,0:T(2,128)S(1)}, u32[]{:S(2)}, u32[]{:S(2)}) %all-to-all-start.1) | async-done | bytes 16416 | tf_op jit(solution)/shard_map/all_to_all | solution.py:356
  29.8 3.1 %shard_map.30 = (bf16[8,128,128]{2,1,0:T(8,128)(2,1)}, bf16[8,128,128]{2,1,0:T(8,128)(2,1)}, bf16[8,128,128]{2,1,0:T(8,128)(2,1)}, bf16[8,128,128]{2,1,0:T(8,128)(2,1)}, s32[128]{0:T(128)S(4)}) custom-call(s32[4]{0:T(128)S(1)} %pad_add_fusion.pos, s32[16,2,128]{2,1,0:T(2,128)S(1)} %all-to-all-done.1.req, bf16[24,128,128]{2,1,0:T(8,128)(2,1)S(1)} %bitcast.16, ...), custom_call_target="tpu_custom_call" | custom-call | bytes 2097152 | tf_op jit(solution)/shard_map/pallas_call | solution.py:120
  33.1 1.8 %collective-permute-start.4 = (bf16[8,128,128]{2,1,0:T(8,128)(2,1)}, bf16[8,128,128]{2,1,0:T(8,128)(2,1)S(1)}, u32[]{:S(2)}, u32[]{:S(2)}) collective-permute-start(bf16[8,128,128]{2,1,0:T(8,128)(2,1)} %get-tuple-element.27), channel_id=1, source_target_pairs={{0,8},{4,12},{8,0},{12,4},{1,9},{5,13},{9,1},{13,5},{2,10},{6,14},... | collective-permute-start | bytes 786440 | tf_op jit(solution)/shard_map/ppermute | solution.py:344
  34.9 2.3 %collective-permute-start.5 = (bf16[8,128,128]{2,1,0:T(8,128)(2,1)}, bf16[8,128,128]{2,1,0:T(8,128)(2,1)S(1)}, u32[]{:S(2)}, u32[]{:S(2)}) collective-permute-start(bf16[8,128,128]{2,1,0:T(8,128)(2,1)} %get-tuple-element.28), channel_id=1, source_target_pairs={{0,12},{4,0},{8,4},{12,8},{1,13},{5,1},{9,5},{13,9},{2,14},{6,2},{... | collective-permute-start | bytes 786440 | tf_op jit(solution)/shard_map/ppermute | solution.py:344
  37.3 2.0 %collective-permute-start.8 = (bf16[24,128,128]{2,1,0:T(8,128)(2,1)S(1)}, bf16[24,128,128]{2,1,0:T(8,128)(2,1)S(1)}, u32[]{:S(2)}, u32[]{:S(2)}) collective-permute-start(bf16[24,128,128]{2,1,0:T(8,128)(2,1)S(1)} %broadcast_select_fusion), channel_id=1, source_target_pairs={{0,32},{32,64},{64,96},{96,0},{16,112},{48,16},{80,48},{112,80},{1... | collective-permute-start | bytes 2359304 | tf_op jit(solution)/shard_map/ppermute | solution.py:366
  39.3 2.0 %collective-permute-done.3.refs_0_.refs_1_ = bf16[8,128,128]{2,1,0:T(8,128)(2,1)S(1)} collective-permute-done((bf16[8,128,128]{2,1,0:T(8,128)(2,1)}, bf16[8,128,128]{2,1,0:T(8,128)(2,1)S(1)}, u32[]{:S(2)}, u32[]{:S(2)}) %collective-permute-start.3) | collective-permute-done | bytes 262176 | tf_op jit(solution)/shard_map/ppermute | solution.py:344
  41.3 2.3 %shard_map.33 = (bf16[8,128,128]{2,1,0:T(8,128)(2,1)}, bf16[8,128,128]{2,1,0:T(8,128)(2,1)}, bf16[8,128,128]{2,1,0:T(8,128)(2,1)}, bf16[8,128,128]{2,1,0:T(8,128)(2,1)}) custom-call(s32[128]{0:T(128)S(4)} %get-tuple-element.29.lists.___, bf16[24,128,128]{2,1,0:T(8,128)(2,1)} %collective-permute-done.refs_1_.outer, ...), custom_call_target="tpu_custom_call" | custom-call | bytes 2097152 | tf_op jit(solution)/shard_map/pallas_call | solution.py:131
  43.7 1.1 %collective-permute-start.9 = (bf16[8,128,128]{2,1,0:T(8,128)(2,1)}, bf16[8,128,128]{2,1,0:T(8,128)(2,1)S(1)}, u32[]{:S(2)}, u32[]{:S(2)}) collective-permute-start(bf16[8,128,128]{2,1,0:T(8,128)(2,1)} %get-tuple-element.34), channel_id=1, source_target_pairs={{0,4},{4,8},{8,12},{12,0},{1,5},{5,9},{9,13},{13,1},{2,6},{6,10},{... | collective-permute-start | bytes 786440 | tf_op jit(solution)/shard_map/ppermute | solution.py:344
  44.7 2.4 %collective-permute-start.10 = (bf16[8,128,128]{2,1,0:T(8,128)(2,1)}, bf16[8,128,128]{2,1,0:T(8,128)(2,1)S(1)}, u32[]{:S(2)}, u32[]{:S(2)}) collective-permute-start(bf16[8,128,128]{2,1,0:T(8,128)(2,1)} %get-tuple-element.35), channel_id=1, source_target_pairs={{0,8},{4,12},{8,0},{12,4},{1,9},{5,13},{9,1},{13,5},{2,10},{6,14},... | collective-permute-start | bytes 786440 | tf_op jit(solution)/shard_map/ppermute | solution.py:344
  47.1 1.2 %collective-permute-start.11 = (bf16[8,128,128]{2,1,0:T(8,128)(2,1)}, bf16[8,128,128]{2,1,0:T(8,128)(2,1)S(1)}, u32[]{:S(2)}, u32[]{:S(2)}) collective-permute-start(bf16[8,128,128]{2,1,0:T(8,128)(2,1)} %get-tuple-element.36), channel_id=1, source_target_pairs={{0,12},{4,0},{8,4},{12,8},{1,13},{5,1},{9,5},{13,9},{2,14},{6,2},{... | collective-permute-start | bytes 786440 | tf_op jit(solution)/shard_map/ppermute | solution.py:344
  48.3 6.2 %collective-permute-start.12 = (bf16[24,128,128]{2,1,0:T(8,128)(2,1)S(1)}, bf16[24,128,128]{2,1,0:T(8,128)(2,1)S(1)}, u32[]{:S(2)}, u32[]{:S(2)}) collective-permute-start(bf16[24,128,128]{2,1,0:T(8,128)(2,1)S(1)} %bitcast.17), channel_id=1, source_target_pairs={{0,16},{16,0},{1,17},{17,1},{2,18},{18,2},{3,19},{19,3},{4,20},{20... | collective-permute-start | bytes 2359304 | tf_op jit(solution)/shard_map/ppermute | solution.py:374
  54.5 3.9 %shard_map.28.plan = s32[512]{0:T(512)S(4)} custom-call(s32[4]{0:T(128)S(1)} %pad_add_fusion.pos, s32[8,1,128]{2,1,0:T(1,128)S(1)} %all-to-all-done.rows, s32[16,2,128]{2,1,0:T(2,128)S(1)} %all-to-all-done.1.req, bf16[24,128,128]{2,1,0:T(8,128)(2,1)S(1)} %collective-permute-done.1._.refs_0_.diag), custom_call_target="tpu_custom_call" | custom-call | bytes 33554432 | tf_op jit(solution)/shard_map/pallas_call | solution.py:180
  58.5 3.3 %collective-permute-start.14 = (bf16[24,128,128]{2,1,0:T(8,128)(2,1)S(1)}, bf16[24,128,128]{2,1,0:T(8,128)(2,1)S(1)}, u32[]{:S(2)}, u32[]{:S(2)}) collective-permute-start(bf16[24,128,128]{2,1,0:T(8,128)(2,1)S(1)} %collective-permute-done.7.refs_6_.refs_10_), channel_id=1, source_target_pairs={{0,16},{16,0},{1,17},{17,1},{2,18},{18,2},{3,19},{19,3},{4,20},{20... | collective-permute-start | bytes 2359304 | tf_op jit(solution)/shard_map/ppermute | solution.py:374
  61.9 1.9 %collective-permute-done.14.refs_9_.refs_14_ = bf16[24,128,128]{2,1,0:T(8,128)(2,1)S(1)} collective-permute-done((bf16[24,128,128]{2,1,0:T(8,128)(2,1)S(1)}, bf16[24,128,128]{2,1,0:T(8,128)(2,1)S(1)}, u32[]{:S(2)}, u32[]{:S(2)}) %collective-permute-start.14) | collective-permute-done | bytes 786464 | tf_op jit(solution)/shard_map/ppermute | solution.py:374
  63.8 1.7 %shard_map.35.refs_16_ = f32[24,3,128,128]{3,2,1,0:T(8,128)S(1)} custom-call(s32[512]{0:T(512)S(4)} %shard_map.28.plan, bf16[8,128,128]{2,1,0:T(8,128)(2,1)S(1)} %copy-done.1, bf16[8,128,128]{2,1,0:T(8,128)(2,1)S(1)} %collective-permute-done.3.refs_0_.refs_1_, bf16[8,128,128]{2,1,0:T(8,128)(2,1)S(1)} %collective-permute-done.4.refs_0_.refs_2_, ...), custom_call_target="tpu_custom_call" | custom-call | flops 402653184 | bytes 16777216 | tf_op jit(solution)/shard_map/pallas_call | solution.py:280
  65.5 4.5 %shard_map.37 = (f32[24,8,128,128]{3,2,1,0:T(8,128)S(1)}, f32[8,24,128]{2,1,0:T(8,128)}) custom-call(s32[512]{0:T(512)S(4)} %shard_map.28.plan, bf16[8,128,128]{2,1,0:T(8,128)(2,1)S(1)} %copy-done.1, bf16[8,128,128]{2,1,0:T(8,128)(2,1)S(1)} %collective-permute-done.3.refs_0_.refs_1_, bf16[8,128,128]{2,1,0:T(8,128)(2,1)S(1)} %collective-permute-done.4.refs_0_.refs_2_, ...), custom_call_target="tpu_custom_call" | custom-call | flops 402653184 | bytes 16777216 | tf_op jit(solution)/shard_map/pallas_call | solution.py:292
  70.0 9.1 %all_to_all.15.totals = f32[8,24,128]{2,1,0:T(8,128)S(1)} all-to-all(f32[8,24,128]{2,1,0:T(8,128)} %get-tuple-element.42), channel_id=1, replica_groups=mesh['z'=4,'core'=2,'y'=4,'x'=4] {'z','core'}, dimensions={0} | all-to-all | bytes 196608 | tf_op jit(solution)/shard_map/all_to_all | solution.py:381
  79.0 3.6 %shard_map.38 = bf16[8,24,128,128]{3,2,1,0:T(8,128)(2,1)} custom-call(s32[512]{0:T(512)S(4)} %shard_map.28.plan, f32[24,8,128,128]{3,2,1,0:T(8,128)S(1)} %get-tuple-element.41.merged, f32[8,24,128]{2,1,0:T(8,128)S(1)} %all_to_all.15.totals), custom_call_target="tpu_custom_call" | custom-call | flops 6291456 | bytes 20971520 | tf_op jit(solution)/shard_map/pallas_call | solution.py:328
  (36 shorter events, 3.3 us)
Async XLA Ops:
  0.0 23.3 %collective-permute-start = (bf16[24,128,128]{2,1,0:T(8,128)(2,1)}, bf16[24,128,128]{2,1,0:T(8,128)(2,1)}, u32[]{:S(2)}, u32[]{:S(2)}) collective-permute-start(bf16[24,128,128]{2,1,0:T(8,128)(2,1)} %bitcast.12), channel_id=1, source_target_pairs={{0,3},{3,0},{1,2},{2,1},{4,7},{7,4},{5,6},{6,5},{8,11},{11,8},{9,1... | collective-permute-start | bytes 2359304 | tf_op jit(solution)/shard_map/ppermute | solution.py:351
  3.3 21.5 %collective-permute-start.2 = (bf16[24,128,128]{2,1,0:T(8,128)(2,1)}, bf16[24,128,128]{2,1,0:T(8,128)(2,1)}, u32[]{:S(2)}, u32[]{:S(2)}) collective-permute-start(bf16[24,128,128]{2,1,0:T(8,128)(2,1)} %bitcast.13), channel_id=1, source_target_pairs={{0,1},{1,0},{2,3},{3,2},{4,5},{5,4},{6,7},{7,6},{8,9},{9,8},{10,11... | collective-permute-start | bytes 2359304 | tf_op jit(solution)/shard_map/ppermute | solution.py:350
  4.7 11.1 %all-to-all-start = ((s32[8,1,128]{2,1,0:T(1,128)}), s32[8,1,128]{2,1,0:T(1,128)S(1)}, u32[]{:S(2)}, u32[]{:S(2)}) async-start(s32[8,1,128]{2,1,0:T(1,128)} %broadcast_in_dim.12), calls=%async_computation | async-start | bytes 8192 | tf_op jit(solution)/shard_map/all_to_all | solution.py:353
  15.8 19.1 %collective-permute-start.7 = (bf16[24,128,128]{2,1,0:T(8,128)(2,1)}, bf16[24,128,128]{2,1,0:T(8,128)(2,1)S(1)}, u32[]{:S(2)}, u32[]{:S(2)}) collective-permute-start(bf16[24,128,128]{2,1,0:T(8,128)(2,1)} %bitcast.14), channel_id=1, source_target_pairs={{0,96},{32,0},{64,32},{96,64},{1,97},{33,1},{65,33},{97,65},{2,98}... | collective-permute-start | bytes 2359304 | tf_op jit(solution)/shard_map/ppermute | solution.py:359
  16.6 20.7 %collective-permute-start.6 = (bf16[24,128,128]{2,1,0:T(8,128)(2,1)}, bf16[24,128,128]{2,1,0:T(8,128)(2,1)S(1)}, u32[]{:S(2)}, u32[]{:S(2)}) collective-permute-start(bf16[24,128,128]{2,1,0:T(8,128)(2,1)} %bitcast.15), channel_id=1, source_target_pairs={{0,32},{32,64},{64,96},{96,0},{1,33},{33,65},{65,97},{97,1},{2,34}... | collective-permute-start | bytes 2359304 | tf_op jit(solution)/shard_map/ppermute | solution.py:358
  17.9 11.9 %all-to-all-start.1 = ((s32[16,2,128]{2,1,0:T(2,128)}), s32[16,2,128]{2,1,0:T(2,128)S(1)}, u32[]{:S(2)}, u32[]{:S(2)}) async-start(s32[16,2,128]{2,1,0:T(2,128)} %bitcast.8), calls=%async_computation.1 | async-start | bytes 32768 | tf_op jit(solution)/shard_map/all_to_all | solution.py:356
  23.3 6.4 %copy-start = (bf16[1,24,128,128]{3,2,1,0:T(8,128)(2,1)S(1)}, bf16[1,24,128,128]{3,2,1,0:T(8,128)(2,1)}, u32[]{:S(2)}) copy-start(bf16[1,24,128,128]{3,2,1,0:T(8,128)(2,1)} %param.2) | copy-start | bytes 2359300
  23.3 18.0 %collective-permute-start.1 = (bf16[24,128,128]{2,1,0:T(8,128)(2,1)}, bf16[24,128,128]{2,1,0:T(8,128)(2,1)S(1)}, u32[]{:S(2)}, u32[]{:S(2)}) collective-permute-start(bf16[24,128,128]{2,1,0:T(8,128)(2,1)} %collective-permute-done.refs_1_.outer), channel_id=1, source_target_pairs={{0,1},{1,0},{2,3},{3,2},{4,5},{5,4},{6,7},{7,6},{8,9},{9,8},{10,11... | collective-permute-start | bytes 2359304 | tf_op jit(solution)/shard_map/ppermute | solution.py:364
  32.8 8.5 %collective-permute-start.3 = (bf16[8,128,128]{2,1,0:T(8,128)(2,1)}, bf16[8,128,128]{2,1,0:T(8,128)(2,1)S(1)}, u32[]{:S(2)}, u32[]{:S(2)}) collective-permute-start(bf16[8,128,128]{2,1,0:T(8,128)(2,1)} %get-tuple-element.26), channel_id=1, source_target_pairs={{0,4},{4,8},{8,12},{12,0},{1,5},{5,9},{9,13},{13,1},{2,6},{6,10},{... | collective-permute-start | bytes 786440 | tf_op jit(solution)/shard_map/ppermute | solution.py:344
  33.1 14.0 %collective-permute-start.4 = (bf16[8,128,128]{2,1,0:T(8,128)(2,1)}, bf16[8,128,128]{2,1,0:T(8,128)(2,1)S(1)}, u32[]{:S(2)}, u32[]{:S(2)}) collective-permute-start(bf16[8,128,128]{2,1,0:T(8,128)(2,1)} %get-tuple-element.27), channel_id=1, source_target_pairs={{0,8},{4,12},{8,0},{12,4},{1,9},{5,13},{9,1},{13,5},{2,10},{6,14},... | collective-permute-start | bytes 786440 | tf_op jit(solution)/shard_map/ppermute | solution.py:344
  34.9 13.4 %collective-permute-start.5 = (bf16[8,128,128]{2,1,0:T(8,128)(2,1)}, bf16[8,128,128]{2,1,0:T(8,128)(2,1)S(1)}, u32[]{:S(2)}, u32[]{:S(2)}) collective-permute-start(bf16[8,128,128]{2,1,0:T(8,128)(2,1)} %get-tuple-element.28), channel_id=1, source_target_pairs={{0,12},{4,0},{8,4},{12,8},{1,13},{5,1},{9,5},{13,9},{2,14},{6,2},{... | collective-permute-start | bytes 786440 | tf_op jit(solution)/shard_map/ppermute | solution.py:344
  37.3 21.1 %collective-permute-start.8 = (bf16[24,128,128]{2,1,0:T(8,128)(2,1)S(1)}, bf16[24,128,128]{2,1,0:T(8,128)(2,1)S(1)}, u32[]{:S(2)}, u32[]{:S(2)}) collective-permute-start(bf16[24,128,128]{2,1,0:T(8,128)(2,1)S(1)} %broadcast_select_fusion), channel_id=1, source_target_pairs={{0,32},{32,64},{64,96},{96,0},{16,112},{48,16},{80,48},{112,80},{1... | collective-permute-start | bytes 2359304 | tf_op jit(solution)/shard_map/ppermute | solution.py:366
  43.7 14.9 %collective-permute-start.9 = (bf16[8,128,128]{2,1,0:T(8,128)(2,1)}, bf16[8,128,128]{2,1,0:T(8,128)(2,1)S(1)}, u32[]{:S(2)}, u32[]{:S(2)}) collective-permute-start(bf16[8,128,128]{2,1,0:T(8,128)(2,1)} %get-tuple-element.34), channel_id=1, source_target_pairs={{0,4},{4,8},{8,12},{12,0},{1,5},{5,9},{9,13},{13,1},{2,6},{6,10},{... | collective-permute-start | bytes 786440 | tf_op jit(solution)/shard_map/ppermute | solution.py:344
  44.7 17.2 %collective-permute-start.10 = (bf16[8,128,128]{2,1,0:T(8,128)(2,1)}, bf16[8,128,128]{2,1,0:T(8,128)(2,1)S(1)}, u32[]{:S(2)}, u32[]{:S(2)}) collective-permute-start(bf16[8,128,128]{2,1,0:T(8,128)(2,1)} %get-tuple-element.35), channel_id=1, source_target_pairs={{0,8},{4,12},{8,0},{12,4},{1,9},{5,13},{9,1},{13,5},{2,10},{6,14},... | collective-permute-start | bytes 786440 | tf_op jit(solution)/shard_map/ppermute | solution.py:344
  47.1 14.8 %collective-permute-start.11 = (bf16[8,128,128]{2,1,0:T(8,128)(2,1)}, bf16[8,128,128]{2,1,0:T(8,128)(2,1)S(1)}, u32[]{:S(2)}, u32[]{:S(2)}) collective-permute-start(bf16[8,128,128]{2,1,0:T(8,128)(2,1)} %get-tuple-element.36), channel_id=1, source_target_pairs={{0,12},{4,0},{8,4},{12,8},{1,13},{5,1},{9,5},{13,9},{2,14},{6,2},{... | collective-permute-start | bytes 786440 | tf_op jit(solution)/shard_map/ppermute | solution.py:344
  48.3 13.6 %collective-permute-start.12 = (bf16[24,128,128]{2,1,0:T(8,128)(2,1)S(1)}, bf16[24,128,128]{2,1,0:T(8,128)(2,1)S(1)}, u32[]{:S(2)}, u32[]{:S(2)}) collective-permute-start(bf16[24,128,128]{2,1,0:T(8,128)(2,1)S(1)} %bitcast.17), channel_id=1, source_target_pairs={{0,16},{16,0},{1,17},{17,1},{2,18},{18,2},{3,19},{19,3},{4,20},{20... | collective-permute-start | bytes 2359304 | tf_op jit(solution)/shard_map/ppermute | solution.py:374
  58.4 5.4 %copy-start.1 = (bf16[8,128,128]{2,1,0:T(8,128)(2,1)S(1)}, bf16[8,128,128]{2,1,0:T(8,128)(2,1)}, u32[]{:S(2)}) copy-start(bf16[8,128,128]{2,1,0:T(8,128)(2,1)} %get-tuple-element.25.refs_0_) | copy-start | bytes 786436
  58.4 5.4 %copy-start.2 = (bf16[8,128,128]{2,1,0:T(8,128)(2,1)S(1)}, bf16[8,128,128]{2,1,0:T(8,128)(2,1)}, u32[]{:S(2)}) copy-start(bf16[8,128,128]{2,1,0:T(8,128)(2,1)} %get-tuple-element.33.refs_10_.refs_4_) | copy-start | bytes 786436
  58.4 3.5 %collective-permute-start.13 = (bf16[24,128,128]{2,1,0:T(8,128)(2,1)S(1)}, bf16[24,128,128]{2,1,0:T(8,128)(2,1)S(1)}, u32[]{:S(2)}, u32[]{:S(2)}) collective-permute-start(bf16[24,128,128]{2,1,0:T(8,128)(2,1)S(1)} %collective-permute-done.6.refs_5_.refs_9_), channel_id=1, source_target_pairs={{0,16},{16,0},{1,17},{17,1},{2,18},{18,2},{3,19},{19,3},{4,20},{20... | collective-permute-start | bytes 2359304 | tf_op jit(solution)/shard_map/ppermute | solution.py:374
  58.5 5.2 %collective-permute-start.14 = (bf16[24,128,128]{2,1,0:T(8,128)(2,1)S(1)}, bf16[24,128,128]{2,1,0:T(8,128)(2,1)S(1)}, u32[]{:S(2)}, u32[]{:S(2)}) collective-permute-start(bf16[24,128,128]{2,1,0:T(8,128)(2,1)S(1)} %collective-permute-done.7.refs_6_.refs_10_), channel_id=1, source_target_pairs={{0,16},{16,0},{1,17},{17,1},{2,18},{18,2},{3,19},{19,3},{4,20},{20... | collective-permute-start | bytes 2359304 | tf_op jit(solution)/shard_map/ppermute | solution.py:374
  61.9 3.6 %collective-permute-start.15 = (bf16[24,128,128]{2,1,0:T(8,128)(2,1)S(1)}, bf16[24,128,128]{2,1,0:T(8,128)(2,1)S(1)}, u32[]{:S(2)}, u32[]{:S(2)}) collective-permute-start(bf16[24,128,128]{2,1,0:T(8,128)(2,1)S(1)} %collective-permute-done.8.refs_11_), channel_id=1, source_target_pairs={{0,16},{16,0},{1,17},{17,1},{2,18},{18,2},{3,19},{19,3},{4,20},{20... | collective-permute-start | bytes 2359304 | tf_op jit(solution)/shard_map/ppermute | solution.py:379

commit v5 on v4

--- a/solution.py
+++ b/solution.py
@@ -209,7 +209,8 @@
 
 
 def own_kernel(plan, *refs):
-    pieces, mine, theirs, (_, _, early, left) = refs[:4], refs[4:7], refs[7:10], refs[10:]
+    pieces, mine, theirs, (_, _, early, done, left) = refs[:4], refs[4:7], refs[7:10], refs[10:]
+    done[0] = jnp.int32(0)
     gather(plan, pieces, left)
 
     def work(rights, _):
@@ -279,16 +280,16 @@
 def multiply_own(plan, left, mine, theirs, after):
     return pl.pallas_call(
         own_kernel,
-        out_shape=pltpu.VMEM(EARLY, jnp.float32),
+        out_shape=(pltpu.VMEM(EARLY, jnp.float32), pltpu.SMEM((8,), jnp.int32)),
         in_specs=[SMEM] + [VMEM] * 10 + [ANY] * 2,
-        out_specs=VMEM,
+        out_specs=(VMEM, SMEM),
         scratch_shapes=[LEFT],
         compiler_params=pltpu.CompilerParams(vmem_limit_bytes=LIMIT),
         cost_estimate=pl.CostEstimate(flops=2 * 96 * TILE**3, bytes_accessed=16 << 20, transcendentals=0),
     )(plan, *in_vmem(*left, *mine, *theirs), *after)
 
 
-def multiply_other(plan, own_left, left, mine, theirs, early):
+def multiply_other(plan, own_left, left, mine, theirs, early, done):
     return pl.pallas_call(
         other_kernel,
         out_shape=(pltpu.VMEM(MERGED, jnp.float32), pltpu.HBM((PANELS, BLK, TILE), jnp.float32)),
@@ -297,7 +298,7 @@
         scratch_shapes=[LEFT, LEFT, pltpu.VMEM((BLK, TILE), jnp.float32)],
         compiler_params=pltpu.CompilerParams(vmem_limit_bytes=LIMIT),
         cost_estimate=pl.CostEstimate(flops=2 * 96 * TILE**3, bytes_accessed=16 << 20, transcendentals=0),
-    )(plan, *in_vmem(*own_left, *left, *mine, *theirs, early), token(Y2_COST, *left[1:]))
+    )(plan, *in_vmem(*own_left, *left, *mine, *theirs, early), token(Y2_COST, *left[1:], done))
 
 
 def scale_kernel(plan, merged, totals, out, factor):
@@ -358,7 +359,8 @@
     below = lax.ppermute(own_z, "z", UP)
     above = lax.ppermute(own_z, "z", DOWN)
 
-    arrived = token(TOKEN_COST, inner, outer)
+    their_own = lax.ppermute(own, "core", SWAP)
+    arrived = token(TOKEN_COST, inner, outer, their_own)
     *send1, lists = select_own(pos, req, own, inner, arrived)
     left1 = exchange(send1)
     diag = lax.ppermute(outer, "x", INNER)
@@ -370,14 +372,14 @@
     send2 = select(select_other_kernel, (sent,) * 4, lists, (outer, diag), after)
     left2 = exchange(send2)
     mine = (own, below, above)
-    kept, *later = lax.optimization_barrier((send2[0], *mine))
-    theirs = tuple(lax.ppermute(block, "core", SWAP) for block in later)
+    kept, *later = lax.optimization_barrier((send2[0], below, above))
+    theirs = (their_own, *(lax.ppermute(block, "core", SWAP) for block in later))
     left2 = (kept, *left2[1:])
-    early = multiply_own(plan, left1, mine, theirs, (kept, token(Y1_LATE_COST, *left1[2:])))
+    early, done = multiply_own(plan, left1, mine, theirs, (kept, token(Y1_LATE_COST, *left1[2:])))
     kept2, far = lax.optimization_barrier((kept, far))
     left2 = (kept2, *left2[1:])
     mine, theirs = (*mine, far), (*theirs, lax.ppermute(far, "core", SWAP))
-    merged, totals = multiply_other(plan, left1, left2, mine, theirs, early)
+    merged, totals = multiply_other(plan, left1, left2, mine, theirs, early, done)
     totals = lax.all_to_all(totals, ("z", "core"), 0, 0)
     return scale(plan, merged, totals)[None]
 

time: 83 us -> 81.1 us (0.977)
  starting transfers between devices: 38.7 us -> 36.1 us
  Pallas kernels: 19 us -> 21.2 us
  waiting for transfers between devices: 13.4 us -> 11.6 us
    ppermute x3, starting transfers between devices: 9.62 us -> 7.45 us  [the longest x2 6.49 us: on_device(): lax.ppermute(block, 'core', SWAP)]
    ppermute x3, waiting for transfers between devices: 1.87 us -> 0.01 us  [the longest x2 0.01 us: on_device(): lax.ppermute(block, 'core', SWAP)]
    pallas_call x1, Pallas kernels: 4.48 us -> 5.63 us  [multiply_other(): pl.pallas_call(other_kernel, out_shape=(pltpu.VMEM(MERGED, jnp.float32),...]
    pallas_call x1, Pallas kernels: 1.69 us -> 2.83 us  [multiply_own(): pl.pallas_call(own_kernel, out_shape=(pltpu.VMEM(EARLY, jnp.float32), plt...]
    all_to_all x1, starting transfers between devices: 6.48 us -> 5.53 us  [on_device(): lax.all_to_all(jnp.broadcast_to(wide_rows, (PANELS, 1, TILE)), ('z', 'cor...]
  transfers between devices with their start and end apart: 18 -> 18, of which waited for: 4 -> 3; matrix products, arithmetic and copies ran while one was open for 3% -> 3% of each run, Pallas kernels for 13% -> 15%
where the time goes in v5:
time: 81.1 us; the launch traced here: 80.7 us
  starting transfers between devices  36.1 us (45%)
  Pallas kernels  21.2 us (26%)
  waiting for transfers between devices  11.6 us (14%)
  blocking collectives  9.46 us (12%)
  local copies, waits for them, and re-layouts  2.02 us (2%)
    all_to_all x1, blocking collectives, on_device(): totals = lax.all_to_all(totals, ('z', 'core'), 0, 0)  9.46 us
    ppermute x6, starting transfers between devices, exchange(): lax.ppermute(part, 'y', way)  9 us
    ppermute x2, starting transfers between devices, on_device(): lax.ppermute(block, 'core', SWAP)  6.49 us
    pallas_call x1, Pallas kernels, multiply_other(): pl.pallas_call(other_kernel, out_shape=(pltpu.VMEM(MERGED, jnp.float32),...  5.63 us
    all_to_all x1, starting transfers between devices, on_device(): lax.all_to_all(jnp.broadcast_to(wide_rows, (PANELS, 1, TILE)), ('z', 'cor...  5.53 us
    all_to_all x1, starting transfers between devices, on_device(): req = lax.all_to_all(asks, ('y', 'x'), 0, 0)  5.44 us
    all_to_all x1, waiting for transfers between devices, on_device(): req = lax.all_to_all(asks, ('y', 'x'), 0, 0)  4.96 us
    all_to_all x1, waiting for transfers between devices, on_device(): lax.all_to_all(jnp.broadcast_to(wide_rows, (PANELS, 1, TILE)), ('z', 'cor...  4.52 us
  transfers between devices with their start and end apart: 18, of which 3 were waited for; matrix products, arithmetic and copies ran while one was open for 3% of the time, Pallas kernels for 15%

profile of v5, /device:TPU:1, one launch (start us, length us, event | category | flops | bytes accessed | tf_op | source)
XLA Modules:
  0.0 80.7 jit_solution(1894359065377662976)
XLA Ops:
  0.0 3.3 %collective-permute-start = (bf16[24,128,128]{2,1,0:T(8,128)(2,1)}, bf16[24,128,128]{2,1,0:T(8,128)(2,1)}, u32[]{:S(2)}, u32[]{:S(2)}) collective-permute-start(bf16[24,128,128]{2,1,0:T(8,128)(2,1)} %bitcast.12), channel_id=1, source_target_pairs={{0,3},{3,0},{1,2},{2,1},{4,7},{7,4},{5,6},{6,5},{8,11},{11,8},{9,1... | collective-permute-start | bytes 2359304 | tf_op jit(solution)/shard_map/ppermute | solution.py:352
  3.3 1.0 %collective-permute-start.3 = (bf16[24,128,128]{2,1,0:T(8,128)(2,1)}, bf16[24,128,128]{2,1,0:T(8,128)(2,1)}, u32[]{:S(2)}, u32[]{:S(2)}) collective-permute-start(bf16[24,128,128]{2,1,0:T(8,128)(2,1)} %bitcast.13), channel_id=1, source_target_pairs={{0,16},{16,0},{1,17},{17,1},{2,18},{18,2},{3,19},{19,3},{4,20},{20... | collective-permute-start | bytes 2359304 | tf_op jit(solution)/shard_map/ppermute | solution.py:362
  4.3 0.8 pad_bitcast_fusion
  5.7 5.5 %all-to-all-start = ((s32[8,1,128]{2,1,0:T(1,128)}), s32[8,1,128]{2,1,0:T(1,128)S(1)}, u32[]{:S(2)}, u32[]{:S(2)}) async-start(s32[8,1,128]{2,1,0:T(1,128)} %broadcast_in_dim.12), calls=%async_computation | async-start | bytes 8192 | tf_op jit(solution)/shard_map/all_to_all | solution.py:354
  11.3 4.5 %all-to-all-done.rows = s32[8,1,128]{2,1,0:T(1,128)S(1)} async-done(((s32[8,1,128]{2,1,0:T(1,128)}), s32[8,1,128]{2,1,0:T(1,128)S(1)}, u32[]{:S(2)}, u32[]{:S(2)}) %all-to-all-start) | async-done | bytes 4128 | tf_op jit(solution)/shard_map/all_to_all | solution.py:354
  15.8 0.8 collective-permute-start.8
  17.9 5.4 %all-to-all-start.1 = ((s32[16,2,128]{2,1,0:T(2,128)}), s32[16,2,128]{2,1,0:T(2,128)S(1)}, u32[]{:S(2)}, u32[]{:S(2)}) async-start(s32[16,2,128]{2,1,0:T(2,128)} %bitcast.8), calls=%async_computation.1 | async-start | bytes 32768 | tf_op jit(solution)/shard_map/all_to_all | solution.py:357
  23.3 1.4 %collective-permute-start.1 = (bf16[24,128,128]{2,1,0:T(8,128)(2,1)}, bf16[24,128,128]{2,1,0:T(8,128)(2,1)S(1)}, u32[]{:S(2)}, u32[]{:S(2)}) collective-permute-start(bf16[24,128,128]{2,1,0:T(8,128)(2,1)} %collective-permute-done.refs_1_.outer), channel_id=1, source_target_pairs={{0,1},{1,0},{2,3},{3,2},{4,5},{5,4},{6,7},{7,6},{8,9},{9,8},{10,11... | collective-permute-start | bytes 2359304 | tf_op jit(solution)/shard_map/ppermute | solution.py:366
  24.8 5.0 %all-to-all-done.1.req = s32[16,2,128]{2,1,0:T(2,128)S(1)} async-done(((s32[16,2,128]{2,1,0:T(2,128)}), s32[16,2,128]{2,1,0:T(2,128)S(1)}, u32[]{:S(2)}, u32[]{:S(2)}) %all-to-all-start.1) | async-done | bytes 16416 | tf_op jit(solution)/shard_map/all_to_all | solution.py:357
  29.8 3.1 %shard_map.30 = (bf16[8,128,128]{2,1,0:T(8,128)(2,1)}, bf16[8,128,128]{2,1,0:T(8,128)(2,1)}, bf16[8,128,128]{2,1,0:T(8,128)(2,1)}, bf16[8,128,128]{2,1,0:T(8,128)(2,1)}, s32[128]{0:T(128)S(4)}) custom-call(s32[4]{0:T(128)S(1)} %pad_add_fusion.pos, s32[16,2,128]{2,1,0:T(2,128)S(1)} %all-to-all-done.1.req, bf16[24,128,128]{2,1,0:T(8,128)(2,1)S(1)} %bitcast.17, ...), custom_call_target="tpu_custom_call" | custom-call | bytes 2097152 | tf_op jit(solution)/shard_map/pallas_call | solution.py:120
  33.1 1.8 %collective-permute-start.5 = (bf16[8,128,128]{2,1,0:T(8,128)(2,1)}, bf16[8,128,128]{2,1,0:T(8,128)(2,1)S(1)}, u32[]{:S(2)}, u32[]{:S(2)}) collective-permute-start(bf16[8,128,128]{2,1,0:T(8,128)(2,1)} %get-tuple-element.28), channel_id=1, source_target_pairs={{0,8},{4,12},{8,0},{12,4},{1,9},{5,13},{9,1},{13,5},{2,10},{6,14},... | collective-permute-start | bytes 786440 | tf_op jit(solution)/shard_map/ppermute | solution.py:345
  34.9 2.3 %collective-permute-start.6 = (bf16[8,128,128]{2,1,0:T(8,128)(2,1)}, bf16[8,128,128]{2,1,0:T(8,128)(2,1)S(1)}, u32[]{:S(2)}, u32[]{:S(2)}) collective-permute-start(bf16[8,128,128]{2,1,0:T(8,128)(2,1)} %get-tuple-element.29), channel_id=1, source_target_pairs={{0,12},{4,0},{8,4},{12,8},{1,13},{5,1},{9,5},{13,9},{2,14},{6,2},{... | collective-permute-start | bytes 786440 | tf_op jit(solution)/shard_map/ppermute | solution.py:345
  37.3 2.0 %collective-permute-start.9 = (bf16[24,128,128]{2,1,0:T(8,128)(2,1)S(1)}, bf16[24,128,128]{2,1,0:T(8,128)(2,1)S(1)}, u32[]{:S(2)}, u32[]{:S(2)}) collective-permute-start(bf16[24,128,128]{2,1,0:T(8,128)(2,1)S(1)} %broadcast_select_fusion), channel_id=1, source_target_pairs={{0,32},{32,64},{64,96},{96,0},{16,112},{48,16},{80,48},{112,80},{1... | collective-permute-start | bytes 2359304 | tf_op jit(solution)/shard_map/ppermute | solution.py:368
  39.3 2.1 %collective-permute-done.4.refs_0_.refs_1_ = bf16[8,128,128]{2,1,0:T(8,128)(2,1)S(1)} collective-permute-done((bf16[8,128,128]{2,1,0:T(8,128)(2,1)}, bf16[8,128,128]{2,1,0:T(8,128)(2,1)S(1)}, u32[]{:S(2)}, u32[]{:S(2)}) %collective-permute-start.4) | collective-permute-done | bytes 262176 | tf_op jit(solution)/shard_map/ppermute | solution.py:345
  41.3 2.2 %shard_map.33 = (bf16[8,128,128]{2,1,0:T(8,128)(2,1)}, bf16[8,128,128]{2,1,0:T(8,128)(2,1)}, bf16[8,128,128]{2,1,0:T(8,128)(2,1)}, bf16[8,128,128]{2,1,0:T(8,128)(2,1)}) custom-call(s32[128]{0:T(128)S(4)} %get-tuple-element.30.lists.___, bf16[24,128,128]{2,1,0:T(8,128)(2,1)} %collective-permute-done.refs_1_.outer, ...), custom_call_target="tpu_custom_call" | custom-call | bytes 2097152 | tf_op jit(solution)/shard_map/pallas_call | solution.py:131
  43.6 1.0 %collective-permute-start.10 = (bf16[8,128,128]{2,1,0:T(8,128)(2,1)}, bf16[8,128,128]{2,1,0:T(8,128)(2,1)S(1)}, u32[]{:S(2)}, u32[]{:S(2)}) collective-permute-start(bf16[8,128,128]{2,1,0:T(8,128)(2,1)} %get-tuple-element.35), channel_id=1, source_target_pairs={{0,4},{4,8},{8,12},{12,0},{1,5},{5,9},{9,13},{13,1},{2,6},{6,10},{... | collective-permute-start | bytes 786440 | tf_op jit(solution)/shard_map/ppermute | solution.py:345
  44.6 2.4 %collective-permute-start.11 = (bf16[8,128,128]{2,1,0:T(8,128)(2,1)}, bf16[8,128,128]{2,1,0:T(8,128)(2,1)S(1)}, u32[]{:S(2)}, u32[]{:S(2)}) collective-permute-start(bf16[8,128,128]{2,1,0:T(8,128)(2,1)} %get-tuple-element.36), channel_id=1, source_target_pairs={{0,8},{4,12},{8,0},{12,4},{1,9},{5,13},{9,1},{13,5},{2,10},{6,14},... | collective-permute-start | bytes 786440 | tf_op jit(solution)/shard_map/ppermute | solution.py:345
  47.0 1.2 %collective-permute-start.12 = (bf16[8,128,128]{2,1,0:T(8,128)(2,1)}, bf16[8,128,128]{2,1,0:T(8,128)(2,1)S(1)}, u32[]{:S(2)}, u32[]{:S(2)}) collective-permute-start(bf16[8,128,128]{2,1,0:T(8,128)(2,1)} %get-tuple-element.37), channel_id=1, source_target_pairs={{0,12},{4,0},{8,4},{12,8},{1,13},{5,1},{9,5},{13,9},{2,14},{6,2},{... | collective-permute-start | bytes 786440 | tf_op jit(solution)/shard_map/ppermute | solution.py:345
  48.2 6.4 %collective-permute-start.13 = (bf16[24,128,128]{2,1,0:T(8,128)(2,1)S(1)}, bf16[24,128,128]{2,1,0:T(8,128)(2,1)S(1)}, u32[]{:S(2)}, u32[]{:S(2)}) collective-permute-start(bf16[24,128,128]{2,1,0:T(8,128)(2,1)S(1)} %collective-permute-done.7.refs_5_.refs_9_), channel_id=1, source_target_pairs={{0,16},{16,0},{1,17},{17,1},{2,18},{18,2},{3,19},{19,3},{4,20},{20... | collective-permute-start | bytes 2359304 | tf_op jit(solution)/shard_map/ppermute | solution.py:376
  54.7 3.9 %shard_map.28.plan = s32[512]{0:T(512)S(4)} custom-call(s32[4]{0:T(128)S(1)} %pad_add_fusion.pos, s32[8,1,128]{2,1,0:T(1,128)S(1)} %all-to-all-done.rows, s32[16,2,128]{2,1,0:T(2,128)S(1)} %all-to-all-done.1.req, bf16[24,128,128]{2,1,0:T(8,128)(2,1)S(1)} %collective-permute-done.1._.refs_0_.diag), custom_call_target="tpu_custom_call" | custom-call | bytes 33554432 | tf_op jit(solution)/shard_map/pallas_call | solution.py:180
  59.1 2.8 %shard_map.35 = (f32[24,3,128,128]{3,2,1,0:T(8,128)S(1)}, s32[8]{0:T(128)S(4)}) custom-call(s32[512]{0:T(512)S(4)} %shard_map.28.plan, bf16[8,128,128]{2,1,0:T(8,128)(2,1)S(1)} %copy-done.1, bf16[8,128,128]{2,1,0:T(8,128)(2,1)S(1)} %collective-permute-done.4.refs_0_.refs_1_, bf16[8,128,128]{2,1,0:T(8,128)(2,1)S(1)} %collective-permute-done.5.refs_0_.refs_2_, ...), custom_call_target="tpu_custom_call" | custom-call | flops 402653184 | bytes 16777216 | tf_op jit(solution)/shard_map/pallas_call | solution.py:281
  62.0 5.6 %shard_map.37 = (f32[24,8,128,128]{3,2,1,0:T(8,128)S(1)}, f32[8,24,128]{2,1,0:T(8,128)}) custom-call(s32[512]{0:T(512)S(4)} %shard_map.28.plan, bf16[8,128,128]{2,1,0:T(8,128)(2,1)S(1)} %copy-done.1, bf16[8,128,128]{2,1,0:T(8,128)(2,1)S(1)} %collective-permute-done.4.refs_0_.refs_1_, bf16[8,128,128]{2,1,0:T(8,128)(2,1)S(1)} %collective-permute-done.5.refs_0_.refs_2_, ...), custom_call_target="tpu_custom_call" | custom-call | flops 402653184 | bytes 16777216 | tf_op jit(solution)/shard_map/pallas_call | solution.py:293
  67.7 9.5 %all_to_all.15.totals = f32[8,24,128]{2,1,0:T(8,128)S(1)} all-to-all(f32[8,24,128]{2,1,0:T(8,128)} %get-tuple-element.44), channel_id=1, replica_groups=mesh['z'=4,'core'=2,'y'=4,'x'=4] {'z','core'}, dimensions={0} | all-to-all | bytes 196608 | tf_op jit(solution)/shard_map/all_to_all | solution.py:383
  77.1 3.6 %shard_map.38 = bf16[8,24,128,128]{3,2,1,0:T(8,128)(2,1)} custom-call(s32[512]{0:T(512)S(4)} %shard_map.28.plan, f32[24,8,128,128]{3,2,1,0:T(8,128)S(1)} %get-tuple-element.43.merged, f32[8,24,128]{2,1,0:T(8,128)S(1)} %all_to_all.15.totals), custom_call_target="tpu_custom_call" | custom-call | flops 6291456 | bytes 20971520 | tf_op jit(solution)/shard_map/pallas_call | solution.py:329
  (36 shorter events, 3.0 us)
Async XLA Ops:
  0.0 23.3 %collective-permute-start = (bf16[24,128,128]{2,1,0:T(8,128)(2,1)}, bf16[24,128,128]{2,1,0:T(8,128)(2,1)}, u32[]{:S(2)}, u32[]{:S(2)}) collective-permute-start(bf16[24,128,128]{2,1,0:T(8,128)(2,1)} %bitcast.12), channel_id=1, source_target_pairs={{0,3},{3,0},{1,2},{2,1},{4,7},{7,4},{5,6},{6,5},{8,11},{11,8},{9,1... | collective-permute-start | bytes 2359304 | tf_op jit(solution)/shard_map/ppermute | solution.py:352
  3.3 21.5 %collective-permute-start.3 = (bf16[24,128,128]{2,1,0:T(8,128)(2,1)}, bf16[24,128,128]{2,1,0:T(8,128)(2,1)}, u32[]{:S(2)}, u32[]{:S(2)}) collective-permute-start(bf16[24,128,128]{2,1,0:T(8,128)(2,1)} %bitcast.13), channel_id=1, source_target_pairs={{0,16},{16,0},{1,17},{17,1},{2,18},{18,2},{3,19},{19,3},{4,20},{20... | collective-permute-start | bytes 2359304 | tf_op jit(solution)/shard_map/ppermute | solution.py:362
  4.3 20.5 %collective-permute-start.2 = (bf16[24,128,128]{2,1,0:T(8,128)(2,1)}, bf16[24,128,128]{2,1,0:T(8,128)(2,1)}, u32[]{:S(2)}, u32[]{:S(2)}) collective-permute-start(bf16[24,128,128]{2,1,0:T(8,128)(2,1)} %bitcast.14), channel_id=1, source_target_pairs={{0,1},{1,0},{2,3},{3,2},{4,5},{5,4},{6,7},{7,6},{8,9},{9,8},{10,11... | collective-permute-start | bytes 2359304 | tf_op jit(solution)/shard_map/ppermute | solution.py:351
  5.7 10.1 %all-to-all-start = ((s32[8,1,128]{2,1,0:T(1,128)}), s32[8,1,128]{2,1,0:T(1,128)S(1)}, u32[]{:S(2)}, u32[]{:S(2)}) async-start(s32[8,1,128]{2,1,0:T(1,128)} %broadcast_in_dim.12), calls=%async_computation | async-start | bytes 8192 | tf_op jit(solution)/shard_map/all_to_all | solution.py:354
  15.8 19.1 %collective-permute-start.8 = (bf16[24,128,128]{2,1,0:T(8,128)(2,1)}, bf16[24,128,128]{2,1,0:T(8,128)(2,1)S(1)}, u32[]{:S(2)}, u32[]{:S(2)}) collective-permute-start(bf16[24,128,128]{2,1,0:T(8,128)(2,1)} %bitcast.15), channel_id=1, source_target_pairs={{0,96},{32,0},{64,32},{96,64},{1,97},{33,1},{65,33},{97,65},{2,98}... | collective-permute-start | bytes 2359304 | tf_op jit(solution)/shard_map/ppermute | solution.py:360
  16.6 20.7 %collective-permute-start.7 = (bf16[24,128,128]{2,1,0:T(8,128)(2,1)}, bf16[24,128,128]{2,1,0:T(8,128)(2,1)S(1)}, u32[]{:S(2)}, u32[]{:S(2)}) collective-permute-start(bf16[24,128,128]{2,1,0:T(8,128)(2,1)} %bitcast.16), channel_id=1, source_target_pairs={{0,32},{32,64},{64,96},{96,0},{1,33},{33,65},{65,97},{97,1},{2,34}... | collective-permute-start | bytes 2359304 | tf_op jit(solution)/shard_map/ppermute | solution.py:359
  17.9 11.9 %all-to-all-start.1 = ((s32[16,2,128]{2,1,0:T(2,128)}), s32[16,2,128]{2,1,0:T(2,128)S(1)}, u32[]{:S(2)}, u32[]{:S(2)}) async-start(s32[16,2,128]{2,1,0:T(2,128)} %bitcast.8), calls=%async_computation.1 | async-start | bytes 32768 | tf_op jit(solution)/shard_map/all_to_all | solution.py:357
  23.3 6.4 %copy-start = (bf16[1,24,128,128]{3,2,1,0:T(8,128)(2,1)S(1)}, bf16[1,24,128,128]{3,2,1,0:T(8,128)(2,1)}, u32[]{:S(2)}) copy-start(bf16[1,24,128,128]{3,2,1,0:T(8,128)(2,1)} %param.2) | copy-start | bytes 2359300
  23.3 18.0 %collective-permute-start.1 = (bf16[24,128,128]{2,1,0:T(8,128)(2,1)}, bf16[24,128,128]{2,1,0:T(8,128)(2,1)S(1)}, u32[]{:S(2)}, u32[]{:S(2)}) collective-permute-start(bf16[24,128,128]{2,1,0:T(8,128)(2,1)} %collective-permute-done.refs_1_.outer), channel_id=1, source_target_pairs={{0,1},{1,0},{2,3},{3,2},{4,5},{5,4},{6,7},{7,6},{8,9},{9,8},{10,11... | collective-permute-start | bytes 2359304 | tf_op jit(solution)/shard_map/ppermute | solution.py:366
  32.9 8.5 %collective-permute-start.4 = (bf16[8,128,128]{2,1,0:T(8,128)(2,1)}, bf16[8,128,128]{2,1,0:T(8,128)(2,1)S(1)}, u32[]{:S(2)}, u32[]{:S(2)}) collective-permute-start(bf16[8,128,128]{2,1,0:T(8,128)(2,1)} %get-tuple-element.27), channel_id=1, source_target_pairs={{0,4},{4,8},{8,12},{12,0},{1,5},{5,9},{9,13},{13,1},{2,6},{6,10},{... | collective-permute-start | bytes 786440 | tf_op jit(solution)/shard_map/ppermute | solution.py:345
  33.1 13.9 %collective-permute-start.5 = (bf16[8,128,128]{2,1,0:T(8,128)(2,1)}, bf16[8,128,128]{2,1,0:T(8,128)(2,1)S(1)}, u32[]{:S(2)}, u32[]{:S(2)}) collective-permute-start(bf16[8,128,128]{2,1,0:T(8,128)(2,1)} %get-tuple-element.28), channel_id=1, source_target_pairs={{0,8},{4,12},{8,0},{12,4},{1,9},{5,13},{9,1},{13,5},{2,10},{6,14},... | collective-permute-start | bytes 786440 | tf_op jit(solution)/shard_map/ppermute | solution.py:345
  34.9 13.3 %collective-permute-start.6 = (bf16[8,128,128]{2,1,0:T(8,128)(2,1)}, bf16[8,128,128]{2,1,0:T(8,128)(2,1)S(1)}, u32[]{:S(2)}, u32[]{:S(2)}) collective-permute-start(bf16[8,128,128]{2,1,0:T(8,128)(2,1)} %get-tuple-element.29), channel_id=1, source_target_pairs={{0,12},{4,0},{8,4},{12,8},{1,13},{5,1},{9,5},{13,9},{2,14},{6,2},{... | collective-permute-start | bytes 786440 | tf_op jit(solution)/shard_map/ppermute | solution.py:345
  37.3 17.3 %collective-permute-start.9 = (bf16[24,128,128]{2,1,0:T(8,128)(2,1)S(1)}, bf16[24,128,128]{2,1,0:T(8,128)(2,1)S(1)}, u32[]{:S(2)}, u32[]{:S(2)}) collective-permute-start(bf16[24,128,128]{2,1,0:T(8,128)(2,1)S(1)} %broadcast_select_fusion), channel_id=1, source_target_pairs={{0,32},{32,64},{64,96},{96,0},{16,112},{48,16},{80,48},{112,80},{1... | collective-permute-start | bytes 2359304 | tf_op jit(solution)/shard_map/ppermute | solution.py:368
  43.6 18.4 %collective-permute-start.10 = (bf16[8,128,128]{2,1,0:T(8,128)(2,1)}, bf16[8,128,128]{2,1,0:T(8,128)(2,1)S(1)}, u32[]{:S(2)}, u32[]{:S(2)}) collective-permute-start(bf16[8,128,128]{2,1,0:T(8,128)(2,1)} %get-tuple-element.35), channel_id=1, source_target_pairs={{0,4},{4,8},{8,12},{12,0},{1,5},{5,9},{9,13},{13,1},{2,6},{6,10},{... | collective-permute-start | bytes 786440 | tf_op jit(solution)/shard_map/ppermute | solution.py:345
  44.6 17.4 %collective-permute-start.11 = (bf16[8,128,128]{2,1,0:T(8,128)(2,1)}, bf16[8,128,128]{2,1,0:T(8,128)(2,1)S(1)}, u32[]{:S(2)}, u32[]{:S(2)}) collective-permute-start(bf16[8,128,128]{2,1,0:T(8,128)(2,1)} %get-tuple-element.36), channel_id=1, source_target_pairs={{0,8},{4,12},{8,0},{12,4},{1,9},{5,13},{9,1},{13,5},{2,10},{6,14},... | collective-permute-start | bytes 786440 | tf_op jit(solution)/shard_map/ppermute | solution.py:345
  47.0 12.1 %copy-start.1 = (bf16[8,128,128]{2,1,0:T(8,128)(2,1)S(1)}, bf16[8,128,128]{2,1,0:T(8,128)(2,1)}, u32[]{:S(2)}) copy-start(bf16[8,128,128]{2,1,0:T(8,128)(2,1)} %get-tuple-element.26.refs_0_) | copy-start | bytes 786436
  47.0 12.1 %copy-start.2 = (bf16[8,128,128]{2,1,0:T(8,128)(2,1)S(1)}, bf16[8,128,128]{2,1,0:T(8,128)(2,1)}, u32[]{:S(2)}) copy-start(bf16[8,128,128]{2,1,0:T(8,128)(2,1)} %get-tuple-element.34.refs_10_.refs_4_) | copy-start | bytes 786436
  47.0 15.0 %collective-permute-start.12 = (bf16[8,128,128]{2,1,0:T(8,128)(2,1)}, bf16[8,128,128]{2,1,0:T(8,128)(2,1)S(1)}, u32[]{:S(2)}, u32[]{:S(2)}) collective-permute-start(bf16[8,128,128]{2,1,0:T(8,128)(2,1)} %get-tuple-element.37), channel_id=1, source_target_pairs={{0,12},{4,0},{8,4},{12,8},{1,13},{5,1},{9,5},{13,9},{2,14},{6,2},{... | collective-permute-start | bytes 786440 | tf_op jit(solution)/shard_map/ppermute | solution.py:345
  48.2 10.4 %collective-permute-start.13 = (bf16[24,128,128]{2,1,0:T(8,128)(2,1)S(1)}, bf16[24,128,128]{2,1,0:T(8,128)(2,1)S(1)}, u32[]{:S(2)}, u32[]{:S(2)}) collective-permute-start(bf16[24,128,128]{2,1,0:T(8,128)(2,1)S(1)} %collective-permute-done.7.refs_5_.refs_9_), channel_id=1, source_target_pairs={{0,16},{16,0},{1,17},{17,1},{2,18},{18,2},{3,19},{19,3},{4,20},{20... | collective-permute-start | bytes 2359304 | tf_op jit(solution)/shard_map/ppermute | solution.py:376
  54.6 4.5 %collective-permute-start.14 = (bf16[24,128,128]{2,1,0:T(8,128)(2,1)S(1)}, bf16[24,128,128]{2,1,0:T(8,128)(2,1)S(1)}, u32[]{:S(2)}, u32[]{:S(2)}) collective-permute-start(bf16[24,128,128]{2,1,0:T(8,128)(2,1)S(1)} %collective-permute-done.8.refs_6_.refs_10_), channel_id=1, source_target_pairs={{0,16},{16,0},{1,17},{17,1},{2,18},{18,2},{3,19},{19,3},{4,20},{20... | collective-permute-start | bytes 2359304 | tf_op jit(solution)/shard_map/ppermute | solution.py:376
  58.6 3.4 %collective-permute-start.15 = (bf16[24,128,128]{2,1,0:T(8,128)(2,1)S(1)}, bf16[24,128,128]{2,1,0:T(8,128)(2,1)S(1)}, u32[]{:S(2)}, u32[]{:S(2)}) collective-permute-start(bf16[24,128,128]{2,1,0:T(8,128)(2,1)S(1)} %collective-permute-done.9.refs_11_), channel_id=1, source_target_pairs={{0,16},{16,0},{1,17},{17,1},{2,18},{18,2},{3,19},{19,3},{4,20},{20... | collective-permute-start | bytes 2359304 | tf_op jit(solution)/shard_map/ppermute | solution.py:381

commit v6 on v5

--- a/solution.py
+++ b/solution.py
@@ -368,14 +368,14 @@
     far = lax.ppermute(jnp.where(lax.axis_index("core") == 0, below, above), ("z", "core"), FAR)
     plan = make_plan(pos, rows_z, req, diag)
     sent = pltpu.HBM((USED, TILE, TILE), jnp.bfloat16)
-    after = (token(Y1_COST, left1[1]), token(DIAG_COST, diag), lists)
+    after = (lists, token(DIAG_COST, diag), lists)
     send2 = select(select_other_kernel, (sent,) * 4, lists, (outer, diag), after)
     left2 = exchange(send2)
     mine = (own, below, above)
     kept, *later = lax.optimization_barrier((send2[0], below, above))
     theirs = (their_own, *(lax.ppermute(block, "core", SWAP) for block in later))
     left2 = (kept, *left2[1:])
-    early, done = multiply_own(plan, left1, mine, theirs, (kept, token(Y1_LATE_COST, *left1[2:])))
+    early, done = multiply_own(plan, left1, mine, theirs, (kept, token(Y1_LATE_COST, *left1[1:])))
     kept2, far = lax.optimization_barrier((kept, far))
     left2 = (kept2, *left2[1:])
     mine, theirs = (*mine, far), (*theirs, lax.ppermute(far, "core", SWAP))

time: 81.1 us -> 78.8 us (0.972)
  starting transfers between devices: 36.1 us -> 33.7 us
    ppermute x1, waiting for transfers between devices: 0.01 us -> 2.06 us  [on_device(): diag = lax.ppermute(outer, 'x', INNER)]
    ppermute x6, waiting for transfers between devices: 2.07 us -> 0.02 us  [exchange(): lax.ppermute(part, 'y', way)]
    ppermute x2, starting transfers between devices: 6.49 us -> 4.51 us  [on_device(): lax.ppermute(block, 'core', SWAP)]
where the time goes in v6:
time: 78.8 us; the launch traced here: 78.4 us
  starting transfers between devices  33.7 us (43%)
  Pallas kernels  21.3 us (27%)
  waiting for transfers between devices  11.6 us (15%)
  blocking collectives  9.48 us (12%)
  local copies, waits for them, and re-layouts  2.02 us (3%)
    all_to_all x1, blocking collectives, on_device(): totals = lax.all_to_all(totals, ('z', 'core'), 0, 0)  9.48 us
    ppermute x6, starting transfers between devices, exchange(): lax.ppermute(part, 'y', way)  9 us
    pallas_call x1, Pallas kernels, multiply_other(): pl.pallas_call(other_kernel, out_shape=(pltpu.VMEM(MERGED, jnp.float32),...  5.64 us
    all_to_all x1, starting transfers between devices, on_device(): lax.all_to_all(jnp.broadcast_to(wide_rows, (PANELS, 1, TILE)), ('z', 'cor...  5.53 us
    all_to_all x1, starting transfers between devices, on_device(): req = lax.all_to_all(asks, ('y', 'x'), 0, 0)  5.44 us
    all_to_all x1, waiting for transfers between devices, on_device(): req = lax.all_to_all(asks, ('y', 'x'), 0, 0)  4.96 us
    all_to_all x1, waiting for transfers between devices, on_device(): lax.all_to_all(jnp.broadcast_to(wide_rows, (PANELS, 1, TILE)), ('z', 'cor...  4.52 us
    ppermute x2, starting transfers between devices, on_device(): lax.ppermute(block, 'core', SWAP)  4.51 us
  transfers between devices with their start and end apart: 18, of which 3 were waited for; matrix products, arithmetic and copies ran while one was open for 3% of the time, Pallas kernels for 15%

profile of v6, /device:TPU:1, one launch (start us, length us, event | category | flops | bytes accessed | tf_op | source)
XLA Modules:
  0.0 78.4 jit_solution(653000047070966179)
XLA Ops:
  0.0 3.3 %collective-permute-start = (bf16[24,128,128]{2,1,0:T(8,128)(2,1)}, bf16[24,128,128]{2,1,0:T(8,128)(2,1)}, u32[]{:S(2)}, u32[]{:S(2)}) collective-permute-start(bf16[24,128,128]{2,1,0:T(8,128)(2,1)} %bitcast.12), channel_id=1, source_target_pairs={{0,3},{3,0},{1,2},{2,1},{4,7},{7,4},{5,6},{6,5},{8,11},{11,8},{9,1... | collective-permute-start | bytes 2359304 | tf_op jit(solution)/shard_map/ppermute | solution.py:352
  3.3 1.0 %collective-permute-start.3 = (bf16[24,128,128]{2,1,0:T(8,128)(2,1)}, bf16[24,128,128]{2,1,0:T(8,128)(2,1)}, u32[]{:S(2)}, u32[]{:S(2)}) collective-permute-start(bf16[24,128,128]{2,1,0:T(8,128)(2,1)} %bitcast.13), channel_id=1, source_target_pairs={{0,16},{16,0},{1,17},{17,1},{2,18},{18,2},{3,19},{19,3},{4,20},{20... | collective-permute-start | bytes 2359304 | tf_op jit(solution)/shard_map/ppermute | solution.py:362
  4.3 0.8 %pad_bitcast_fusion = (s32[128]{0:T(128)S(1)}, s32[128]{0:T(128)S(1)}) fusion(s32[1,24]{1,0:T(1,128)} %param.3), kind=kLoop, calls=%fused_computation.3 | loop fusion | bytes 1120 | tf_op jit(solution)/shard_map/add | solution.py:356
  5.7 5.5 %all-to-all-start = ((s32[8,1,128]{2,1,0:T(1,128)}), s32[8,1,128]{2,1,0:T(1,128)S(1)}, u32[]{:S(2)}, u32[]{:S(2)}) async-start(s32[8,1,128]{2,1,0:T(1,128)} %broadcast_in_dim.12), calls=%async_computation | async-start | bytes 8192 | tf_op jit(solution)/shard_map/all_to_all | solution.py:354
  11.3 4.5 %all-to-all-done.rows = s32[8,1,128]{2,1,0:T(1,128)S(1)} async-done(((s32[8,1,128]{2,1,0:T(1,128)}), s32[8,1,128]{2,1,0:T(1,128)S(1)}, u32[]{:S(2)}, u32[]{:S(2)}) %all-to-all-start) | async-done | bytes 4128 | tf_op jit(solution)/shard_map/all_to_all | solution.py:354
  17.9 5.4 %all-to-all-start.1 = ((s32[16,2,128]{2,1,0:T(2,128)}), s32[16,2,128]{2,1,0:T(2,128)S(1)}, u32[]{:S(2)}, u32[]{:S(2)}) async-start(s32[16,2,128]{2,1,0:T(2,128)} %bitcast.8), calls=%async_computation.1 | async-start | bytes 32768 | tf_op jit(solution)/shard_map/all_to_all | solution.py:357
  23.3 1.4 %collective-permute-start.1 = (bf16[24,128,128]{2,1,0:T(8,128)(2,1)}, bf16[24,128,128]{2,1,0:T(8,128)(2,1)S(1)}, u32[]{:S(2)}, u32[]{:S(2)}) collective-permute-start(bf16[24,128,128]{2,1,0:T(8,128)(2,1)} %collective-permute-done.refs_1_.outer), channel_id=1, source_target_pairs={{0,1},{1,0},{2,3},{3,2},{4,5},{5,4},{6,7},{7,6},{8,9},{9,8},{10,11... | collective-permute-start | bytes 2359304 | tf_op jit(solution)/shard_map/ppermute | solution.py:366
  24.8 5.0 %all-to-all-done.1.req = s32[16,2,128]{2,1,0:T(2,128)S(1)} async-done(((s32[16,2,128]{2,1,0:T(2,128)}), s32[16,2,128]{2,1,0:T(2,128)S(1)}, u32[]{:S(2)}, u32[]{:S(2)}) %all-to-all-start.1) | async-done | bytes 16416 | tf_op jit(solution)/shard_map/all_to_all | solution.py:357
  29.8 3.1 %shard_map.30 = (bf16[8,128,128]{2,1,0:T(8,128)(2,1)}, bf16[8,128,128]{2,1,0:T(8,128)(2,1)}, bf16[8,128,128]{2,1,0:T(8,128)(2,1)}, bf16[8,128,128]{2,1,0:T(8,128)(2,1)}, s32[128]{0:T(128)S(4)}) custom-call(s32[4]{0:T(128)S(1)} %pad_add_fusion.pos, s32[16,2,128]{2,1,0:T(2,128)S(1)} %all-to-all-done.1.req, bf16[24,128,128]{2,1,0:T(8,128)(2,1)S(1)} %bitcast.17, ...), custom_call_target="tpu_custom_call" | custom-call | bytes 2097152 | tf_op jit(solution)/shard_map/pallas_call | solution.py:120
  33.1 1.8 %collective-permute-start.5 = (bf16[8,128,128]{2,1,0:T(8,128)(2,1)}, bf16[8,128,128]{2,1,0:T(8,128)(2,1)S(1)}, u32[]{:S(2)}, u32[]{:S(2)}) collective-permute-start(bf16[8,128,128]{2,1,0:T(8,128)(2,1)} %get-tuple-element.28), channel_id=1, source_target_pairs={{0,8},{4,12},{8,0},{12,4},{1,9},{5,13},{9,1},{13,5},{2,10},{6,14},... | collective-permute-start | bytes 786440 | tf_op jit(solution)/shard_map/ppermute | solution.py:345
  34.9 2.3 %collective-permute-start.6 = (bf16[8,128,128]{2,1,0:T(8,128)(2,1)}, bf16[8,128,128]{2,1,0:T(8,128)(2,1)S(1)}, u32[]{:S(2)}, u32[]{:S(2)}) collective-permute-start(bf16[8,128,128]{2,1,0:T(8,128)(2,1)} %get-tuple-element.29), channel_id=1, source_target_pairs={{0,12},{4,0},{8,4},{12,8},{1,13},{5,1},{9,5},{13,9},{2,14},{6,2},{... | collective-permute-start | bytes 786440 | tf_op jit(solution)/shard_map/ppermute | solution.py:345
  37.3 2.0 %collective-permute-start.9 = (bf16[24,128,128]{2,1,0:T(8,128)(2,1)S(1)}, bf16[24,128,128]{2,1,0:T(8,128)(2,1)S(1)}, u32[]{:S(2)}, u32[]{:S(2)}) collective-permute-start(bf16[24,128,128]{2,1,0:T(8,128)(2,1)S(1)} %broadcast_select_fusion), channel_id=1, source_target_pairs={{0,32},{32,64},{64,96},{96,0},{16,112},{48,16},{80,48},{112,80},{1... | collective-permute-start | bytes 2359304 | tf_op jit(solution)/shard_map/ppermute | solution.py:368
  39.3 2.1 %collective-permute-done.1._.refs_0_.diag = bf16[24,128,128]{2,1,0:T(8,128)(2,1)S(1)} collective-permute-done((bf16[24,128,128]{2,1,0:T(8,128)(2,1)}, bf16[24,128,128]{2,1,0:T(8,128)(2,1)S(1)}, u32[]{:S(2)}, u32[]{:S(2)}) %collective-permute-start.1) | collective-permute-done | bytes 786464 | tf_op jit(solution)/shard_map/ppermute | solution.py:366
  41.3 2.2 %shard_map.32 = (bf16[8,128,128]{2,1,0:T(8,128)(2,1)}, bf16[8,128,128]{2,1,0:T(8,128)(2,1)}, bf16[8,128,128]{2,1,0:T(8,128)(2,1)}, bf16[8,128,128]{2,1,0:T(8,128)(2,1)}) custom-call(s32[128]{0:T(128)S(4)} %get-tuple-element.30.lists._.___, bf16[24,128,128]{2,1,0:T(8,128)(2,1)} %collective-permute-done.refs_1_.outer, ...), custom_call_target="tpu_custom_call" | custom-call | bytes 2097152 | tf_op jit(solution)/shard_map/pallas_call | solution.py:131
  43.6 1.1 %collective-permute-start.10 = (bf16[8,128,128]{2,1,0:T(8,128)(2,1)}, bf16[8,128,128]{2,1,0:T(8,128)(2,1)S(1)}, u32[]{:S(2)}, u32[]{:S(2)}) collective-permute-start(bf16[8,128,128]{2,1,0:T(8,128)(2,1)} %get-tuple-element.35), channel_id=1, source_target_pairs={{0,4},{4,8},{8,12},{12,0},{1,5},{5,9},{9,13},{13,1},{2,6},{6,10},{... | collective-permute-start | bytes 786440 | tf_op jit(solution)/shard_map/ppermute | solution.py:345
  44.6 2.4 %collective-permute-start.11 = (bf16[8,128,128]{2,1,0:T(8,128)(2,1)}, bf16[8,128,128]{2,1,0:T(8,128)(2,1)S(1)}, u32[]{:S(2)}, u32[]{:S(2)}) collective-permute-start(bf16[8,128,128]{2,1,0:T(8,128)(2,1)} %get-tuple-element.36), channel_id=1, source_target_pairs={{0,8},{4,12},{8,0},{12,4},{1,9},{5,13},{9,1},{13,5},{2,10},{6,14},... | collective-permute-start | bytes 786440 | tf_op jit(solution)/shard_map/ppermute | solution.py:345
  47.0 1.2 %collective-permute-start.12 = (bf16[8,128,128]{2,1,0:T(8,128)(2,1)}, bf16[8,128,128]{2,1,0:T(8,128)(2,1)S(1)}, u32[]{:S(2)}, u32[]{:S(2)}) collective-permute-start(bf16[8,128,128]{2,1,0:T(8,128)(2,1)} %get-tuple-element.37), channel_id=1, source_target_pairs={{0,12},{4,0},{8,4},{12,8},{1,13},{5,1},{9,5},{13,9},{2,14},{6,2},{... | collective-permute-start | bytes 786440 | tf_op jit(solution)/shard_map/ppermute | solution.py:345
  48.2 3.5 %collective-permute-start.13 = (bf16[24,128,128]{2,1,0:T(8,128)(2,1)S(1)}, bf16[24,128,128]{2,1,0:T(8,128)(2,1)S(1)}, u32[]{:S(2)}, u32[]{:S(2)}) collective-permute-start(bf16[24,128,128]{2,1,0:T(8,128)(2,1)S(1)} %collective-permute-done.7.refs_5_.refs_9_), channel_id=1, source_target_pairs={{0,16},{16,0},{1,17},{17,1},{2,18},{18,2},{3,19},{19,3},{4,20},{20... | collective-permute-start | bytes 2359304 | tf_op jit(solution)/shard_map/ppermute | solution.py:376
  51.7 1.0 %collective-permute-start.14 = (bf16[24,128,128]{2,1,0:T(8,128)(2,1)S(1)}, bf16[24,128,128]{2,1,0:T(8,128)(2,1)S(1)}, u32[]{:S(2)}, u32[]{:S(2)}) collective-permute-start(bf16[24,128,128]{2,1,0:T(8,128)(2,1)S(1)} %collective-permute-done.8.refs_6_.refs_10_), channel_id=1, source_target_pairs={{0,16},{16,0},{1,17},{17,1},{2,18},{18,2},{3,19},{19,3},{4,20},{20... | collective-permute-start | bytes 2359304 | tf_op jit(solution)/shard_map/ppermute | solution.py:376
  52.7 3.9 %shard_map.28.plan = s32[512]{0:T(512)S(4)} custom-call(s32[4]{0:T(128)S(1)} %pad_add_fusion.pos, s32[8,1,128]{2,1,0:T(1,128)S(1)} %all-to-all-done.rows, s32[16,2,128]{2,1,0:T(2,128)S(1)} %all-to-all-done.1.req, bf16[24,128,128]{2,1,0:T(8,128)(2,1)S(1)} %collective-permute-done.1._.refs_0_.diag), custom_call_target="tpu_custom_call" | custom-call | bytes 33554432 | tf_op jit(solution)/shard_map/pallas_call | solution.py:180
  56.8 2.8 %shard_map.34 = (f32[24,3,128,128]{3,2,1,0:T(8,128)S(1)}, s32[8]{0:T(128)S(4)}) custom-call(s32[512]{0:T(512)S(4)} %shard_map.28.plan, bf16[8,128,128]{2,1,0:T(8,128)(2,1)S(1)} %copy-done.1, bf16[8,128,128]{2,1,0:T(8,128)(2,1)S(1)} %collective-permute-done.4.refs_0_.refs_1_, bf16[8,128,128]{2,1,0:T(8,128)(2,1)S(1)} %collective-permute-done.5.refs_1_.refs_2_, ...), custom_call_target="tpu_custom_call" | custom-call | flops 402653184 | bytes 16777216 | tf_op jit(solution)/shard_map/pallas_call | solution.py:281
  59.7 5.6 %shard_map.36 = (f32[24,8,128,128]{3,2,1,0:T(8,128)S(1)}, f32[8,24,128]{2,1,0:T(8,128)}) custom-call(s32[512]{0:T(512)S(4)} %shard_map.28.plan, bf16[8,128,128]{2,1,0:T(8,128)(2,1)S(1)} %copy-done.1, bf16[8,128,128]{2,1,0:T(8,128)(2,1)S(1)} %collective-permute-done.4.refs_0_.refs_1_, bf16[8,128,128]{2,1,0:T(8,128)(2,1)S(1)} %collective-permute-done.5.refs_1_.refs_2_, ...), custom_call_target="tpu_custom_call" | custom-call | flops 402653184 | bytes 16777216 | tf_op jit(solution)/shard_map/pallas_call | solution.py:293
  65.3 9.5 %all_to_all.15.totals = f32[8,24,128]{2,1,0:T(8,128)S(1)} all-to-all(f32[8,24,128]{2,1,0:T(8,128)} %get-tuple-element.44), channel_id=1, replica_groups=mesh['z'=4,'core'=2,'y'=4,'x'=4] {'z','core'}, dimensions={0} | all-to-all | bytes 196608 | tf_op jit(solution)/shard_map/all_to_all | solution.py:383
  74.8 3.6 %shard_map.37 = bf16[8,24,128,128]{3,2,1,0:T(8,128)(2,1)} custom-call(s32[512]{0:T(512)S(4)} %shard_map.28.plan, f32[24,8,128,128]{3,2,1,0:T(8,128)S(1)} %get-tuple-element.43.merged, f32[8,24,128]{2,1,0:T(8,128)S(1)} %all_to_all.15.totals), custom_call_target="tpu_custom_call" | custom-call | flops 6291456 | bytes 20971520 | tf_op jit(solution)/shard_map/pallas_call | solution.py:329
  (35 shorter events, 3.3 us)
Async XLA Ops:
  0.0 23.3 %collective-permute-start = (bf16[24,128,128]{2,1,0:T(8,128)(2,1)}, bf16[24,128,128]{2,1,0:T(8,128)(2,1)}, u32[]{:S(2)}, u32[]{:S(2)}) collective-permute-start(bf16[24,128,128]{2,1,0:T(8,128)(2,1)} %bitcast.12), channel_id=1, source_target_pairs={{0,3},{3,0},{1,2},{2,1},{4,7},{7,4},{5,6},{6,5},{8,11},{11,8},{9,1... | collective-permute-start | bytes 2359304 | tf_op jit(solution)/shard_map/ppermute | solution.py:352
  3.3 21.5 %collective-permute-start.3 = (bf16[24,128,128]{2,1,0:T(8,128)(2,1)}, bf16[24,128,128]{2,1,0:T(8,128)(2,1)}, u32[]{:S(2)}, u32[]{:S(2)}) collective-permute-start(bf16[24,128,128]{2,1,0:T(8,128)(2,1)} %bitcast.13), channel_id=1, source_target_pairs={{0,16},{16,0},{1,17},{17,1},{2,18},{18,2},{3,19},{19,3},{4,20},{20... | collective-permute-start | bytes 2359304 | tf_op jit(solution)/shard_map/ppermute | solution.py:362
  4.3 20.5 %collective-permute-start.2 = (bf16[24,128,128]{2,1,0:T(8,128)(2,1)}, bf16[24,128,128]{2,1,0:T(8,128)(2,1)}, u32[]{:S(2)}, u32[]{:S(2)}) collective-permute-start(bf16[24,128,128]{2,1,0:T(8,128)(2,1)} %bitcast.14), channel_id=1, source_target_pairs={{0,1},{1,0},{2,3},{3,2},{4,5},{5,4},{6,7},{7,6},{8,9},{9,8},{10,11... | collective-permute-start | bytes 2359304 | tf_op jit(solution)/shard_map/ppermute | solution.py:351
  5.7 10.1 %all-to-all-start = ((s32[8,1,128]{2,1,0:T(1,128)}), s32[8,1,128]{2,1,0:T(1,128)S(1)}, u32[]{:S(2)}, u32[]{:S(2)}) async-start(s32[8,1,128]{2,1,0:T(1,128)} %broadcast_in_dim.12), calls=%async_computation | async-start | bytes 8192 | tf_op jit(solution)/shard_map/all_to_all | solution.py:354
  15.8 19.1 %collective-permute-start.8 = (bf16[24,128,128]{2,1,0:T(8,128)(2,1)}, bf16[24,128,128]{2,1,0:T(8,128)(2,1)S(1)}, u32[]{:S(2)}, u32[]{:S(2)}) collective-permute-start(bf16[24,128,128]{2,1,0:T(8,128)(2,1)} %bitcast.15), channel_id=1, source_target_pairs={{0,96},{32,0},{64,32},{96,64},{1,97},{33,1},{65,33},{97,65},{2,98}... | collective-permute-start | bytes 2359304 | tf_op jit(solution)/shard_map/ppermute | solution.py:360
  16.6 20.7 %collective-permute-start.7 = (bf16[24,128,128]{2,1,0:T(8,128)(2,1)}, bf16[24,128,128]{2,1,0:T(8,128)(2,1)S(1)}, u32[]{:S(2)}, u32[]{:S(2)}) collective-permute-start(bf16[24,128,128]{2,1,0:T(8,128)(2,1)} %bitcast.16), channel_id=1, source_target_pairs={{0,32},{32,64},{64,96},{96,0},{1,33},{33,65},{65,97},{97,1},{2,34}... | collective-permute-start | bytes 2359304 | tf_op jit(solution)/shard_map/ppermute | solution.py:359
  17.9 11.9 %all-to-all-start.1 = ((s32[16,2,128]{2,1,0:T(2,128)}), s32[16,2,128]{2,1,0:T(2,128)S(1)}, u32[]{:S(2)}, u32[]{:S(2)}) async-start(s32[16,2,128]{2,1,0:T(2,128)} %bitcast.8), calls=%async_computation.1 | async-start | bytes 32768 | tf_op jit(solution)/shard_map/all_to_all | solution.py:357
  23.3 6.4 %copy-start = (bf16[1,24,128,128]{3,2,1,0:T(8,128)(2,1)S(1)}, bf16[1,24,128,128]{3,2,1,0:T(8,128)(2,1)}, u32[]{:S(2)}) copy-start(bf16[1,24,128,128]{3,2,1,0:T(8,128)(2,1)} %param.2) | copy-start | bytes 2359300
  23.3 18.0 %collective-permute-start.1 = (bf16[24,128,128]{2,1,0:T(8,128)(2,1)}, bf16[24,128,128]{2,1,0:T(8,128)(2,1)S(1)}, u32[]{:S(2)}, u32[]{:S(2)}) collective-permute-start(bf16[24,128,128]{2,1,0:T(8,128)(2,1)} %collective-permute-done.refs_1_.outer), channel_id=1, source_target_pairs={{0,1},{1,0},{2,3},{3,2},{4,5},{5,4},{6,7},{7,6},{8,9},{9,8},{10,11... | collective-permute-start | bytes 2359304 | tf_op jit(solution)/shard_map/ppermute | solution.py:366
  32.9 11.8 %collective-permute-start.4 = (bf16[8,128,128]{2,1,0:T(8,128)(2,1)}, bf16[8,128,128]{2,1,0:T(8,128)(2,1)S(1)}, u32[]{:S(2)}, u32[]{:S(2)}) collective-permute-start(bf16[8,128,128]{2,1,0:T(8,128)(2,1)} %get-tuple-element.27), channel_id=1, source_target_pairs={{0,4},{4,8},{8,12},{12,0},{1,5},{5,9},{9,13},{13,1},{2,6},{6,10},{... | collective-permute-start | bytes 786440 | tf_op jit(solution)/shard_map/ppermute | solution.py:345
  33.1 13.9 %collective-permute-start.5 = (bf16[8,128,128]{2,1,0:T(8,128)(2,1)}, bf16[8,128,128]{2,1,0:T(8,128)(2,1)S(1)}, u32[]{:S(2)}, u32[]{:S(2)}) collective-permute-start(bf16[8,128,128]{2,1,0:T(8,128)(2,1)} %get-tuple-element.28), channel_id=1, source_target_pairs={{0,8},{4,12},{8,0},{12,4},{1,9},{5,13},{9,1},{13,5},{2,10},{6,14},... | collective-permute-start | bytes 786440 | tf_op jit(solution)/shard_map/ppermute | solution.py:345
  34.9 13.3 %collective-permute-start.6 = (bf16[8,128,128]{2,1,0:T(8,128)(2,1)}, bf16[8,128,128]{2,1,0:T(8,128)(2,1)S(1)}, u32[]{:S(2)}, u32[]{:S(2)}) collective-permute-start(bf16[8,128,128]{2,1,0:T(8,128)(2,1)} %get-tuple-element.29), channel_id=1, source_target_pairs={{0,12},{4,0},{8,4},{12,8},{1,13},{5,1},{9,5},{13,9},{2,14},{6,2},{... | collective-permute-start | bytes 786440 | tf_op jit(solution)/shard_map/ppermute | solution.py:345
  37.3 14.4 %collective-permute-start.9 = (bf16[24,128,128]{2,1,0:T(8,128)(2,1)S(1)}, bf16[24,128,128]{2,1,0:T(8,128)(2,1)S(1)}, u32[]{:S(2)}, u32[]{:S(2)}) collective-permute-start(bf16[24,128,128]{2,1,0:T(8,128)(2,1)S(1)} %broadcast_select_fusion), channel_id=1, source_target_pairs={{0,32},{32,64},{64,96},{96,0},{16,112},{48,16},{80,48},{112,80},{1... | collective-permute-start | bytes 2359304 | tf_op jit(solution)/shard_map/ppermute | solution.py:368
  43.6 16.0 %collective-permute-start.10 = (bf16[8,128,128]{2,1,0:T(8,128)(2,1)}, bf16[8,128,128]{2,1,0:T(8,128)(2,1)S(1)}, u32[]{:S(2)}, u32[]{:S(2)}) collective-permute-start(bf16[8,128,128]{2,1,0:T(8,128)(2,1)} %get-tuple-element.35), channel_id=1, source_target_pairs={{0,4},{4,8},{8,12},{12,0},{1,5},{5,9},{9,13},{13,1},{2,6},{6,10},{... | collective-permute-start | bytes 786440 | tf_op jit(solution)/shard_map/ppermute | solution.py:345
  44.6 15.0 %collective-permute-start.11 = (bf16[8,128,128]{2,1,0:T(8,128)(2,1)}, bf16[8,128,128]{2,1,0:T(8,128)(2,1)S(1)}, u32[]{:S(2)}, u32[]{:S(2)}) collective-permute-start(bf16[8,128,128]{2,1,0:T(8,128)(2,1)} %get-tuple-element.36), channel_id=1, source_target_pairs={{0,8},{4,12},{8,0},{12,4},{1,9},{5,13},{9,1},{13,5},{2,10},{6,14},... | collective-permute-start | bytes 786440 | tf_op jit(solution)/shard_map/ppermute | solution.py:345
  47.0 9.7 %copy-start.1 = (bf16[8,128,128]{2,1,0:T(8,128)(2,1)S(1)}, bf16[8,128,128]{2,1,0:T(8,128)(2,1)}, u32[]{:S(2)}) copy-start(bf16[8,128,128]{2,1,0:T(8,128)(2,1)} %get-tuple-element.26.refs_0_) | copy-start | bytes 786436
  47.0 9.7 %copy-start.2 = (bf16[8,128,128]{2,1,0:T(8,128)(2,1)S(1)}, bf16[8,128,128]{2,1,0:T(8,128)(2,1)}, u32[]{:S(2)}) copy-start(bf16[8,128,128]{2,1,0:T(8,128)(2,1)} %get-tuple-element.34.refs_10_.refs_4_) | copy-start | bytes 786436
  47.0 12.6 %collective-permute-start.12 = (bf16[8,128,128]{2,1,0:T(8,128)(2,1)}, bf16[8,128,128]{2,1,0:T(8,128)(2,1)S(1)}, u32[]{:S(2)}, u32[]{:S(2)}) collective-permute-start(bf16[8,128,128]{2,1,0:T(8,128)(2,1)} %get-tuple-element.37), channel_id=1, source_target_pairs={{0,12},{4,0},{8,4},{12,8},{1,13},{5,1},{9,5},{13,9},{2,14},{6,2},{... | collective-permute-start | bytes 786440 | tf_op jit(solution)/shard_map/ppermute | solution.py:345
  48.2 8.4 %collective-permute-start.13 = (bf16[24,128,128]{2,1,0:T(8,128)(2,1)S(1)}, bf16[24,128,128]{2,1,0:T(8,128)(2,1)S(1)}, u32[]{:S(2)}, u32[]{:S(2)}) collective-permute-start(bf16[24,128,128]{2,1,0:T(8,128)(2,1)S(1)} %collective-permute-done.7.refs_5_.refs_9_), channel_id=1, source_target_pairs={{0,16},{16,0},{1,17},{17,1},{2,18},{18,2},{3,19},{19,3},{4,20},{20... | collective-permute-start | bytes 2359304 | tf_op jit(solution)/shard_map/ppermute | solution.py:376
  51.7 5.0 %collective-permute-start.14 = (bf16[24,128,128]{2,1,0:T(8,128)(2,1)S(1)}, bf16[24,128,128]{2,1,0:T(8,128)(2,1)S(1)}, u32[]{:S(2)}, u32[]{:S(2)}) collective-permute-start(bf16[24,128,128]{2,1,0:T(8,128)(2,1)S(1)} %collective-permute-done.8.refs_6_.refs_10_), channel_id=1, source_target_pairs={{0,16},{16,0},{1,17},{17,1},{2,18},{18,2},{3,19},{19,3},{4,20},{20... | collective-permute-start | bytes 2359304 | tf_op jit(solution)/shard_map/ppermute | solution.py:376
  56.7 3.0 %collective-permute-start.15 = (bf16[24,128,128]{2,1,0:T(8,128)(2,1)S(1)}, bf16[24,128,128]{2,1,0:T(8,128)(2,1)S(1)}, u32[]{:S(2)}, u32[]{:S(2)}) collective-permute-start(bf16[24,128,128]{2,1,0:T(8,128)(2,1)S(1)} %collective-permute-done.9.refs_11_), channel_id=1, source_target_pairs={{0,16},{16,0},{1,17},{17,1},{2,18},{18,2},{3,19},{19,3},{4,20},{20... | collective-permute-start | bytes 2359304 | tf_op jit(solution)/shard_map/ppermute | solution.py:381

commit v7 on v6

--- a/solution.py
+++ b/solution.py
@@ -66,6 +66,25 @@
     )(*arrays)
 
 
+def bring_kernel(source, _, out, flag, sem):
+    copy = pltpu.make_async_copy(source, out, sem)
+    copy.start()
+    copy.wait()
+    flag[0] = jnp.int32(0)
+
+
+def bring(block, after):
+    return pl.pallas_call(
+        bring_kernel,
+        out_shape=(pltpu.VMEM(block.shape, block.dtype), pltpu.SMEM((8,), jnp.int32)),
+        in_specs=[ANY, ANY],
+        out_specs=(VMEM, SMEM),
+        scratch_shapes=[pltpu.SemaphoreType.DMA],
+        compiler_params=pltpu.CompilerParams(vmem_limit_bytes=2 << 20),
+        cost_estimate=pl.CostEstimate(flops=0, bytes_accessed=2 << 20, transcendentals=0),
+    )(block, after)
+
+
 def bit(mask, v):
     return lax.shift_right_logical(mask, jnp.int32(v)) & 1
 
@@ -368,7 +387,8 @@
     far = lax.ppermute(jnp.where(lax.axis_index("core") == 0, below, above), ("z", "core"), FAR)
     plan = make_plan(pos, rows_z, req, diag)
     sent = pltpu.HBM((USED, TILE, TILE), jnp.bfloat16)
-    after = (lists, token(DIAG_COST, diag), lists)
+    their_own, brought = bring(their_own, send1[0])
+    after = (brought, token(DIAG_COST, diag), lists)
     send2 = select(select_other_kernel, (sent,) * 4, lists, (outer, diag), after)
     left2 = exchange(send2)
     mine = (own, below, above)

time: 78.8 us -> 78 us (0.990)
  Pallas kernels: 21.3 us -> 20.1 us
  blocking collectives: 9.48 us -> 8.38 us
  starting transfers between devices: 33.7 us -> 34.7 us
  local copies, waits for them, and re-layouts: 2.02 us -> 2.97 us
    ppermute x2, starting transfers between devices: 4.51 us -> 6.63 us  [on_device(): lax.ppermute(block, 'core', SWAP)]
    ppermute x6, starting transfers between devices: 9 us -> 7.67 us  [exchange(): lax.ppermute(part, 'y', way)]
    pallas_call x1, Pallas kernels: 5.64 us -> 4.45 us  [multiply_other(): pl.pallas_call(other_kernel, out_shape=(pltpu.VMEM(MERGED, jnp.float32),...]
    pallas_call x0 -> x1, Pallas kernels: none -> 1.14 us  [bring(): pl.pallas_call(bring_kernel, out_shape=(pltpu.VMEM(block.shape, block.dty...]
    pallas_call x1, Pallas kernels: 2.83 us -> 1.7 us  [multiply_own(): pl.pallas_call(own_kernel, out_shape=(pltpu.VMEM(EARLY, jnp.float32), plt...]
    all_to_all x1, blocking collectives: 9.48 us -> 8.38 us  [on_device(): totals = lax.all_to_all(totals, ('z', 'core'), 0, 0)]
    ppermute x1, waiting for transfers between devices: 2.06 us -> 1.1 us  [on_device(): diag = lax.ppermute(outer, 'x', INNER)]
    unnamed x6 -> x8, local copies, waits for them, and re-layouts: 0.01 us -> 0.96 us
  transfers between devices with their start and end apart: 18 -> 18, of which waited for: 3 -> 4; matrix products, arithmetic and copies ran while one was open for 3% -> 3% of each run, Pallas kernels for 15% -> 16%
where the time goes in v7:
time: 78 us; the launch traced here: 77.6 us
  starting transfers between devices  34.7 us (44%)
  Pallas kernels  20.1 us (26%)
  waiting for transfers between devices  11.1 us (14%)
  blocking collectives  8.38 us (11%)
  local copies, waits for them, and re-layouts  2.97 us (4%)
    all_to_all x1, blocking collectives, on_device(): totals = lax.all_to_all(totals, ('z', 'core'), 0, 0)  8.38 us
    ppermute x6, starting transfers between devices, exchange(): lax.ppermute(part, 'y', way)  7.67 us
    ppermute x2, starting transfers between devices, on_device(): lax.ppermute(block, 'core', SWAP)  6.63 us
    all_to_all x1, starting transfers between devices, on_device(): lax.all_to_all(jnp.broadcast_to(wide_rows, (PANELS, 1, TILE)), ('z', 'cor...  5.53 us
    all_to_all x1, starting transfers between devices, on_device(): req = lax.all_to_all(asks, ('y', 'x'), 0, 0)  5.44 us
    all_to_all x1, waiting for transfers between devices, on_device(): req = lax.all_to_all(asks, ('y', 'x'), 0, 0)  4.96 us
    all_to_all x1, waiting for transfers between devices, on_device(): lax.all_to_all(jnp.broadcast_to(wide_rows, (PANELS, 1, TILE)), ('z', 'cor...  4.52 us
    pallas_call x1, Pallas kernels, multiply_other(): pl.pallas_call(other_kernel, out_shape=(pltpu.VMEM(MERGED, jnp.float32),...  4.45 us
  transfers between devices with their start and end apart: 18, of which 4 were waited for; matrix products, arithmetic and copies ran while one was open for 3% of the time, Pallas kernels for 16%

profile of v7, /device:TPU:1, one launch (start us, length us, event | category | flops | bytes accessed | tf_op | source)
XLA Modules:
  0.0 77.6 jit_solution(15558026729187231373)
XLA Ops:
  0.0 3.3 %collective-permute-start = (bf16[24,128,128]{2,1,0:T(8,128)(2,1)}, bf16[24,128,128]{2,1,0:T(8,128)(2,1)}, u32[]{:S(2)}, u32[]{:S(2)}) collective-permute-start(bf16[24,128,128]{2,1,0:T(8,128)(2,1)} %bitcast.12), channel_id=1, source_target_pairs={{0,3},{3,0},{1,2},{2,1},{4,7},{7,4},{5,6},{6,5},{8,11},{11,8},{9,1... | collective-permute-start | bytes 2359304 | tf_op jit(solution)/shard_map/ppermute | solution.py:371
  3.3 1.0 %collective-permute-start.3 = (bf16[24,128,128]{2,1,0:T(8,128)(2,1)}, bf16[24,128,128]{2,1,0:T(8,128)(2,1)}, u32[]{:S(2)}, u32[]{:S(2)}) collective-permute-start(bf16[24,128,128]{2,1,0:T(8,128)(2,1)} %bitcast.13), channel_id=1, source_target_pairs={{0,16},{16,0},{1,17},{17,1},{2,18},{18,2},{3,19},{19,3},{4,20},{20... | collective-permute-start | bytes 2359304 | tf_op jit(solution)/shard_map/ppermute | solution.py:381
  5.7 5.5 %all-to-all-start = ((s32[8,1,128]{2,1,0:T(1,128)}), s32[8,1,128]{2,1,0:T(1,128)S(1)}, u32[]{:S(2)}, u32[]{:S(2)}) async-start(s32[8,1,128]{2,1,0:T(1,128)} %broadcast_in_dim.12), calls=%async_computation | async-start | bytes 8192 | tf_op jit(solution)/shard_map/all_to_all | solution.py:373
  11.3 4.5 %all-to-all-done.rows = s32[8,1,128]{2,1,0:T(1,128)S(1)} async-done(((s32[8,1,128]{2,1,0:T(1,128)}), s32[8,1,128]{2,1,0:T(1,128)S(1)}, u32[]{:S(2)}, u32[]{:S(2)}) %all-to-all-start) | async-done | bytes 4128 | tf_op jit(solution)/shard_map/all_to_all | solution.py:373
  17.9 5.4 %all-to-all-start.1 = ((s32[16,2,128]{2,1,0:T(2,128)}), s32[16,2,128]{2,1,0:T(2,128)S(1)}, u32[]{:S(2)}, u32[]{:S(2)}) async-start(s32[16,2,128]{2,1,0:T(2,128)} %bitcast.8), calls=%async_computation.1 | async-start | bytes 32768 | tf_op jit(solution)/shard_map/all_to_all | solution.py:376
  23.3 1.4 %collective-permute-start.1 = (bf16[24,128,128]{2,1,0:T(8,128)(2,1)}, bf16[24,128,128]{2,1,0:T(8,128)(2,1)S(1)}, u32[]{:S(2)}, u32[]{:S(2)}) collective-permute-start(bf16[24,128,128]{2,1,0:T(8,128)(2,1)} %collective-permute-done.refs_1_.outer), channel_id=1, source_target_pairs={{0,1},{1,0},{2,3},{3,2},{4,5},{5,4},{6,7},{7,6},{8,9},{9,8},{10,11... | collective-permute-start | bytes 2359304 | tf_op jit(solution)/shard_map/ppermute | solution.py:385
  24.8 5.0 %all-to-all-done.1.req = s32[16,2,128]{2,1,0:T(2,128)S(1)} async-done(((s32[16,2,128]{2,1,0:T(2,128)}), s32[16,2,128]{2,1,0:T(2,128)S(1)}, u32[]{:S(2)}, u32[]{:S(2)}) %all-to-all-start.1) | async-done | bytes 16416 | tf_op jit(solution)/shard_map/all_to_all | solution.py:376
  29.8 3.1 %shard_map.30 = (bf16[8,128,128]{2,1,0:T(8,128)(2,1)}, bf16[8,128,128]{2,1,0:T(8,128)(2,1)}, bf16[8,128,128]{2,1,0:T(8,128)(2,1)}, bf16[8,128,128]{2,1,0:T(8,128)(2,1)}, s32[128]{0:T(128)S(4)}) custom-call(s32[4]{0:T(128)S(1)} %pad_add_fusion.pos, s32[16,2,128]{2,1,0:T(2,128)S(1)} %all-to-all-done.1.req, bf16[24,128,128]{2,1,0:T(8,128)(2,1)S(1)} %bitcast.17, ...), custom_call_target="tpu_custom_call" | custom-call | bytes 2097152 | tf_op jit(solution)/shard_map/pallas_call | solution.py:139
  33.1 1.8 %collective-permute-start.5 = (bf16[8,128,128]{2,1,0:T(8,128)(2,1)}, bf16[8,128,128]{2,1,0:T(8,128)(2,1)S(1)}, u32[]{:S(2)}, u32[]{:S(2)}) collective-permute-start(bf16[8,128,128]{2,1,0:T(8,128)(2,1)} %get-tuple-element.30), channel_id=1, source_target_pairs={{0,8},{4,12},{8,0},{12,4},{1,9},{5,13},{9,1},{13,5},{2,10},{6,14},... | collective-permute-start | bytes 786440 | tf_op jit(solution)/shard_map/ppermute | solution.py:364
  35.9 1.1 %shard_map.31 = (bf16[24,128,128]{2,1,0:T(8,128)(2,1)S(1)}, s32[8]{0:T(128)S(4)}) custom-call(bf16[24,128,128]{2,1,0:T(8,128)(2,1)} %collective-permute-done.3.refs_2_.source, bf16[8,128,128]{2,1,0:T(8,128)(2,1)S(1)} %copy-done.1), custom_call_target="tpu_custom_call" | custom-call | bytes 2097152 | tf_op jit(solution)/shard_map/pallas_call | solution.py:77
  37.0 1.0 %collective-permute-start.6 = (bf16[8,128,128]{2,1,0:T(8,128)(2,1)}, bf16[8,128,128]{2,1,0:T(8,128)(2,1)S(1)}, u32[]{:S(2)}, u32[]{:S(2)}) collective-permute-start(bf16[8,128,128]{2,1,0:T(8,128)(2,1)} %get-tuple-element.31), channel_id=1, source_target_pairs={{0,12},{4,0},{8,4},{12,8},{1,13},{5,1},{9,5},{13,9},{2,14},{6,2},{... | collective-permute-start | bytes 786440 | tf_op jit(solution)/shard_map/ppermute | solution.py:364
  38.1 2.2 %collective-permute-start.9 = (bf16[24,128,128]{2,1,0:T(8,128)(2,1)S(1)}, bf16[24,128,128]{2,1,0:T(8,128)(2,1)S(1)}, u32[]{:S(2)}, u32[]{:S(2)}) collective-permute-start(bf16[24,128,128]{2,1,0:T(8,128)(2,1)S(1)} %broadcast_select_fusion), channel_id=1, source_target_pairs={{0,32},{32,64},{64,96},{96,0},{16,112},{48,16},{80,48},{112,80},{1... | collective-permute-start | bytes 2359304 | tf_op jit(solution)/shard_map/ppermute | solution.py:387
  40.2 1.1 %collective-permute-done.1._.refs_0_.diag = bf16[24,128,128]{2,1,0:T(8,128)(2,1)S(1)} collective-permute-done((bf16[24,128,128]{2,1,0:T(8,128)(2,1)}, bf16[24,128,128]{2,1,0:T(8,128)(2,1)S(1)}, u32[]{:S(2)}, u32[]{:S(2)}) %collective-permute-start.1) | collective-permute-done | bytes 786464 | tf_op jit(solution)/shard_map/ppermute | solution.py:385
  41.3 2.3 %shard_map.33 = (bf16[8,128,128]{2,1,0:T(8,128)(2,1)}, bf16[8,128,128]{2,1,0:T(8,128)(2,1)}, bf16[8,128,128]{2,1,0:T(8,128)(2,1)}, bf16[8,128,128]{2,1,0:T(8,128)(2,1)}) custom-call(s32[128]{0:T(128)S(4)} %get-tuple-element.32.lists.___, bf16[24,128,128]{2,1,0:T(8,128)(2,1)} %collective-permute-done.refs_1_.outer, ...), custom_call_target="tpu_custom_call" | custom-call | bytes 2097152 | tf_op jit(solution)/shard_map/pallas_call | solution.py:150
  43.6 1.1 %collective-permute-start.10 = (bf16[8,128,128]{2,1,0:T(8,128)(2,1)}, bf16[8,128,128]{2,1,0:T(8,128)(2,1)S(1)}, u32[]{:S(2)}, u32[]{:S(2)}) collective-permute-start(bf16[8,128,128]{2,1,0:T(8,128)(2,1)} %get-tuple-element.38), channel_id=1, source_target_pairs={{0,4},{4,8},{8,12},{12,0},{1,5},{5,9},{9,13},{13,1},{2,6},{6,10},{... | collective-permute-start | bytes 786440 | tf_op jit(solution)/shard_map/ppermute | solution.py:364
  44.7 2.4 %collective-permute-start.11 = (bf16[8,128,128]{2,1,0:T(8,128)(2,1)}, bf16[8,128,128]{2,1,0:T(8,128)(2,1)S(1)}, u32[]{:S(2)}, u32[]{:S(2)}) collective-permute-start(bf16[8,128,128]{2,1,0:T(8,128)(2,1)} %get-tuple-element.39), channel_id=1, source_target_pairs={{0,8},{4,12},{8,0},{12,4},{1,9},{5,13},{9,1},{13,5},{2,10},{6,14},... | collective-permute-start | bytes 786440 | tf_op jit(solution)/shard_map/ppermute | solution.py:364
  47.1 1.2 %collective-permute-start.12 = (bf16[8,128,128]{2,1,0:T(8,128)(2,1)}, bf16[8,128,128]{2,1,0:T(8,128)(2,1)S(1)}, u32[]{:S(2)}, u32[]{:S(2)}) collective-permute-start(bf16[8,128,128]{2,1,0:T(8,128)(2,1)} %get-tuple-element.40), channel_id=1, source_target_pairs={{0,12},{4,0},{8,4},{12,8},{1,13},{5,1},{9,5},{13,9},{2,14},{6,2},{... | collective-permute-start | bytes 786440 | tf_op jit(solution)/shard_map/ppermute | solution.py:364
  48.3 3.5 %collective-permute-start.13 = (bf16[24,128,128]{2,1,0:T(8,128)(2,1)S(1)}, bf16[24,128,128]{2,1,0:T(8,128)(2,1)S(1)}, u32[]{:S(2)}, u32[]{:S(2)}) collective-permute-start(bf16[24,128,128]{2,1,0:T(8,128)(2,1)S(1)} %collective-permute-done.7.refs_5_.refs_9_), channel_id=1, source_target_pairs={{0,16},{16,0},{1,17},{17,1},{2,18},{18,2},{3,19},{19,3},{4,20},{20... | collective-permute-start | bytes 2359304 | tf_op jit(solution)/shard_map/ppermute | solution.py:396
  51.8 3.1 %collective-permute-start.14 = (bf16[24,128,128]{2,1,0:T(8,128)(2,1)S(1)}, bf16[24,128,128]{2,1,0:T(8,128)(2,1)S(1)}, u32[]{:S(2)}, u32[]{:S(2)}) collective-permute-start(bf16[24,128,128]{2,1,0:T(8,128)(2,1)S(1)} %collective-permute-done.8.refs_6_.refs_10_), channel_id=1, source_target_pairs={{0,16},{16,0},{1,17},{17,1},{2,18},{18,2},{3,19},{19,3},{4,20},{20... | collective-permute-start | bytes 2359304 | tf_op jit(solution)/shard_map/ppermute | solution.py:396
  54.9 3.9 %shard_map.28.plan = s32[512]{0:T(512)S(4)} custom-call(s32[4]{0:T(128)S(1)} %pad_add_fusion.pos, s32[8,1,128]{2,1,0:T(1,128)S(1)} %all-to-all-done.rows, s32[16,2,128]{2,1,0:T(2,128)S(1)} %all-to-all-done.1.req, bf16[24,128,128]{2,1,0:T(8,128)(2,1)S(1)} %collective-permute-done.1._.refs_0_.diag), custom_call_target="tpu_custom_call" | custom-call | bytes 33554432 | tf_op jit(solution)/shard_map/pallas_call | solution.py:199
  58.9 1.7 %shard_map.35 = (f32[24,3,128,128]{3,2,1,0:T(8,128)S(1)}, s32[8]{0:T(128)S(4)}) custom-call(s32[512]{0:T(512)S(4)} %shard_map.28.plan, bf16[8,128,128]{2,1,0:T(8,128)(2,1)S(1)} %copy-done.2, bf16[8,128,128]{2,1,0:T(8,128)(2,1)S(1)} %collective-permute-done.4.refs_0_.refs_1_, bf16[8,128,128]{2,1,0:T(8,128)(2,1)S(1)} %collective-permute-done.5.refs_1_.refs_2_, ...), custom_call_target="tpu_custom_call" | custom-call | flops 402653184 | bytes 16777216 | tf_op jit(solution)/shard_map/pallas_call | solution.py:300
  61.2 4.5 %shard_map.37 = (f32[24,8,128,128]{3,2,1,0:T(8,128)S(1)}, f32[8,24,128]{2,1,0:T(8,128)}) custom-call(s32[512]{0:T(512)S(4)} %shard_map.28.plan, bf16[8,128,128]{2,1,0:T(8,128)(2,1)S(1)} %copy-done.2, bf16[8,128,128]{2,1,0:T(8,128)(2,1)S(1)} %collective-permute-done.4.refs_0_.refs_1_, bf16[8,128,128]{2,1,0:T(8,128)(2,1)S(1)} %collective-permute-done.5.refs_1_.refs_2_, ...), custom_call_target="tpu_custom_call" | custom-call | flops 402653184 | bytes 16777216 | tf_op jit(solution)/shard_map/pallas_call | solution.py:312
  65.6 8.4 %all_to_all.15.totals = f32[8,24,128]{2,1,0:T(8,128)S(1)} all-to-all(f32[8,24,128]{2,1,0:T(8,128)} %get-tuple-element.48), channel_id=1, replica_groups=mesh['z'=4,'core'=2,'y'=4,'x'=4] {'z','core'}, dimensions={0} | all-to-all | bytes 196608 | tf_op jit(solution)/shard_map/all_to_all | solution.py:403
  74.0 3.6 %shard_map.38 = bf16[8,24,128,128]{3,2,1,0:T(8,128)(2,1)} custom-call(s32[512]{0:T(512)S(4)} %shard_map.28.plan, f32[24,8,128,128]{3,2,1,0:T(8,128)S(1)} %get-tuple-element.47.merged, f32[8,24,128]{2,1,0:T(8,128)S(1)} %all_to_all.15.totals), custom_call_target="tpu_custom_call" | custom-call | flops 6291456 | bytes 20971520 | tf_op jit(solution)/shard_map/pallas_call | solution.py:348
  (38 shorter events, 5.5 us)
Async XLA Ops:
  0.0 23.3 %collective-permute-start = (bf16[24,128,128]{2,1,0:T(8,128)(2,1)}, bf16[24,128,128]{2,1,0:T(8,128)(2,1)}, u32[]{:S(2)}, u32[]{:S(2)}) collective-permute-start(bf16[24,128,128]{2,1,0:T(8,128)(2,1)} %bitcast.12), channel_id=1, source_target_pairs={{0,3},{3,0},{1,2},{2,1},{4,7},{7,4},{5,6},{6,5},{8,11},{11,8},{9,1... | collective-permute-start | bytes 2359304 | tf_op jit(solution)/shard_map/ppermute | solution.py:371
  3.3 21.5 %collective-permute-start.3 = (bf16[24,128,128]{2,1,0:T(8,128)(2,1)}, bf16[24,128,128]{2,1,0:T(8,128)(2,1)}, u32[]{:S(2)}, u32[]{:S(2)}) collective-permute-start(bf16[24,128,128]{2,1,0:T(8,128)(2,1)} %bitcast.13), channel_id=1, source_target_pairs={{0,16},{16,0},{1,17},{17,1},{2,18},{18,2},{3,19},{19,3},{4,20},{20... | collective-permute-start | bytes 2359304 | tf_op jit(solution)/shard_map/ppermute | solution.py:381
  4.3 20.5 %collective-permute-start.2 = (bf16[24,128,128]{2,1,0:T(8,128)(2,1)}, bf16[24,128,128]{2,1,0:T(8,128)(2,1)}, u32[]{:S(2)}, u32[]{:S(2)}) collective-permute-start(bf16[24,128,128]{2,1,0:T(8,128)(2,1)} %bitcast.14), channel_id=1, source_target_pairs={{0,1},{1,0},{2,3},{3,2},{4,5},{5,4},{6,7},{7,6},{8,9},{9,8},{10,11... | collective-permute-start | bytes 2359304 | tf_op jit(solution)/shard_map/ppermute | solution.py:370
  5.7 10.1 %all-to-all-start = ((s32[8,1,128]{2,1,0:T(1,128)}), s32[8,1,128]{2,1,0:T(1,128)S(1)}, u32[]{:S(2)}, u32[]{:S(2)}) async-start(s32[8,1,128]{2,1,0:T(1,128)} %broadcast_in_dim.12), calls=%async_computation | async-start | bytes 8192 | tf_op jit(solution)/shard_map/all_to_all | solution.py:373
  15.8 21.2 %collective-permute-start.8 = (bf16[24,128,128]{2,1,0:T(8,128)(2,1)}, bf16[24,128,128]{2,1,0:T(8,128)(2,1)S(1)}, u32[]{:S(2)}, u32[]{:S(2)}) collective-permute-start(bf16[24,128,128]{2,1,0:T(8,128)(2,1)} %bitcast.15), channel_id=1, source_target_pairs={{0,96},{32,0},{64,32},{96,64},{1,97},{33,1},{65,33},{97,65},{2,98}... | collective-permute-start | bytes 2359304 | tf_op jit(solution)/shard_map/ppermute | solution.py:379
  16.6 21.4 %collective-permute-start.7 = (bf16[24,128,128]{2,1,0:T(8,128)(2,1)}, bf16[24,128,128]{2,1,0:T(8,128)(2,1)S(1)}, u32[]{:S(2)}, u32[]{:S(2)}) collective-permute-start(bf16[24,128,128]{2,1,0:T(8,128)(2,1)} %bitcast.16), channel_id=1, source_target_pairs={{0,32},{32,64},{64,96},{96,0},{1,33},{33,65},{65,97},{97,1},{2,34}... | collective-permute-start | bytes 2359304 | tf_op jit(solution)/shard_map/ppermute | solution.py:378
  17.9 11.9 %all-to-all-start.1 = ((s32[16,2,128]{2,1,0:T(2,128)}), s32[16,2,128]{2,1,0:T(2,128)S(1)}, u32[]{:S(2)}, u32[]{:S(2)}) async-start(s32[16,2,128]{2,1,0:T(2,128)} %bitcast.8), calls=%async_computation.1 | async-start | bytes 32768 | tf_op jit(solution)/shard_map/all_to_all | solution.py:376
  23.3 6.4 %copy-start = (bf16[1,24,128,128]{3,2,1,0:T(8,128)(2,1)S(1)}, bf16[1,24,128,128]{3,2,1,0:T(8,128)(2,1)}, u32[]{:S(2)}) copy-start(bf16[1,24,128,128]{3,2,1,0:T(8,128)(2,1)} %param.2) | copy-start | bytes 2359300
  23.3 18.0 %collective-permute-start.1 = (bf16[24,128,128]{2,1,0:T(8,128)(2,1)}, bf16[24,128,128]{2,1,0:T(8,128)(2,1)S(1)}, u32[]{:S(2)}, u32[]{:S(2)}) collective-permute-start(bf16[24,128,128]{2,1,0:T(8,128)(2,1)} %collective-permute-done.refs_1_.outer), channel_id=1, source_target_pairs={{0,1},{1,0},{2,3},{3,2},{4,5},{5,4},{6,7},{7,6},{8,9},{9,8},{10,11... | collective-permute-start | bytes 2359304 | tf_op jit(solution)/shard_map/ppermute | solution.py:385
  32.8 11.8 %collective-permute-start.4 = (bf16[8,128,128]{2,1,0:T(8,128)(2,1)}, bf16[8,128,128]{2,1,0:T(8,128)(2,1)S(1)}, u32[]{:S(2)}, u32[]{:S(2)}) collective-permute-start(bf16[8,128,128]{2,1,0:T(8,128)(2,1)} %get-tuple-element.29), channel_id=1, source_target_pairs={{0,4},{4,8},{8,12},{12,0},{1,5},{5,9},{9,13},{13,1},{2,6},{6,10},{... | collective-permute-start | bytes 786440 | tf_op jit(solution)/shard_map/ppermute | solution.py:364
  33.1 14.0 %collective-permute-start.5 = (bf16[8,128,128]{2,1,0:T(8,128)(2,1)}, bf16[8,128,128]{2,1,0:T(8,128)(2,1)S(1)}, u32[]{:S(2)}, u32[]{:S(2)}) collective-permute-start(bf16[8,128,128]{2,1,0:T(8,128)(2,1)} %get-tuple-element.30), channel_id=1, source_target_pairs={{0,8},{4,12},{8,0},{12,4},{1,9},{5,13},{9,1},{13,5},{2,10},{6,14},... | collective-permute-start | bytes 786440 | tf_op jit(solution)/shard_map/ppermute | solution.py:364
  34.9 0.9 %copy-start.1 = (bf16[8,128,128]{2,1,0:T(8,128)(2,1)S(1)}, bf16[8,128,128]{2,1,0:T(8,128)(2,1)}, u32[]{:S(2)}) copy-start(bf16[8,128,128]{2,1,0:T(8,128)(2,1)} %get-tuple-element.28._.refs_0_) | copy-start | bytes 786436
  37.0 11.2 %collective-permute-start.6 = (bf16[8,128,128]{2,1,0:T(8,128)(2,1)}, bf16[8,128,128]{2,1,0:T(8,128)(2,1)S(1)}, u32[]{:S(2)}, u32[]{:S(2)}) collective-permute-start(bf16[8,128,128]{2,1,0:T(8,128)(2,1)} %get-tuple-element.31), channel_id=1, source_target_pairs={{0,12},{4,0},{8,4},{12,8},{1,13},{5,1},{9,5},{13,9},{2,14},{6,2},{... | collective-permute-start | bytes 786440 | tf_op jit(solution)/shard_map/ppermute | solution.py:364
  38.1 13.7 %collective-permute-start.9 = (bf16[24,128,128]{2,1,0:T(8,128)(2,1)S(1)}, bf16[24,128,128]{2,1,0:T(8,128)(2,1)S(1)}, u32[]{:S(2)}, u32[]{:S(2)}) collective-permute-start(bf16[24,128,128]{2,1,0:T(8,128)(2,1)S(1)} %broadcast_select_fusion), channel_id=1, source_target_pairs={{0,32},{32,64},{64,96},{96,0},{16,112},{48,16},{80,48},{112,80},{1... | collective-permute-start | bytes 2359304 | tf_op jit(solution)/shard_map/ppermute | solution.py:387
  43.6 17.0 %collective-permute-start.10 = (bf16[8,128,128]{2,1,0:T(8,128)(2,1)}, bf16[8,128,128]{2,1,0:T(8,128)(2,1)S(1)}, u32[]{:S(2)}, u32[]{:S(2)}) collective-permute-start(bf16[8,128,128]{2,1,0:T(8,128)(2,1)} %get-tuple-element.38), channel_id=1, source_target_pairs={{0,4},{4,8},{8,12},{12,0},{1,5},{5,9},{9,13},{13,1},{2,6},{6,10},{... | collective-permute-start | bytes 786440 | tf_op jit(solution)/shard_map/ppermute | solution.py:364
  44.7 16.0 %collective-permute-start.11 = (bf16[8,128,128]{2,1,0:T(8,128)(2,1)}, bf16[8,128,128]{2,1,0:T(8,128)(2,1)S(1)}, u32[]{:S(2)}, u32[]{:S(2)}) collective-permute-start(bf16[8,128,128]{2,1,0:T(8,128)(2,1)} %get-tuple-element.39), channel_id=1, source_target_pairs={{0,8},{4,12},{8,0},{12,4},{1,9},{5,13},{9,1},{13,5},{2,10},{6,14},... | collective-permute-start | bytes 786440 | tf_op jit(solution)/shard_map/ppermute | solution.py:364
  47.1 11.8 %copy-start.2 = (bf16[8,128,128]{2,1,0:T(8,128)(2,1)S(1)}, bf16[8,128,128]{2,1,0:T(8,128)(2,1)}, u32[]{:S(2)}) copy-start(bf16[8,128,128]{2,1,0:T(8,128)(2,1)} %get-tuple-element.28._.refs_0_) | copy-start | bytes 786436
  47.1 11.8 %copy-start.3 = (bf16[8,128,128]{2,1,0:T(8,128)(2,1)S(1)}, bf16[8,128,128]{2,1,0:T(8,128)(2,1)}, u32[]{:S(2)}) copy-start(bf16[8,128,128]{2,1,0:T(8,128)(2,1)} %get-tuple-element.37.refs_10_.refs_4_) | copy-start | bytes 786436
  47.1 13.6 %collective-permute-start.12 = (bf16[8,128,128]{2,1,0:T(8,128)(2,1)}, bf16[8,128,128]{2,1,0:T(8,128)(2,1)S(1)}, u32[]{:S(2)}, u32[]{:S(2)}) collective-permute-start(bf16[8,128,128]{2,1,0:T(8,128)(2,1)} %get-tuple-element.40), channel_id=1, source_target_pairs={{0,12},{4,0},{8,4},{12,8},{1,13},{5,1},{9,5},{13,9},{2,14},{6,2},{... | collective-permute-start | bytes 786440 | tf_op jit(solution)/shard_map/ppermute | solution.py:364
  48.3 10.5 %collective-permute-start.13 = (bf16[24,128,128]{2,1,0:T(8,128)(2,1)S(1)}, bf16[24,128,128]{2,1,0:T(8,128)(2,1)S(1)}, u32[]{:S(2)}, u32[]{:S(2)}) collective-permute-start(bf16[24,128,128]{2,1,0:T(8,128)(2,1)S(1)} %collective-permute-done.7.refs_5_.refs_9_), channel_id=1, source_target_pairs={{0,16},{16,0},{1,17},{17,1},{2,18},{18,2},{3,19},{19,3},{4,20},{20... | collective-permute-start | bytes 2359304 | tf_op jit(solution)/shard_map/ppermute | solution.py:396
  51.8 7.1 %collective-permute-start.14 = (bf16[24,128,128]{2,1,0:T(8,128)(2,1)S(1)}, bf16[24,128,128]{2,1,0:T(8,128)(2,1)S(1)}, u32[]{:S(2)}, u32[]{:S(2)}) collective-permute-start(bf16[24,128,128]{2,1,0:T(8,128)(2,1)S(1)} %collective-permute-done.8.refs_6_.refs_10_), channel_id=1, source_target_pairs={{0,16},{16,0},{1,17},{17,1},{2,18},{18,2},{3,19},{19,3},{4,20},{20... | collective-permute-start | bytes 2359304 | tf_op jit(solution)/shard_map/ppermute | solution.py:396
  58.8 2.4 %collective-permute-start.15 = (bf16[24,128,128]{2,1,0:T(8,128)(2,1)S(1)}, bf16[24,128,128]{2,1,0:T(8,128)(2,1)S(1)}, u32[]{:S(2)}, u32[]{:S(2)}) collective-permute-start(bf16[24,128,128]{2,1,0:T(8,128)(2,1)S(1)} %collective-permute-done.9.refs_11_), channel_id=1, source_target_pairs={{0,16},{16,0},{1,17},{17,1},{2,18},{18,2},{3,19},{19,3},{4,20},{20... | collective-permute-start | bytes 2359304 | tf_op jit(solution)/shard_map/ppermute | solution.py:401

commit v8 on v7

--- a/solution.py
+++ b/solution.py
@@ -369,10 +369,9 @@
     pos = jnp.stack([lax.axis_index(a) for a in ("x", "y", "z", "core")]).astype(jnp.int32)
     inner = lax.ppermute(own, "x", INNER)
     outer = lax.ppermute(own, "x", OUTER)
-    wide_rows = jnp.pad(tile_rows, ((0, 0), (0, TILE - BLK)))
-    rows = lax.all_to_all(jnp.broadcast_to(wide_rows, (PANELS, 1, TILE)), ("z", "core"), 0, 0)
+    rows = lax.all_to_all(jnp.broadcast_to(tile_rows, (PANELS, 1, BLK)), ("z", "core"), 0, 0)
     own_rows = jnp.pad(tile_rows, ((0, 0), (OWN_ROWS, TILE - OWN_ROWS - BLK)))
-    asks = jnp.broadcast_to(rows.reshape(4, 1, 2, TILE) + own_rows, (4, 4, 2, TILE)).reshape(COLS, 2, TILE)
+    asks = jnp.broadcast_to(jnp.pad(rows, ((0, 0), (0, 0), (0, TILE - BLK))).reshape(4, 1, 2, TILE) + own_rows, (4, 4, 2, TILE)).reshape(COLS, 2, TILE)
     req = lax.all_to_all(asks, ("y", "x"), 0, 0)
     own_z, rows_z = lax.optimization_barrier((own, rows))
     below = lax.ppermute(own_z, "z", UP)

time: 78 us -> 78 us (level)
  transfers between devices with their start and end apart: 18 -> 18, of which waited for: 4 -> 4; matrix products, arithmetic and copies ran while one was open for 3% -> 4% of each run, Pallas kernels for 16% -> 16%
where the time goes in v8:
time: 78 us; the launch traced here: 77.5 us
  starting transfers between devices  34.7 us (44%)
  Pallas kernels  20.1 us (26%)
  waiting for transfers between devices  10.4 us (13%)
  blocking collectives  8.43 us (11%)
  local copies, waits for them, and re-layouts  3.56 us (5%)
    all_to_all x1, blocking collectives, on_device(): totals = lax.all_to_all(totals, ('z', 'core'), 0, 0)  8.43 us
    ppermute x6, starting transfers between devices, exchange(): lax.ppermute(part, 'y', way)  7.67 us
    ppermute x2, starting transfers between devices, on_device(): lax.ppermute(block, 'core', SWAP)  6.64 us
    all_to_all x1, starting transfers between devices, on_device(): lax.all_to_all(jnp.broadcast_to(tile_rows, (PANELS, 1, BLK)), ('z', 'core...  5.53 us
    all_to_all x1, starting transfers between devices, on_device(): req = lax.all_to_all(asks, ('y', 'x'), 0, 0)  5.44 us
    all_to_all x1, waiting for transfers between devices, on_device(): req = lax.all_to_all(asks, ('y', 'x'), 0, 0)  4.96 us
    pallas_call x1, Pallas kernels, multiply_other(): pl.pallas_call(other_kernel, out_shape=(pltpu.VMEM(MERGED, jnp.float32),...  4.45 us
    pallas_call x1, Pallas kernels, make_plan(): pl.pallas_call(plan_kernel, out_shape=pltpu.SMEM((512,), jnp.int32), in_s...  3.89 us
  transfers between devices with their start and end apart: 18, of which 4 were waited for; matrix products, arithmetic and copies ran while one was open for 4% of the time, Pallas kernels for 16%

profile of v8, /device:TPU:1, one launch (start us, length us, event | category | flops | bytes accessed | tf_op | source)
XLA Modules:
  0.0 77.5 jit_solution(2305354089450668684)
XLA Ops:
  0.0 3.3 %collective-permute-start = (bf16[24,128,128]{2,1,0:T(8,128)(2,1)}, bf16[24,128,128]{2,1,0:T(8,128)(2,1)}, u32[]{:S(2)}, u32[]{:S(2)}) collective-permute-start(bf16[24,128,128]{2,1,0:T(8,128)(2,1)} %bitcast.11), channel_id=1, source_target_pairs={{0,3},{3,0},{1,2},{2,1},{4,7},{7,4},{5,6},{6,5},{8,11},{11,8},{9,1... | collective-permute-start | bytes 2359304 | tf_op jit(solution)/shard_map/ppermute | solution.py:371
  4.3 1.2 %broadcast_in_dim.12 = s32[8,1,24]{2,1,0:T(1,128)} broadcast(s32[24]{0:T(128)} %bitcast.20), dimensions={2} | broadcast | bytes 864 | tf_op jit(solution)/shard_map/broadcast_in_dim | solution.py:372
  5.5 5.5 %all-to-all-start = ((s32[8,1,24]{2,1,0:T(1,128)}), s32[8,1,24]{2,1,0:T(1,128)S(1)}, u32[]{:S(2)}, u32[]{:S(2)}) async-start(s32[8,1,24]{2,1,0:T(1,128)} %broadcast_in_dim.12), calls=%async_computation | async-start | bytes 8192 | tf_op jit(solution)/shard_map/all_to_all | solution.py:372
  11.9 3.8 %all-to-all-done.rows = s32[8,1,24]{2,1,0:T(1,128)S(1)} async-done(((s32[8,1,24]{2,1,0:T(1,128)}), s32[8,1,24]{2,1,0:T(1,128)S(1)}, u32[]{:S(2)}, u32[]{:S(2)}) %all-to-all-start) | async-done | bytes 800 | tf_op jit(solution)/shard_map/all_to_all | solution.py:372
  17.7 5.4 %all-to-all-start.1 = ((s32[16,2,128]{2,1,0:T(2,128)}), s32[16,2,128]{2,1,0:T(2,128)S(1)}, u32[]{:S(2)}, u32[]{:S(2)}) async-start(s32[16,2,128]{2,1,0:T(2,128)} %bitcast.8), calls=%async_computation.1 | async-start | bytes 32768 | tf_op jit(solution)/shard_map/all_to_all | solution.py:375
  23.2 1.4 %collective-permute-start.1 = (bf16[24,128,128]{2,1,0:T(8,128)(2,1)}, bf16[24,128,128]{2,1,0:T(8,128)(2,1)S(1)}, u32[]{:S(2)}, u32[]{:S(2)}) collective-permute-start(bf16[24,128,128]{2,1,0:T(8,128)(2,1)} %collective-permute-done.refs_1_.outer), channel_id=1, source_target_pairs={{0,1},{1,0},{2,3},{3,2},{4,5},{5,4},{6,7},{7,6},{8,9},{9,8},{10,11... | collective-permute-start | bytes 2359304 | tf_op jit(solution)/shard_map/ppermute | solution.py:384
  24.7 5.0 %all-to-all-done.1.req = s32[16,2,128]{2,1,0:T(2,128)S(1)} async-done(((s32[16,2,128]{2,1,0:T(2,128)}), s32[16,2,128]{2,1,0:T(2,128)S(1)}, u32[]{:S(2)}, u32[]{:S(2)}) %all-to-all-start.1) | async-done | bytes 16416 | tf_op jit(solution)/shard_map/all_to_all | solution.py:375
  29.6 3.1 %shard_map.33 = (bf16[8,128,128]{2,1,0:T(8,128)(2,1)}, bf16[8,128,128]{2,1,0:T(8,128)(2,1)}, bf16[8,128,128]{2,1,0:T(8,128)(2,1)}, bf16[8,128,128]{2,1,0:T(8,128)(2,1)}, s32[128]{0:T(128)S(4)}) custom-call(s32[4]{0:T(128)S(1)} %pad_add_fusion.pos, s32[16,2,128]{2,1,0:T(2,128)S(1)} %all-to-all-done.1.req, bf16[24,128,128]{2,1,0:T(8,128)(2,1)S(1)} %bitcast.16, ...), custom_call_target="tpu_custom_call" | custom-call | bytes 2097152 | tf_op jit(solution)/shard_map/pallas_call | solution.py:139
  33.0 1.8 %collective-permute-start.5 = (bf16[8,128,128]{2,1,0:T(8,128)(2,1)}, bf16[8,128,128]{2,1,0:T(8,128)(2,1)S(1)}, u32[]{:S(2)}, u32[]{:S(2)}) collective-permute-start(bf16[8,128,128]{2,1,0:T(8,128)(2,1)} %get-tuple-element.30), channel_id=1, source_target_pairs={{0,8},{4,12},{8,0},{12,4},{1,9},{5,13},{9,1},{13,5},{2,10},{6,14},... | collective-permute-start | bytes 786440 | tf_op jit(solution)/shard_map/ppermute | solution.py:364
  35.7 1.1 %shard_map.34 = (bf16[24,128,128]{2,1,0:T(8,128)(2,1)S(1)}, s32[8]{0:T(128)S(4)}) custom-call(bf16[24,128,128]{2,1,0:T(8,128)(2,1)} %collective-permute-done.3.refs_2_.source, bf16[8,128,128]{2,1,0:T(8,128)(2,1)S(1)} %copy-done.1), custom_call_target="tpu_custom_call" | custom-call | bytes 2097152 | tf_op jit(solution)/shard_map/pallas_call | solution.py:77
  36.9 1.0 %collective-permute-start.6 = (bf16[8,128,128]{2,1,0:T(8,128)(2,1)}, bf16[8,128,128]{2,1,0:T(8,128)(2,1)S(1)}, u32[]{:S(2)}, u32[]{:S(2)}) collective-permute-start(bf16[8,128,128]{2,1,0:T(8,128)(2,1)} %get-tuple-element.31), channel_id=1, source_target_pairs={{0,12},{4,0},{8,4},{12,8},{1,13},{5,1},{9,5},{13,9},{2,14},{6,2},{... | collective-permute-start | bytes 786440 | tf_op jit(solution)/shard_map/ppermute | solution.py:364
  38.0 2.2 %collective-permute-start.9 = (bf16[24,128,128]{2,1,0:T(8,128)(2,1)S(1)}, bf16[24,128,128]{2,1,0:T(8,128)(2,1)S(1)}, u32[]{:S(2)}, u32[]{:S(2)}) collective-permute-start(bf16[24,128,128]{2,1,0:T(8,128)(2,1)S(1)} %broadcast_select_fusion), channel_id=1, source_target_pairs={{0,32},{32,64},{64,96},{96,0},{16,112},{48,16},{80,48},{112,80},{1... | collective-permute-start | bytes 2359304 | tf_op jit(solution)/shard_map/ppermute | solution.py:386
  40.1 1.1 %collective-permute-done.1._.refs_0_.diag = bf16[24,128,128]{2,1,0:T(8,128)(2,1)S(1)} collective-permute-done((bf16[24,128,128]{2,1,0:T(8,128)(2,1)}, bf16[24,128,128]{2,1,0:T(8,128)(2,1)S(1)}, u32[]{:S(2)}, u32[]{:S(2)}) %collective-permute-start.1) | collective-permute-done | bytes 786464 | tf_op jit(solution)/shard_map/ppermute | solution.py:384
  41.2 2.3 %shard_map.36 = (bf16[8,128,128]{2,1,0:T(8,128)(2,1)}, bf16[8,128,128]{2,1,0:T(8,128)(2,1)}, bf16[8,128,128]{2,1,0:T(8,128)(2,1)}, bf16[8,128,128]{2,1,0:T(8,128)(2,1)}) custom-call(s32[128]{0:T(128)S(4)} %get-tuple-element.32.lists.___, bf16[24,128,128]{2,1,0:T(8,128)(2,1)} %collective-permute-done.refs_1_.outer, ...), custom_call_target="tpu_custom_call" | custom-call | bytes 2097152 | tf_op jit(solution)/shard_map/pallas_call | solution.py:150
  43.5 1.1 %collective-permute-start.10 = (bf16[8,128,128]{2,1,0:T(8,128)(2,1)}, bf16[8,128,128]{2,1,0:T(8,128)(2,1)S(1)}, u32[]{:S(2)}, u32[]{:S(2)}) collective-permute-start(bf16[8,128,128]{2,1,0:T(8,128)(2,1)} %get-tuple-element.38), channel_id=1, source_target_pairs={{0,4},{4,8},{8,12},{12,0},{1,5},{5,9},{9,13},{13,1},{2,6},{6,10},{... | collective-permute-start | bytes 786440 | tf_op jit(solution)/shard_map/ppermute | solution.py:364
  44.5 2.4 %collective-permute-start.11 = (bf16[8,128,128]{2,1,0:T(8,128)(2,1)}, bf16[8,128,128]{2,1,0:T(8,128)(2,1)S(1)}, u32[]{:S(2)}, u32[]{:S(2)}) collective-permute-start(bf16[8,128,128]{2,1,0:T(8,128)(2,1)} %get-tuple-element.39), channel_id=1, source_target_pairs={{0,8},{4,12},{8,0},{12,4},{1,9},{5,13},{9,1},{13,5},{2,10},{6,14},... | collective-permute-start | bytes 786440 | tf_op jit(solution)/shard_map/ppermute | solution.py:364
  47.0 1.2 %collective-permute-start.12 = (bf16[8,128,128]{2,1,0:T(8,128)(2,1)}, bf16[8,128,128]{2,1,0:T(8,128)(2,1)S(1)}, u32[]{:S(2)}, u32[]{:S(2)}) collective-permute-start(bf16[8,128,128]{2,1,0:T(8,128)(2,1)} %get-tuple-element.40), channel_id=1, source_target_pairs={{0,12},{4,0},{8,4},{12,8},{1,13},{5,1},{9,5},{13,9},{2,14},{6,2},{... | collective-permute-start | bytes 786440 | tf_op jit(solution)/shard_map/ppermute | solution.py:364
  48.1 3.5 %collective-permute-start.13 = (bf16[24,128,128]{2,1,0:T(8,128)(2,1)S(1)}, bf16[24,128,128]{2,1,0:T(8,128)(2,1)S(1)}, u32[]{:S(2)}, u32[]{:S(2)}) collective-permute-start(bf16[24,128,128]{2,1,0:T(8,128)(2,1)S(1)} %collective-permute-done.7.refs_5_.refs_9_), channel_id=1, source_target_pairs={{0,16},{16,0},{1,17},{17,1},{2,18},{18,2},{3,19},{19,3},{4,20},{20... | collective-permute-start | bytes 2359304 | tf_op jit(solution)/shard_map/ppermute | solution.py:395
  51.6 3.1 %collective-permute-start.14 = (bf16[24,128,128]{2,1,0:T(8,128)(2,1)S(1)}, bf16[24,128,128]{2,1,0:T(8,128)(2,1)S(1)}, u32[]{:S(2)}, u32[]{:S(2)}) collective-permute-start(bf16[24,128,128]{2,1,0:T(8,128)(2,1)S(1)} %collective-permute-done.8.refs_6_.refs_10_), channel_id=1, source_target_pairs={{0,16},{16,0},{1,17},{17,1},{2,18},{18,2},{3,19},{19,3},{4,20},{20... | collective-permute-start | bytes 2359304 | tf_op jit(solution)/shard_map/ppermute | solution.py:395
  54.8 3.9 %shard_map.31.plan = s32[512]{0:T(512)S(4)} custom-call(s32[4]{0:T(128)S(1)} %pad_add_fusion.pos, s32[8,1,24]{2,1,0:T(1,128)S(1)} %all-to-all-done.rows, s32[16,2,128]{2,1,0:T(2,128)S(1)} %all-to-all-done.1.req, bf16[24,128,128]{2,1,0:T(8,128)(2,1)S(1)} %collective-permute-done.1._.refs_0_.diag), custom_call_target="tpu_custom_call" | custom-call | bytes 33554432 | tf_op jit(solution)/shard_map/pallas_call | solution.py:199
  58.8 1.7 %shard_map.38 = (f32[24,3,128,128]{3,2,1,0:T(8,128)S(1)}, s32[8]{0:T(128)S(4)}) custom-call(s32[512]{0:T(512)S(4)} %shard_map.31.plan, bf16[8,128,128]{2,1,0:T(8,128)(2,1)S(1)} %copy-done.2, bf16[8,128,128]{2,1,0:T(8,128)(2,1)S(1)} %collective-permute-done.4.refs_0_.refs_1_, bf16[8,128,128]{2,1,0:T(8,128)(2,1)S(1)} %collective-permute-done.5.refs_1_.refs_2_, ...), custom_call_target="tpu_custom_call" | custom-call | flops 402653184 | bytes 16777216 | tf_op jit(solution)/shard_map/pallas_call | solution.py:300
  61.1 4.5 %shard_map.40 = (f32[24,8,128,128]{3,2,1,0:T(8,128)S(1)}, f32[8,24,128]{2,1,0:T(8,128)}) custom-call(s32[512]{0:T(512)S(4)} %shard_map.31.plan, bf16[8,128,128]{2,1,0:T(8,128)(2,1)S(1)} %copy-done.2, bf16[8,128,128]{2,1,0:T(8,128)(2,1)S(1)} %collective-permute-done.4.refs_0_.refs_1_, bf16[8,128,128]{2,1,0:T(8,128)(2,1)S(1)} %collective-permute-done.5.refs_1_.refs_2_, ...), custom_call_target="tpu_custom_call" | custom-call | flops 402653184 | bytes 16777216 | tf_op jit(solution)/shard_map/pallas_call | solution.py:312
  65.5 8.4 %all_to_all.15.totals = f32[8,24,128]{2,1,0:T(8,128)S(1)} all-to-all(f32[8,24,128]{2,1,0:T(8,128)} %get-tuple-element.48), channel_id=1, replica_groups=mesh['z'=4,'core'=2,'y'=4,'x'=4] {'z','core'}, dimensions={0} | all-to-all | bytes 196608 | tf_op jit(solution)/shard_map/all_to_all | solution.py:402
  73.9 3.6 %shard_map.41 = bf16[8,24,128,128]{3,2,1,0:T(8,128)(2,1)} custom-call(s32[512]{0:T(512)S(4)} %shard_map.31.plan, f32[24,8,128,128]{3,2,1,0:T(8,128)S(1)} %get-tuple-element.47.merged, f32[8,24,128]{2,1,0:T(8,128)S(1)} %all_to_all.15.totals), custom_call_target="tpu_custom_call" | custom-call | flops 6291456 | bytes 20971520 | tf_op jit(solution)/shard_map/pallas_call | solution.py:348
  (39 shorter events, 5.8 us)
Async XLA Ops:
  0.0 23.2 %collective-permute-start = (bf16[24,128,128]{2,1,0:T(8,128)(2,1)}, bf16[24,128,128]{2,1,0:T(8,128)(2,1)}, u32[]{:S(2)}, u32[]{:S(2)}) collective-permute-start(bf16[24,128,128]{2,1,0:T(8,128)(2,1)} %bitcast.11), channel_id=1, source_target_pairs={{0,3},{3,0},{1,2},{2,1},{4,7},{7,4},{5,6},{6,5},{8,11},{11,8},{9,1... | collective-permute-start | bytes 2359304 | tf_op jit(solution)/shard_map/ppermute | solution.py:371
  3.3 21.3 %collective-permute-start.3 = (bf16[24,128,128]{2,1,0:T(8,128)(2,1)}, bf16[24,128,128]{2,1,0:T(8,128)(2,1)}, u32[]{:S(2)}, u32[]{:S(2)}) collective-permute-start(bf16[24,128,128]{2,1,0:T(8,128)(2,1)} %bitcast.12), channel_id=1, source_target_pairs={{0,16},{16,0},{1,17},{17,1},{2,18},{18,2},{3,19},{19,3},{4,20},{20... | collective-permute-start | bytes 2359304 | tf_op jit(solution)/shard_map/ppermute | solution.py:380
  4.3 20.4 %collective-permute-start.2 = (bf16[24,128,128]{2,1,0:T(8,128)(2,1)}, bf16[24,128,128]{2,1,0:T(8,128)(2,1)}, u32[]{:S(2)}, u32[]{:S(2)}) collective-permute-start(bf16[24,128,128]{2,1,0:T(8,128)(2,1)} %bitcast.13), channel_id=1, source_target_pairs={{0,1},{1,0},{2,3},{3,2},{4,5},{5,4},{6,7},{7,6},{8,9},{9,8},{10,11... | collective-permute-start | bytes 2359304 | tf_op jit(solution)/shard_map/ppermute | solution.py:370
  5.5 10.1 %all-to-all-start = ((s32[8,1,24]{2,1,0:T(1,128)}), s32[8,1,24]{2,1,0:T(1,128)S(1)}, u32[]{:S(2)}, u32[]{:S(2)}) async-start(s32[8,1,24]{2,1,0:T(1,128)} %broadcast_in_dim.12), calls=%async_computation | async-start | bytes 8192 | tf_op jit(solution)/shard_map/all_to_all | solution.py:372
  15.6 21.2 %collective-permute-start.8 = (bf16[24,128,128]{2,1,0:T(8,128)(2,1)}, bf16[24,128,128]{2,1,0:T(8,128)(2,1)S(1)}, u32[]{:S(2)}, u32[]{:S(2)}) collective-permute-start(bf16[24,128,128]{2,1,0:T(8,128)(2,1)} %bitcast.14), channel_id=1, source_target_pairs={{0,96},{32,0},{64,32},{96,64},{1,97},{33,1},{65,33},{97,65},{2,98}... | collective-permute-start | bytes 2359304 | tf_op jit(solution)/shard_map/ppermute | solution.py:378
  16.4 21.4 %collective-permute-start.7 = (bf16[24,128,128]{2,1,0:T(8,128)(2,1)}, bf16[24,128,128]{2,1,0:T(8,128)(2,1)S(1)}, u32[]{:S(2)}, u32[]{:S(2)}) collective-permute-start(bf16[24,128,128]{2,1,0:T(8,128)(2,1)} %bitcast.15), channel_id=1, source_target_pairs={{0,32},{32,64},{64,96},{96,0},{1,33},{33,65},{65,97},{97,1},{2,34}... | collective-permute-start | bytes 2359304 | tf_op jit(solution)/shard_map/ppermute | solution.py:377
  17.7 11.9 %all-to-all-start.1 = ((s32[16,2,128]{2,1,0:T(2,128)}), s32[16,2,128]{2,1,0:T(2,128)S(1)}, u32[]{:S(2)}, u32[]{:S(2)}) async-start(s32[16,2,128]{2,1,0:T(2,128)} %bitcast.8), calls=%async_computation.1 | async-start | bytes 32768 | tf_op jit(solution)/shard_map/all_to_all | solution.py:375
  23.2 6.4 %copy-start = (bf16[1,24,128,128]{3,2,1,0:T(8,128)(2,1)S(1)}, bf16[1,24,128,128]{3,2,1,0:T(8,128)(2,1)}, u32[]{:S(2)}) copy-start(bf16[1,24,128,128]{3,2,1,0:T(8,128)(2,1)} %param.2) | copy-start | bytes 2359300
  23.2 18.0 %collective-permute-start.1 = (bf16[24,128,128]{2,1,0:T(8,128)(2,1)}, bf16[24,128,128]{2,1,0:T(8,128)(2,1)S(1)}, u32[]{:S(2)}, u32[]{:S(2)}) collective-permute-start(bf16[24,128,128]{2,1,0:T(8,128)(2,1)} %collective-permute-done.refs_1_.outer), channel_id=1, source_target_pairs={{0,1},{1,0},{2,3},{3,2},{4,5},{5,4},{6,7},{7,6},{8,9},{9,8},{10,11... | collective-permute-start | bytes 2359304 | tf_op jit(solution)/shard_map/ppermute | solution.py:384
  32.7 11.8 %collective-permute-start.4 = (bf16[8,128,128]{2,1,0:T(8,128)(2,1)}, bf16[8,128,128]{2,1,0:T(8,128)(2,1)S(1)}, u32[]{:S(2)}, u32[]{:S(2)}) collective-permute-start(bf16[8,128,128]{2,1,0:T(8,128)(2,1)} %get-tuple-element.29), channel_id=1, source_target_pairs={{0,4},{4,8},{8,12},{12,0},{1,5},{5,9},{9,13},{13,1},{2,6},{6,10},{... | collective-permute-start | bytes 786440 | tf_op jit(solution)/shard_map/ppermute | solution.py:364
  33.0 13.9 %collective-permute-start.5 = (bf16[8,128,128]{2,1,0:T(8,128)(2,1)}, bf16[8,128,128]{2,1,0:T(8,128)(2,1)S(1)}, u32[]{:S(2)}, u32[]{:S(2)}) collective-permute-start(bf16[8,128,128]{2,1,0:T(8,128)(2,1)} %get-tuple-element.30), channel_id=1, source_target_pairs={{0,8},{4,12},{8,0},{12,4},{1,9},{5,13},{9,1},{13,5},{2,10},{6,14},... | collective-permute-start | bytes 786440 | tf_op jit(solution)/shard_map/ppermute | solution.py:364
  34.8 0.9 %copy-start.1 = (bf16[8,128,128]{2,1,0:T(8,128)(2,1)S(1)}, bf16[8,128,128]{2,1,0:T(8,128)(2,1)}, u32[]{:S(2)}) copy-start(bf16[8,128,128]{2,1,0:T(8,128)(2,1)} %get-tuple-element.28._.refs_0_) | copy-start | bytes 786436
  36.9 11.2 %collective-permute-start.6 = (bf16[8,128,128]{2,1,0:T(8,128)(2,1)}, bf16[8,128,128]{2,1,0:T(8,128)(2,1)S(1)}, u32[]{:S(2)}, u32[]{:S(2)}) collective-permute-start(bf16[8,128,128]{2,1,0:T(8,128)(2,1)} %get-tuple-element.31), channel_id=1, source_target_pairs={{0,12},{4,0},{8,4},{12,8},{1,13},{5,1},{9,5},{13,9},{2,14},{6,2},{... | collective-permute-start | bytes 786440 | tf_op jit(solution)/shard_map/ppermute | solution.py:364
  38.0 13.7 %collective-permute-start.9 = (bf16[24,128,128]{2,1,0:T(8,128)(2,1)S(1)}, bf16[24,128,128]{2,1,0:T(8,128)(2,1)S(1)}, u32[]{:S(2)}, u32[]{:S(2)}) collective-permute-start(bf16[24,128,128]{2,1,0:T(8,128)(2,1)S(1)} %broadcast_select_fusion), channel_id=1, source_target_pairs={{0,32},{32,64},{64,96},{96,0},{16,112},{48,16},{80,48},{112,80},{1... | collective-permute-start | bytes 2359304 | tf_op jit(solution)/shard_map/ppermute | solution.py:386
  43.5 17.0 %collective-permute-start.10 = (bf16[8,128,128]{2,1,0:T(8,128)(2,1)}, bf16[8,128,128]{2,1,0:T(8,128)(2,1)S(1)}, u32[]{:S(2)}, u32[]{:S(2)}) collective-permute-start(bf16[8,128,128]{2,1,0:T(8,128)(2,1)} %get-tuple-element.38), channel_id=1, source_target_pairs={{0,4},{4,8},{8,12},{12,0},{1,5},{5,9},{9,13},{13,1},{2,6},{6,10},{... | collective-permute-start | bytes 786440 | tf_op jit(solution)/shard_map/ppermute | solution.py:364
  44.5 16.0 %collective-permute-start.11 = (bf16[8,128,128]{2,1,0:T(8,128)(2,1)}, bf16[8,128,128]{2,1,0:T(8,128)(2,1)S(1)}, u32[]{:S(2)}, u32[]{:S(2)}) collective-permute-start(bf16[8,128,128]{2,1,0:T(8,128)(2,1)} %get-tuple-element.39), channel_id=1, source_target_pairs={{0,8},{4,12},{8,0},{12,4},{1,9},{5,13},{9,1},{13,5},{2,10},{6,14},... | collective-permute-start | bytes 786440 | tf_op jit(solution)/shard_map/ppermute | solution.py:364
  46.9 11.8 %copy-start.2 = (bf16[8,128,128]{2,1,0:T(8,128)(2,1)S(1)}, bf16[8,128,128]{2,1,0:T(8,128)(2,1)}, u32[]{:S(2)}) copy-start(bf16[8,128,128]{2,1,0:T(8,128)(2,1)} %get-tuple-element.28._.refs_0_) | copy-start | bytes 786436
  46.9 11.9 %copy-start.3 = (bf16[8,128,128]{2,1,0:T(8,128)(2,1)S(1)}, bf16[8,128,128]{2,1,0:T(8,128)(2,1)}, u32[]{:S(2)}) copy-start(bf16[8,128,128]{2,1,0:T(8,128)(2,1)} %get-tuple-element.37.refs_10_.refs_4_) | copy-start | bytes 786436
  47.0 13.6 %collective-permute-start.12 = (bf16[8,128,128]{2,1,0:T(8,128)(2,1)}, bf16[8,128,128]{2,1,0:T(8,128)(2,1)S(1)}, u32[]{:S(2)}, u32[]{:S(2)}) collective-permute-start(bf16[8,128,128]{2,1,0:T(8,128)(2,1)} %get-tuple-element.40), channel_id=1, source_target_pairs={{0,12},{4,0},{8,4},{12,8},{1,13},{5,1},{9,5},{13,9},{2,14},{6,2},{... | collective-permute-start | bytes 786440 | tf_op jit(solution)/shard_map/ppermute | solution.py:364
  48.1 10.5 %collective-permute-start.13 = (bf16[24,128,128]{2,1,0:T(8,128)(2,1)S(1)}, bf16[24,128,128]{2,1,0:T(8,128)(2,1)S(1)}, u32[]{:S(2)}, u32[]{:S(2)}) collective-permute-start(bf16[24,128,128]{2,1,0:T(8,128)(2,1)S(1)} %collective-permute-done.7.refs_5_.refs_9_), channel_id=1, source_target_pairs={{0,16},{16,0},{1,17},{17,1},{2,18},{18,2},{3,19},{19,3},{4,20},{20... | collective-permute-start | bytes 2359304 | tf_op jit(solution)/shard_map/ppermute | solution.py:395
  51.6 7.2 %collective-permute-start.14 = (bf16[24,128,128]{2,1,0:T(8,128)(2,1)S(1)}, bf16[24,128,128]{2,1,0:T(8,128)(2,1)S(1)}, u32[]{:S(2)}, u32[]{:S(2)}) collective-permute-start(bf16[24,128,128]{2,1,0:T(8,128)(2,1)S(1)} %collective-permute-done.8.refs_6_.refs_10_), channel_id=1, source_target_pairs={{0,16},{16,0},{1,17},{17,1},{2,18},{18,2},{3,19},{19,3},{4,20},{20... | collective-permute-start | bytes 2359304 | tf_op jit(solution)/shard_map/ppermute | solution.py:395
  58.7 2.4 %collective-permute-start.15 = (bf16[24,128,128]{2,1,0:T(8,128)(2,1)S(1)}, bf16[24,128,128]{2,1,0:T(8,128)(2,1)S(1)}, u32[]{:S(2)}, u32[]{:S(2)}) collective-permute-start(bf16[24,128,128]{2,1,0:T(8,128)(2,1)S(1)} %collective-permute-done.9.refs_11_), channel_id=1, source_target_pairs={{0,16},{16,0},{1,17},{17,1},{2,18},{18,2},{3,19},{19,3},{4,20},{20... | collective-permute-start | bytes 2359304 | tf_op jit(solution)/shard_map/ppermute | solution.py:400
